TPU v7x, 32 devices: a whole 2x2x4 slice. The times are simulated.
32 devices in a mesh: dp: 4 (over x, core), ctx: 4 (over z), tensor: 2 (over y).
Axes of the slice: x: 2, y: 2, z: 4, core: 2. Of those that a mesh axis runs over, the one named last changes fastest.
Arguments:
- inputs: bfloat16 [4, 2048, 1024], P('dp', 'ctx'), may hold values from -6 to 6
- qkv_weight: bfloat16 [1024, 3, 1024], P('dp', None, 'tensor'), may hold values from -0.1875 to 0.1875
- qv_bias: bfloat16 [2, 16, 64], P(None, 'tensor', 'dp'), may hold values from -3 to 3
- out_weight: bfloat16 [1024, 1024], P('tensor', 'dp'), may hold values from -1.5 to 1.5
- out_bias: bfloat16 [1024], P('dp'), may hold values from -2 to 2
- up_weight: bfloat16 [1024, 4096], P('dp', 'tensor'), may hold values from -0.1875 to 0.1875
- up_bias: bfloat16 [64, 64], P('tensor', 'dp'), may hold values from -3 to 3
- down_weight: bfloat16 [4096, 1024], P('tensor', 'dp'), may hold values from -0.09375 to 0.09375
- down_bias: bfloat16 [1024], P('dp'), may hold values from -2 to 2
- first_gain: bfloat16 [1024], P('dp'), may hold values from 0.099609375 to 1.8984375
- first_shift: bfloat16 [1024], P('dp'), may hold values from -2 to 2
- second_gain: bfloat16 [1024], P('dp'), may hold values from 0.099609375 to 1.8984375
- second_shift: bfloat16 [1024], P('dp'), may hold values from -2 to 2
- grad_output: bfloat16 [4, 2048, 1024], P('dp', 'ctx'), may hold values from -6 to 6
Outputs:
- output: bfloat16 [4, 2048, 1024], P('dp', 'ctx')
- grad_inputs: bfloat16 [4, 2048, 1024], P('dp', 'ctx')
- grad_qkv_weight: float32 [1024, 3, 1024], P('dp', None, 'tensor')
- grad_qv_bias: float32 [2, 16, 64], P(None, 'tensor', 'dp')
- grad_out_weight: float32 [1024, 1024], P('tensor', 'dp')
- grad_out_bias: float32 [1024], P('dp')
- grad_up_weight: float32 [1024, 4096], P('dp', 'tensor')
- grad_up_bias: float32 [64, 64], P('tensor', 'dp')
- grad_down_weight: float32 [4096, 1024], P('tensor', 'dp')
- grad_down_bias: float32 [1024], P('dp')
- grad_first_gain: float32 [1024], P('dp')
- grad_first_shift: float32 [1024], P('dp')
- grad_second_gain: float32 [1024], P('dp')
- grad_second_shift: float32 [1024], P('dp')
All inputs are finite; a program needn't handle non-finite values.
Results may differ from a plain program's by a relative error of at most 0.023.
Values may be sent and summed in bfloat16 or wider, within the bound.
A program may use at most 320 MiB of HBM per device.

v0:
```python
import jax
import jax.numpy as jnp
from jax import lax
from jax.sharding import PartitionSpec as P

HEAD_DIM = 64


def shifted(value, axis, steps):
    count = lax.axis_size(axis)
    pairs = [(source, (source + steps) % count) for source in range(count)]
    return lax.ppermute(value, axis, pairs)


def from_behind(value, axis, steps):
    count = lax.axis_size(axis)
    initial, last = (max(0, -steps), min(count, count - steps))
    return lax.ppermute(value, axis, [(source, source + steps) for source in range(initial, last)])


def layer_norm(values, gain, shift):
    center = values - jnp.mean(values, axis=-1, keepdims=True)
    spread = jnp.mean(center * center, axis=-1, keepdims=True)
    return center * lax.rsqrt(spread + 1e-05) * gain + shift


def block_scores(q_heads, k_heads, q_pos, key_pos):
    scores = (
        jnp.einsum("qhd,khd->hqk", q_heads, k_heads, preferred_element_type=jnp.float32) * 0.125
    )
    allowed = key_pos[None, :] <= q_pos[:, None]
    return (scores, allowed)


def local(
    inputs,
    qkv_weight,
    qv_bias,
    out_weight,
    out_bias,
    up_weight,
    up_bias,
    down_weight,
    down_bias,
    first_gain,
    first_shift,
    second_gain,
    second_shift,
    grad_output,
):
    shape = inputs.shape
    width = shape[-1]
    rows = inputs.reshape(-1, width).astype(jnp.float32)
    count = rows.shape[0]
    ctx_size = lax.axis_size("ctx")
    place = lax.axis_index("ctx")
    positions = place * count + jnp.arange(count)
    gathered = (
        lax.all_gather(qkv_weight, "dp", axis=0, tiled=True),
        lax.all_gather(qv_bias, "dp", axis=2, tiled=True),
        lax.all_gather(out_weight, "dp", axis=1, tiled=True),
        lax.all_gather(out_bias, "dp", axis=0, tiled=True),
        lax.all_gather(up_weight, "dp", axis=0, tiled=True),
        lax.all_gather(up_bias, "dp", axis=1, tiled=True),
        lax.all_gather(down_weight, "dp", axis=1, tiled=True),
        lax.all_gather(down_bias, "dp", axis=0, tiled=True),
        lax.all_gather(first_gain, "dp", axis=0, tiled=True),
        lax.all_gather(first_shift, "dp", axis=0, tiled=True),
        lax.all_gather(second_gain, "dp", axis=0, tiled=True),
        lax.all_gather(second_shift, "dp", axis=0, tiled=True),
    )
    (
        attn_in,
        bias_in,
        attn_out,
        bias_out,
        mlp_up,
        bias_up,
        mlp_down,
        bias_down,
        gain_one,
        shift_one,
        gain_two,
        shift_two,
    ) = gathered
    half_width = attn_in.shape[2]
    heads = half_width // HEAD_DIM
    normed_one = layer_norm(rows, gain_one.astype(jnp.float32), shift_one.astype(jnp.float32))
    normed_low = normed_one.astype(jnp.bfloat16)
    mixed = jnp.einsum("td,dch->tch", normed_low, attn_in, preferred_element_type=jnp.float32)
    query = (mixed[:, 0] + bias_in[0].reshape(-1).astype(jnp.float32)).astype(jnp.bfloat16)
    keys = mixed[:, 1].astype(jnp.bfloat16)
    values = (mixed[:, 2] + bias_in[1].reshape(-1).astype(jnp.float32)).astype(jnp.bfloat16)
    q_heads = query.reshape(count, heads, HEAD_DIM)
    k_heads = lax.all_gather(keys, "ctx", axis=0, tiled=True).reshape(-1, heads, HEAD_DIM)
    v_heads = lax.all_gather(values, "ctx", axis=0, tiled=True).reshape(-1, heads, HEAD_DIM)
    key_pos = jnp.arange(k_heads.shape[0])
    peak = jnp.full((heads, count), -1e30, jnp.float32)
    scores, allowed = block_scores(q_heads, k_heads, positions, key_pos)
    masked = jnp.where(allowed[None], scores, -1e30)
    new_peak = jnp.maximum(peak, jnp.max(masked, axis=2))
    weights = jnp.where(allowed[None], jnp.exp(scores - new_peak[:, :, None]), 0.0)
    total = jnp.sum(weights, axis=2)
    accum = jnp.einsum(
        "hqk,khd->hqd", weights.astype(jnp.bfloat16), v_heads, preferred_element_type=jnp.float32
    )
    peak, total, accum = (new_peak, total, accum)
    attn_heads = accum / total[:, :, None]
    log_total = peak + jnp.log(total)
    attended_low = attn_heads.transpose(1, 0, 2).reshape(count, half_width).astype(jnp.bfloat16)
    branch = lax.psum(
        jnp.dot(attended_low, attn_out, preferred_element_type=jnp.float32).astype(jnp.bfloat16),
        "tensor",
    ).astype(jnp.float32)
    resid = rows + branch + bias_out.astype(jnp.float32)
    normed_two = layer_norm(resid, gain_two.astype(jnp.float32), shift_two.astype(jnp.float32))
    normed_two_low = normed_two.astype(jnp.bfloat16)
    hidden_pre = jnp.dot(
        normed_two_low, mlp_up, preferred_element_type=jnp.float32
    ) + bias_up.reshape(-1).astype(jnp.float32)
    hidden_act = jax.nn.gelu(hidden_pre, approximate=True).astype(jnp.bfloat16)
    mlp_part = lax.psum(
        jnp.dot(hidden_act, mlp_down, preferred_element_type=jnp.float32).astype(jnp.bfloat16),
        "tensor",
    ).astype(jnp.float32)
    output = (resid + mlp_part + bias_down.astype(jnp.float32)).astype(jnp.bfloat16).reshape(shape)
    again = (
        lax.all_gather(qkv_weight, "dp", axis=0, tiled=True),
        lax.all_gather(qv_bias, "dp", axis=2, tiled=True),
        lax.all_gather(out_weight, "dp", axis=1, tiled=True),
        lax.all_gather(out_bias, "dp", axis=0, tiled=True),
        lax.all_gather(up_weight, "dp", axis=0, tiled=True),
        lax.all_gather(up_bias, "dp", axis=1, tiled=True),
        lax.all_gather(down_weight, "dp", axis=1, tiled=True),
        lax.all_gather(down_bias, "dp", axis=0, tiled=True),
        lax.all_gather(first_gain, "dp", axis=0, tiled=True),
        lax.all_gather(first_shift, "dp", axis=0, tiled=True),
        lax.all_gather(second_gain, "dp", axis=0, tiled=True),
        lax.all_gather(second_shift, "dp", axis=0, tiled=True),
    )
    (
        back_in,
        unused_bias_in,
        back_out,
        unused_bias_out,
        back_up,
        unused_bias_up,
        back_down,
        unused_bias_down,
        back_gain_one,
        back_shift_one,
        back_gain_two,
        back_shift_two,
    ) = again
    grad_rows = grad_output.reshape(count, width)
    grad_float = grad_rows.astype(jnp.float32)
    grad_bias_down = jnp.sum(grad_float, axis=0)
    grad_down = jnp.einsum("tf,td->fd", hidden_act, grad_rows, preferred_element_type=jnp.float32)
    grad_act = jnp.einsum("td,fd->tf", grad_rows, back_down, preferred_element_type=jnp.float32)
    unused_act, gelu_pull = jax.vjp(lambda pre: jax.nn.gelu(pre, approximate=True), hidden_pre)
    grad_pre = gelu_pull(grad_act)[0].astype(jnp.bfloat16)
    grad_bias_up = jnp.sum(grad_pre, axis=0, dtype=jnp.float32)
    grad_up = jnp.einsum("td,tf->df", normed_two_low, grad_pre, preferred_element_type=jnp.float32)
    grad_normed_two = lax.psum(
        jnp.einsum("tf,df->td", grad_pre, back_up, preferred_element_type=jnp.float32).astype(
            jnp.bfloat16
        ),
        "tensor",
    ).astype(jnp.float32)
    unused_two, second_pull = jax.vjp(
        layer_norm, resid, back_gain_two.astype(jnp.float32), back_shift_two.astype(jnp.float32)
    )
    grad_resid_norm, grad_gain_two, grad_shift_two = second_pull(grad_normed_two)
    grad_resid = grad_float + grad_resid_norm
    grad_branch = grad_resid.astype(jnp.bfloat16)
    grad_bias_out = jnp.sum(grad_branch, axis=0, dtype=jnp.float32)
    grad_attn_out = jnp.einsum(
        "th,td->hd", attended_low, grad_branch, preferred_element_type=jnp.float32
    )
    grad_attended = jnp.einsum(
        "td,hd->th", grad_branch, back_out, preferred_element_type=jnp.float32
    ).astype(jnp.bfloat16)
    grad_heads = grad_attended.reshape(count, heads, HEAD_DIM)
    delta = jnp.einsum("qhd,hqd->hq", grad_heads.astype(jnp.float32), attn_heads)

    def cycle_step(step, carry):
        key_block, value_block, grad_keys, grad_values, grad_query = carry
        anchor = (place - step) % ctx_size
        start = anchor * count
        k_heads = key_block.reshape(count, heads, HEAD_DIM)
        v_heads = value_block.reshape(count, heads, HEAD_DIM)
        key_pos = start + jnp.arange(count)
        cycle_grad_keys = grad_keys
        cycle_grad_values = grad_values
        cycle_grad_query = grad_query
        scores, allowed = block_scores(q_heads, k_heads, positions, key_pos)
        probs = jnp.where(allowed[None], jnp.exp(scores - log_total[:, :, None]), 0.0)
        grad_probs = jnp.einsum(
            "qhd,khd->hqk", grad_heads, v_heads, preferred_element_type=jnp.float32
        )
        grad_scores = (probs * (grad_probs - delta[:, :, None])).astype(jnp.bfloat16)
        cycle_grad_values = cycle_grad_values + jnp.einsum(
            "hqk,qhd->khd",
            probs.astype(jnp.bfloat16),
            grad_heads,
            preferred_element_type=jnp.float32,
        )
        cycle_grad_keys = cycle_grad_keys + 0.125 * jnp.einsum(
            "hqk,qhd->khd", grad_scores, q_heads, preferred_element_type=jnp.float32
        )
        cycle_grad_query = cycle_grad_query + 0.125 * jnp.einsum(
            "hqk,khd->qhd", grad_scores, k_heads, preferred_element_type=jnp.float32
        )
        grad_keys = cycle_grad_keys
        grad_values = cycle_grad_values
        grad_keys, grad_values = (
            shifted(grad_keys.astype(jnp.bfloat16), "ctx", 1).astype(grad_keys.dtype),
            shifted(grad_values.astype(jnp.bfloat16), "ctx", 1).astype(grad_values.dtype),
        )
        key_block, value_block = from_behind((key_block, value_block), "ctx", 1)
        return (key_block, value_block, grad_keys, grad_values, cycle_grad_query)

    zero_heads = jnp.zeros((count, heads, HEAD_DIM), jnp.float32)
    cycle_state = lax.fori_loop(
        0, ctx_size, cycle_step, (keys, values, zero_heads, zero_heads, zero_heads)
    )
    grad_mixed = jnp.stack(
        [
            cycle_state[4].reshape(count, half_width),
            cycle_state[2].reshape(count, half_width),
            cycle_state[3].reshape(count, half_width),
        ],
        axis=1,
    ).astype(jnp.bfloat16)
    grad_bias_in = jnp.sum(grad_mixed[:, 0::2], axis=0, dtype=jnp.float32).reshape(
        2, heads, HEAD_DIM
    )
    grad_attn_in = jnp.einsum(
        "td,tch->dch", normed_low, grad_mixed, preferred_element_type=jnp.float32
    )
    grad_normed_one = lax.psum(
        jnp.einsum("tch,dch->td", grad_mixed, back_in, preferred_element_type=jnp.float32).astype(
            jnp.bfloat16
        ),
        "tensor",
    ).astype(jnp.float32)
    unused_one, first_pull = jax.vjp(
        layer_norm, rows, back_gain_one.astype(jnp.float32), back_shift_one.astype(jnp.float32)
    )
    grad_rows_norm, grad_gain_one, grad_shift_one = first_pull(grad_normed_one)
    grad_inputs = (grad_resid + grad_rows_norm).astype(jnp.bfloat16).reshape(shape)
    grad_bias_rows = grad_bias_up.reshape(-1, 64)
    summed = (
        lax.psum(grad_attn_in.astype(jnp.bfloat16), "ctx").astype(jnp.float32),
        lax.psum(grad_bias_in.astype(jnp.bfloat16), "ctx").astype(jnp.float32),
        lax.psum(grad_attn_out.astype(jnp.bfloat16), "ctx").astype(jnp.float32),
        lax.psum(grad_bias_out.astype(jnp.bfloat16), "ctx").astype(jnp.float32),
        lax.psum(grad_up.astype(jnp.bfloat16), "ctx").astype(jnp.float32),
        lax.psum(grad_bias_rows.astype(jnp.bfloat16), "ctx").astype(jnp.float32),
        lax.psum(grad_down.astype(jnp.bfloat16), "ctx").astype(jnp.float32),
        lax.psum(grad_bias_down.astype(jnp.bfloat16), "ctx").astype(jnp.float32),
        lax.psum(grad_gain_one.astype(jnp.bfloat16), "ctx").astype(jnp.float32),
        lax.psum(grad_shift_one.astype(jnp.bfloat16), "ctx").astype(jnp.float32),
        lax.psum(grad_gain_two.astype(jnp.bfloat16), "ctx").astype(jnp.float32),
        lax.psum(grad_shift_two.astype(jnp.bfloat16), "ctx").astype(jnp.float32),
    )
    (
        summed_a,
        summed_b,
        summed_c,
        summed_d,
        summed_e,
        summed_f,
        summed_g,
        summed_h,
        summed_i,
        summed_j,
        summed_k,
        summed_l,
    ) = summed
    final = (
        lax.psum_scatter(
            summed_a.astype(jnp.bfloat16), "dp", scatter_dimension=0, tiled=True
        ).astype(jnp.float32),
        lax.psum_scatter(
            summed_b.astype(jnp.bfloat16), "dp", scatter_dimension=2, tiled=True
        ).astype(jnp.float32),
        lax.psum_scatter(
            summed_c.astype(jnp.bfloat16), "dp", scatter_dimension=1, tiled=True
        ).astype(jnp.float32),
        lax.psum_scatter(
            summed_d.astype(jnp.bfloat16), "dp", scatter_dimension=0, tiled=True
        ).astype(jnp.float32),
        lax.psum_scatter(
            summed_e.astype(jnp.bfloat16), "dp", scatter_dimension=0, tiled=True
        ).astype(jnp.float32),
        lax.psum_scatter(
            summed_f.astype(jnp.bfloat16), "dp", scatter_dimension=1, tiled=True
        ).astype(jnp.float32),
        lax.psum_scatter(
            summed_g.astype(jnp.bfloat16), "dp", scatter_dimension=1, tiled=True
        ).astype(jnp.float32),
        lax.psum_scatter(
            summed_h.astype(jnp.bfloat16), "dp", scatter_dimension=0, tiled=True
        ).astype(jnp.float32),
        lax.psum_scatter(
            summed_i.astype(jnp.bfloat16), "dp", scatter_dimension=0, tiled=True
        ).astype(jnp.float32),
        lax.psum_scatter(
            summed_j.astype(jnp.bfloat16), "dp", scatter_dimension=0, tiled=True
        ).astype(jnp.float32),
        lax.psum_scatter(
            summed_k.astype(jnp.bfloat16), "dp", scatter_dimension=0, tiled=True
        ).astype(jnp.float32),
        lax.psum_scatter(
            summed_l.astype(jnp.bfloat16), "dp", scatter_dimension=0, tiled=True
        ).astype(jnp.float32),
    )
    return (
        output,
        grad_inputs,
        final[0],
        final[1],
        final[2],
        final[3],
        final[4],
        final[5],
        final[6],
        final[7],
        final[8],
        final[9],
        final[10],
        final[11],
    )


def solution(mesh):
    in_specs = (
        P("dp", "ctx", None),
        P("dp", None, "tensor"),
        P(None, "tensor", "dp"),
        P("tensor", "dp"),
        P("dp"),
        P("dp", "tensor"),
        P("tensor", "dp"),
        P("tensor", "dp"),
        P("dp"),
        P("dp"),
        P("dp"),
        P("dp"),
        P("dp"),
        P("dp", "ctx", None),
    )
    out_specs = (
        P("dp", "ctx", None),
        P("dp", "ctx", None),
        P("dp", None, "tensor"),
        P(None, "tensor", "dp"),
        P("tensor", "dp"),
        P("dp"),
        P("dp", "tensor"),
        P("tensor", "dp"),
        P("tensor", "dp"),
        P("dp"),
        P("dp"),
        P("dp"),
        P("dp"),
        P("dp"),
    )
    return jax.shard_map(local, mesh=mesh, in_specs=in_specs, out_specs=out_specs, check_vma=False)
```

profile of v0, /device:TPU:0, one launch (start us, length us, event | category | flops | bytes accessed | tf_op | source)
XLA Modules:
  0.0 957.6 jit_solution(9288797184443283257)
XLA Ops:
  9.7 6.0 all-gather.1
  15.7 5.4 all-gather.2
  22.3 19.5 %all-gather.14.cloned.1.call-done = bf16[1024,3,512]{0,2,1:T(8,128)(2,1)} async-done(((bf16[256,3,512]{0,2,1:T(8,128)(2,1)}), bf16[1024,3,512]{0,2,1:T(8,128)(2,1)}) %all-gather.14.cloned.1.call-update) | async-done | bytes 3145744 | tf_op jit(solution)/shard_map/all_gather | solution.py:59
  41.8 3.9 fusion.74
  48.5 5.2 all_gather.51
  59.5 35.1 %all-gather.24.cloned.1.call-done = bf16[2048,1,512]{0,2,1:T(8,128)(2,1)} async-done(((bf16[512,1,512]{0,2,1:T(8,128)(2,1)}), bf16[2048,1,512]{0,2,1:T(8,128)(2,1)}) %all-gather.24.cloned.1.call-update) | async-done | bytes 2097168 | tf_op jit(solution)/shard_map/all_gather | solution.py:95
  94.5 15.8 %select_reduce_fusion = (f32[8,512]{1,0:T(8,128)S(1)}, f32[8,512,2048]{2,1,0:T(8,128)}) fusion(pred[512,2048]{1,0:T(8,128)(4,1)S(1)} %iota_compare_fusion, bf16[512,8,64]{0,2,1:T(8,128)(2,1)S(1)} %add_convert_fusion.3, bf16[2048,8,64]{0,2,1:T(8,128)(2,1)} %bitcast.204), kind=kOutput, calls=%fused_computation.22 | convolution fusion | flops 1098903552 | bytes 37240832 | tf_op jit(solution)/shard_map/qhd,khd->hqk/dot_general | solution.py:29
  110.3 15.3 %fusion.22 = f32[8,512]{1,0:T(8,128)S(1)} fusion(f32[8,512,2048]{2,1,0:T(8,128)} %get-tuple-element.474, f32[8,512]{1,0:T(8,128)S(1)} %broadcast_maximum_fusion, pred[512,2048]{1,0:T(8,128)(4,1)S(1)} %iota_compare_fusion), kind=kLoop, calls=%fused_computation.23 | loop fusion | flops 33550336 | bytes 34635776 | tf_op jit(solution)/shard_map/reduce_sum | solution.py:103
  125.6 15.5 %all-gather.16.cloned.1.call-done = bf16[2048,512]{0,1:T(8,128)(2,1)} async-done(((bf16[512,512]{0,1:T(8,128)(2,1)}), bf16[2048,512]{0,1:T(8,128)(2,1)}) %all-gather.16.cloned.1.call-update) | async-done | bytes 2097168 | tf_op jit(solution)/shard_map/all_gather | solution.py:96
  141.2 15.8 %fusion.66 = (bf16[512,8,64]{0,2,1:T(8,128)(2,1)S(1)}, f32[8,512,64]{1,2,0:T(8,128)}) fusion(f32[512,8]{0,1:T(8,128)S(1)} %bitcast.218, bf16[2048,8,64]{0,2,1:T(8,128)(2,1)} %bitcast.240, f32[8,512,2048]{2,1,0:T(8,128)} %get-tuple-element.474, f32[8,512]{1,0:T(8,128)S(1)} %broadcast_maximum_fusion, pred[512,2048]{1,0:T(8,128)(4,1)S(1)} %iota_compare_fusion), kind=kOutput, calls=%fused_computation.95 | convolution fusion | flops 1107820544 | bytes 38305792 | tf_op jit(solution)/shard_map/hqk,khd->hqd/dot_general | solution.py:104
  162.5 5.1 all-gather.3
  167.6 5.1 all-gather.4
  172.7 5.1 all-gather.5
  177.8 5.3 all_gather.59
  183.3 18.1 %all-reduce.15.cloned.1.call-done = bf16[512,1024]{1,0:T(8,128)(2,1)} async-done(((bf16[512,1024]{1,0:T(8,128)(2,1)}), bf16[512,1024]{1,0:T(8,128)(2,1)}) %all-reduce.15.cloned.1.call-update) | async-done | bytes 1048592 | tf_op jit(solution)/shard_map/psum | solution.py:111
  203.7 33.7 %all-gather.20.cloned.1.call-done = bf16[1024,2048]{1,0:T(8,128)(2,1)} async-done(((bf16[256,2048]{1,0:T(8,128)(2,1)}), bf16[1024,2048]{1,0:T(8,128)(2,1)}) %all-gather.20.cloned.1.call-update) | async-done | bytes 4194320 | tf_op jit(solution)/shard_map/all_gather | solution.py:63
  237.4 6.8 fusion.72
  244.2 29.9 %all-gather.22.cloned.1.call-done = bf16[2048,1024]{1,0:T(8,128)(2,1)} async-done(((bf16[2048,256]{1,0:T(8,128)(2,1)}), bf16[2048,1024]{1,0:T(8,128)(2,1)}) %all-gather.22.cloned.1.call-update) | async-done | bytes 4194320 | tf_op jit(solution)/shard_map/all_gather | solution.py:65
  274.1 8.7 fusion.81
  284.1 3.4 convolution_convert_fusion.5
  289.7 38.0 %all-reduce.17.cloned.1.call-done = bf16[512,1024]{1,0:T(8,128)(2,1)} async-done(((bf16[512,1024]{1,0:T(8,128)(2,1)}), bf16[512,1024]{1,0:T(8,128)(2,1)}) %all-reduce.17.cloned.1.call-update) | async-done | bytes 1048592 | tf_op jit(solution)/shard_map/psum | solution.py:164
  336.2 3.4 fusion.60
  339.6 228.5 %while.24 = (s32[]{:T(128)}, bf16[512,512]{0,1:T(8,128)(2,1)}, bf16[512,512]{0,1:T(8,128)(2,1)}, f32[512,8,64]{0,2,1:T(8,128)S(1)}, f32[512,8,64]{0,2,1:T(8,128)...) while((s32[]{:T(128)}, bf16[512,512]{0,1:T(8,128)(2,1)}, ...), condition=%wide.region_12.13_spmd.clone, body=%wide.region_11.12_spmd.clone.sunk | while | flops 1366557696 | bytes 92594792 | solution.py:224
  344.1 4.5 multiply_convert_fusion.5
  352.3 2.9 fusion.135
  356.7 4.2 collective-permute-start
  363.3 3.6 fusion.136
  369.1 8.7 collective-permute-done.3
  379.9 7.4 collective-permute-done
  387.3 10.1 %collective-permute-done.1 = bf16[512,512]{0,1:T(8,128)(2,1)} collective-permute-done((bf16[512,512]{0,1:T(8,128)(2,1)}, bf16[512,512]{0,1:T(8,128)(2,1)}, u32[]{:S(2)}, u32[]{:S(2)}) %collective-permute-start.1) | collective-permute-done | bytes 524320 | tf_op jit(solution)/shard_map/while/body/eval_jaxpr/ppermute | solution.py:18
  401.9 4.5 multiply_convert_fusion.5
  415.4 4.2 collective-permute-start
  421.7 3.6 fusion.136
  427.5 7.8 collective-permute-done.3
  437.5 8.5 collective-permute-done
  446.0 9.2 collective-permute-done.1
  459.7 4.5 multiply_convert_fusion.5
  473.2 4.2 collective-permute-start
  479.6 3.6 fusion.136
  485.3 7.4 collective-permute-done.3
  494.9 9.0 collective-permute-done
  503.9 8.3 collective-permute-done.1
  516.6 4.5 multiply_convert_fusion.5
  530.2 4.2 collective-permute-start
  536.5 3.6 fusion.136
  542.2 7.4 collective-permute-done.3
  551.8 9.0 collective-permute-done
  560.8 7.3 collective-permute-done.1
  571.8 3.7 convolution_convert_fusion.2
  576.7 6.2 convolution_convert_fusion.1
  584.0 8.0 convolution_convert_fusion
  593.1 7.9 convolution_convert_fusion.6
  602.3 5.1 bitcast_convert_fusion
  607.5 7.3 reduce-scatter.11.cloned.1.call-done
  614.9 47.1 %reduce-scatter.15.cloned.1.call-done = bf16[256,2048]{1,0:T(8,128)(2,1)} async-done(((bf16[1024,2048]{1,0:T(8,128)(2,1)}), bf16[256,2048]{1,0:T(8,128)(2,1)}) %reduce-scatter.15.cloned.1.call-update) | async-done | bytes 1048592 | tf_op jit(solution)/shard_map/reduce_scatter | solution.py:294
  662.0 47.1 %reduce-scatter.17.cloned.1.call-done = bf16[2048,256]{1,0:T(8,128)(2,1)} async-done(((bf16[2048,1024]{1,0:T(8,128)(2,1)}), bf16[2048,256]{1,0:T(8,128)(2,1)}) %reduce-scatter.17.cloned.1.call-update) | async-done | bytes 1048592 | tf_op jit(solution)/shard_map/reduce_scatter | solution.py:300
  709.7 5.1 all-gather.6
  716.0 15.4 %reduce-scatter.21.cloned.1.call-done = bf16[16,32]{1,0:T(8,128)(2,1)} async-done(((bf16[64,32]{1,0:T(8,128)(2,1)}), bf16[16,32]{1,0:T(8,128)(2,1)}) %reduce-scatter.21.cloned.1.call-update) | async-done | bytes 1040
  732.2 21.0 %reduce-scatter.19.cloned.1.call-done = bf16[16,16]{1,0:T(8,128)(2,1)} async-done(((bf16[64,16]{1,0:T(8,128)(2,1)}), bf16[16,16]{1,0:T(8,128)(2,1)}) %reduce-scatter.19.cloned.1.call-update) | async-done | bytes 528
  754.0 65.1 %all-reduce.21.cloned.1.call-done = (bf16[512,1024]{1,0:T(8,128)(2,1)}, bf16[512,1024]{1,0:T(8,128)(2,1)}) async-done(((bf16[512,1024]{1,0:T(8,128)(2,1)}, bf16[512,1024]{1,0:T(8,128)(2,1)}), (bf16[512,1024]{1,0:T(8,128)(2,1)}, bf16[512,1024]{1,0:T(8,128)(2,1)})) %all-reduce.21.cloned.1.call-update) | async-done | bytes 2097168 | tf_op jit(solution)/shard_map/psum | solution.py:241
  823.6 11.5 %all-reduce.8 = (bf16[1024]{0:T(1024)(128)(2,1)S(1)}, bf16[1024]{0:T(1024)(128)(2,1)S(1)}, bf16[1024]{0:T(1024)(128)(2,1)S(1)}, bf16[1024]{0:T(1024)(128)(2,1)S(...) all-reduce(bf16[1024]{0:T(1024)(128)(2,1)S(1)} %get-tuple-element.4, ...), channel_id=6, replica_groups=mesh['dp'=4,'ctx'=4,'tensor'=2] {'dp'}, use_global_device_ids=true, to_apply=%region_25.26.clone | all-reduce | flops 6144 | bytes 24576
  835.6 19.8 %all-reduce.6 = (bf16[32,16]{1,0:T(8,128)(2,1)S(1)}, bf16[2,8,16]{2,1,0:T(8,128)(2,1)S(1)}, bf16[256]{0:T(256)(128)(2,1)S(1)}, bf16[256]{0:T(256)(128)(2,1)S(1)}...) all-reduce(bf16[32,16]{1,0:T(8,128)(2,1)S(1)} %copy.97, ...), channel_id=1, replica_groups=mesh['dp'=4,'ctx'=4,'tensor'=2] {'ctx'}, use_global_device_ids=true, to_apply=%region_29.30 | all-reduce | flops 2304 | bytes 9216 | tf_op jit(solution)/shard_map/psum | solution.py:259
  860.1 4.5 fusion.67
  864.5 79.8 %all-reduce.19.cloned.1.call-done = (bf16[256,3,512]{2,0,1:T(8,128)(2,1)}, bf16[512,256]{1,0:T(8,128)(2,1)}, bf16[256,2048]{1,0:T(8,128)(2,1)}, bf16[2048,256]{1,0:T(8,128)(2,1)}) async-done(((bf16[256,3,512]{2,0,1:T(8,128)(2,1)}, bf16[512,256]{1,0:T(8,128)(2,1)}, bf16[256,2048]{1,0:T(8,128)(2,1)}, bf16[2048,256]{1,0:T(8,128)(2,1)}), (bf16[256,3,512]{2,0,1:T(8,128)(2,1)}, bf16[512,256]{1,0:T(8,128)(2,1)}, ...) | async-done | bytes 3145744 | tf_op jit(solution)/shard_map/psum | solution.py:254
  (301 shorter events, 135.0 us)
Async XLA Ops:
  7.2 2.5 copy-start.37
  7.2 8.5 copy-start.38
  7.2 13.9 %copy-start.1 = (bf16[1,512,1024]{2,1,0:T(8,128)(2,1)S(1)}, bf16[1,512,1024]{2,1,0:T(8,128)(2,1)}, u32[]{:S(2)}) copy-start(bf16[1,512,1024]{2,1,0:T(8,128)(2,1)} %param.16) | copy-start | bytes 3145732
  7.2 34.6 %all-gather.14.cloned.1.call-start = ((), (), s32[]{:S(2)}) async-start(), calls=%async_computation.6 | async-start | bytes 3932160 | tf_op jit(solution)/shard_map/all_gather | solution.py:59
  9.6 84.9 %all-gather.24.cloned.1.call-start = ((), (), s32[]{:S(2)}) async-start(), calls=%async_computation.13 | async-start | bytes 2621440 | tf_op jit(solution)/shard_map/all_gather | solution.py:95
  15.7 30.1 %copy-start.24 = (f32[4,1,256]{2,1,0:T(1,128)}, f32[4,1,256]{2,1,0:T(1,128)S(1)}, u32[]{:S(2)}) copy-start(f32[4,1,256]{2,1,0:T(1,128)S(1)} %convert_element_type.342) | copy-start | bytes 12292
  21.1 24.7 %copy-start.34 = (f32[4,1,256]{2,1,0:T(1,128)}, f32[4,1,256]{2,1,0:T(1,128)S(1)}, u32[]{:S(2)}) copy-start(f32[4,1,256]{2,1,0:T(1,128)S(1)} %convert_element_type.343) | copy-start | bytes 12292
  21.3 24.5 %copy-start.26 = (f32[512]{0:T(512)}, f32[512]{0:T(512)S(1)}, u32[]{:S(2)}) copy-start(f32[512]{0:T(512)S(1)} %broadcast_multiply_fusion.1) | copy-start | bytes 6148
  22.3 23.5 %copy-start.30 = (f32[512]{0:T(512)}, f32[512]{0:T(512)S(1)}, u32[]{:S(2)}) copy-start(f32[512]{0:T(512)S(1)} %fusion.68) | copy-start | bytes 6148
  41.8 6.6 copy-start.32
  48.4 92.8 %all-gather.16.cloned.1.call-start = ((), (), s32[]{:S(2)}) async-start(), calls=%async_computation.7 | async-start | bytes 2621440 | tf_op jit(solution)/shard_map/all_gather | solution.py:96
  56.2 102.0 %all-gather.18.cloned.1.call-start = ((), (), s32[]{:S(2)}) async-start(), calls=%async_computation.8 | async-start | bytes 1310720 | tf_op jit(solution)/shard_map/all_gather | solution.py:61
  56.8 144.6 %all-reduce.15.cloned.1.call-start = ((), (), s32[]{:S(2)}) async-start(), calls=%async_computation.9 | async-start | bytes 2097152 | tf_op jit(solution)/shard_map/psum | solution.py:111
  161.1 6.5 copy-start.40
  161.1 11.6 %copy-start.41 = (bf16[256]{0:T(256)(128)(2,1)S(1)}, bf16[256]{0:T(256)(128)(2,1)}, u32[]{:S(2)}) copy-start(bf16[256]{0:T(256)(128)(2,1)} %param.28) | copy-start | bytes 1540
  161.1 16.7 %copy-start.33 = (bf16[32,16]{0,1:T(8,128)(2,1)S(1)}, bf16[32,16]{0,1:T(8,128)(2,1)}, u32[]{:S(2)}) copy-start(bf16[32,16]{0,1:T(8,128)(2,1)} %param.22) | copy-start | bytes 3076
  161.1 76.3 %all-gather.20.cloned.1.call-start = ((), (), s32[]{:S(2)}) async-start(), calls=%async_computation.10 | async-start | bytes 5242880 | tf_op jit(solution)/shard_map/all_gather | solution.py:63
  161.7 112.4 %all-gather.22.cloned.1.call-start = ((), (), s32[]{:S(2)}) async-start(), calls=%async_computation.11 | async-start | bytes 5242880 | tf_op jit(solution)/shard_map/all_gather | solution.py:65
  162.5 165.2 %all-reduce.17.cloned.1.call-start = ((), (), s32[]{:S(2)}) async-start(), calls=%async_computation.12 | async-start | bytes 2097152 | tf_op jit(solution)/shard_map/psum | solution.py:164
  274.1 10.0 %copy-start.36 = (bf16[1024,2048]{1,0:T(8,128)(2,1)S(1)}, bf16[1024,2048]{1,0:T(8,128)(2,1)}, u32[]{:S(2)}) copy-start(bf16[1024,2048]{1,0:T(8,128)(2,1)} %all-gather.20.cloned.1.call-done) | copy-start | bytes 12582916
  287.5 320.1 %reduce-scatter.13.cloned.1.call-start = ((), (), s32[]{:S(2)}) async-start(), calls=%async_computation.15 | async-start | bytes 1310720 | tf_op jit(solution)/shard_map/reduce_scatter | solution.py:288
  327.7 2.4 copy-start.3
  327.7 2.5 copy-start.8
  331.5 2.5 copy-start.44
  335.8 279.1 %reduce-scatter.11.cloned.1.call-start = ((), (), s32[]{:S(2)}) async-start(), calls=%async_computation.14 | async-start | bytes 3932160 | tf_op jit(solution)/shard_map/reduce_scatter | solution.py:282
  348.6 3.7 copy-start.20
  350.7 17.2 %collective-permute-start.2 = (bf16[512,8,64]{0,2,1:T(8,128)(2,1)}, bf16[512,8,64]{0,2,1:T(8,128)(2,1)}, u32[]{:S(2)}, u32[]{:S(2)}) collective-permute-start(bf16[512,8,64]{0,2,1:T(8,128)(2,1)} %fusion.134), channel_id=1, source_target_pairs={{0,2},{2,4},{4,6},{6,0},{1,3},{3,5},{5,7},{7,1},{8,10},{10,12},{12... | collective-permute-start | bytes 1572872 | tf_op jit(solution)/shard_map/while/body/eval_jaxpr/ppermute | solution.py:12
  352.3 11.0 %copy-start.5 = (f32[512,8,64]{0,2,1:T(8,128)S(1)}, f32[512,8,64]{0,2,1:T(8,128)}, u32[]{:S(2)}) copy-start(f32[512,8,64]{0,2,1:T(8,128)} %get-tuple-element.576) | copy-start | bytes 3145732 | tf_op jit(solution)/shard_map/while
  355.2 22.5 %collective-permute-start.3 = (bf16[512,8,64]{0,2,1:T(8,128)(2,1)}, bf16[512,8,64]{0,2,1:T(8,128)(2,1)}, u32[]{:S(2)}, u32[]{:S(2)}) collective-permute-start(bf16[512,8,64]{0,2,1:T(8,128)(2,1)} %fusion.135), channel_id=1, source_target_pairs={{0,2},{2,4},{4,6},{6,0},{1,3},{3,5},{5,7},{7,1},{8,10},{10,12},{12... | collective-permute-start | bytes 1572872 | tf_op jit(solution)/shard_map/while/body/eval_jaxpr/ppermute | solution.py:12
  356.7 30.6 %collective-permute-start = (bf16[512,512]{0,1:T(8,128)(2,1)S(1)}, bf16[512,512]{0,1:T(8,128)(2,1)}, u32[]{:S(2)}, u32[]{:S(2)}) collective-permute-start(bf16[512,512]{0,1:T(8,128)(2,1)S(1)} %copy.108), channel_id=1, source_target_pairs={{0,2},{2,4},{4,6},{1,3},{3,5},{5,7},{8,10},{10,12},{12,14},{9,11},... | collective-permute-start | bytes 1572872 | tf_op jit(solution)/shard_map/while/body/eval_jaxpr/ppermute | solution.py:18
  360.9 36.5 %collective-permute-start.1 = (bf16[512,512]{0,1:T(8,128)(2,1)}, bf16[512,512]{0,1:T(8,128)(2,1)}, u32[]{:S(2)}, u32[]{:S(2)}) collective-permute-start(bf16[512,512]{0,1:T(8,128)(2,1)} %copy.109), channel_id=1, source_target_pairs={{0,2},{2,4},{4,6},{1,3},{3,5},{5,7},{8,10},{10,12},{12,14},{9,11},... | collective-permute-start | bytes 1572872 | tf_op jit(solution)/shard_map/while/body/eval_jaxpr/ppermute | solution.py:18
  406.4 4.6 copy-start.20
  408.5 17.8 %collective-permute-start.2 = (bf16[512,8,64]{0,2,1:T(8,128)(2,1)}, bf16[512,8,64]{0,2,1:T(8,128)(2,1)}, u32[]{:S(2)}, u32[]{:S(2)}) collective-permute-start(bf16[512,8,64]{0,2,1:T(8,128)(2,1)} %fusion.134), channel_id=1, source_target_pairs={{0,2},{2,4},{4,6},{6,0},{1,3},{3,5},{5,7},{7,1},{8,10},{10,12},{12... | collective-permute-start | bytes 1572872 | tf_op jit(solution)/shard_map/while/body/eval_jaxpr/ppermute | solution.py:12
  411.0 10.7 %copy-start.5 = (f32[512,8,64]{0,2,1:T(8,128)S(1)}, f32[512,8,64]{0,2,1:T(8,128)}, u32[]{:S(2)}) copy-start(f32[512,8,64]{0,2,1:T(8,128)} %get-tuple-element.576) | copy-start | bytes 3145732 | tf_op jit(solution)/shard_map/while
  413.9 21.4 %collective-permute-start.3 = (bf16[512,8,64]{0,2,1:T(8,128)(2,1)}, bf16[512,8,64]{0,2,1:T(8,128)(2,1)}, u32[]{:S(2)}, u32[]{:S(2)}) collective-permute-start(bf16[512,8,64]{0,2,1:T(8,128)(2,1)} %fusion.135), channel_id=1, source_target_pairs={{0,2},{2,4},{4,6},{6,0},{1,3},{3,5},{5,7},{7,1},{8,10},{10,12},{12... | collective-permute-start | bytes 1572872 | tf_op jit(solution)/shard_map/while/body/eval_jaxpr/ppermute | solution.py:12
  415.4 30.6 %collective-permute-start = (bf16[512,512]{0,1:T(8,128)(2,1)S(1)}, bf16[512,512]{0,1:T(8,128)(2,1)}, u32[]{:S(2)}, u32[]{:S(2)}) collective-permute-start(bf16[512,512]{0,1:T(8,128)(2,1)S(1)} %copy.108), channel_id=1, source_target_pairs={{0,2},{2,4},{4,6},{1,3},{3,5},{5,7},{8,10},{10,12},{12,14},{9,11},... | collective-permute-start | bytes 1572872 | tf_op jit(solution)/shard_map/while/body/eval_jaxpr/ppermute | solution.py:18
  419.6 35.6 %collective-permute-start.1 = (bf16[512,512]{0,1:T(8,128)(2,1)}, bf16[512,512]{0,1:T(8,128)(2,1)}, u32[]{:S(2)}, u32[]{:S(2)}) collective-permute-start(bf16[512,512]{0,1:T(8,128)(2,1)} %copy.109), channel_id=1, source_target_pairs={{0,2},{2,4},{4,6},{1,3},{3,5},{5,7},{8,10},{10,12},{12,14},{9,11},... | collective-permute-start | bytes 1572872 | tf_op jit(solution)/shard_map/while/body/eval_jaxpr/ppermute | solution.py:18
  464.2 4.6 copy-start.20
  466.3 17.8 %collective-permute-start.2 = (bf16[512,8,64]{0,2,1:T(8,128)(2,1)}, bf16[512,8,64]{0,2,1:T(8,128)(2,1)}, u32[]{:S(2)}, u32[]{:S(2)}) collective-permute-start(bf16[512,8,64]{0,2,1:T(8,128)(2,1)} %fusion.134), channel_id=1, source_target_pairs={{0,2},{2,4},{4,6},{6,0},{1,3},{3,5},{5,7},{7,1},{8,10},{10,12},{12... | collective-permute-start | bytes 1572872 | tf_op jit(solution)/shard_map/while/body/eval_jaxpr/ppermute | solution.py:12
  468.8 10.7 %copy-start.5 = (f32[512,8,64]{0,2,1:T(8,128)S(1)}, f32[512,8,64]{0,2,1:T(8,128)}, u32[]{:S(2)}) copy-start(f32[512,8,64]{0,2,1:T(8,128)} %get-tuple-element.576) | copy-start | bytes 3145732 | tf_op jit(solution)/shard_map/while
  471.8 21.0 %collective-permute-start.3 = (bf16[512,8,64]{0,2,1:T(8,128)(2,1)}, bf16[512,8,64]{0,2,1:T(8,128)(2,1)}, u32[]{:S(2)}, u32[]{:S(2)}) collective-permute-start(bf16[512,8,64]{0,2,1:T(8,128)(2,1)} %fusion.135), channel_id=1, source_target_pairs={{0,2},{2,4},{4,6},{6,0},{1,3},{3,5},{5,7},{7,1},{8,10},{10,12},{12... | collective-permute-start | bytes 1572872 | tf_op jit(solution)/shard_map/while/body/eval_jaxpr/ppermute | solution.py:12
  473.2 30.6 %collective-permute-start = (bf16[512,512]{0,1:T(8,128)(2,1)S(1)}, bf16[512,512]{0,1:T(8,128)(2,1)}, u32[]{:S(2)}, u32[]{:S(2)}) collective-permute-start(bf16[512,512]{0,1:T(8,128)(2,1)S(1)} %copy.108), channel_id=1, source_target_pairs={{0,2},{2,4},{4,6},{1,3},{3,5},{5,7},{8,10},{10,12},{12,14},{9,11},... | collective-permute-start | bytes 1572872 | tf_op jit(solution)/shard_map/while/body/eval_jaxpr/ppermute | solution.py:18
  477.4 34.7 %collective-permute-start.1 = (bf16[512,512]{0,1:T(8,128)(2,1)}, bf16[512,512]{0,1:T(8,128)(2,1)}, u32[]{:S(2)}, u32[]{:S(2)}) collective-permute-start(bf16[512,512]{0,1:T(8,128)(2,1)} %copy.109), channel_id=1, source_target_pairs={{0,2},{2,4},{4,6},{1,3},{3,5},{5,7},{8,10},{10,12},{12,14},{9,11},... | collective-permute-start | bytes 1572872 | tf_op jit(solution)/shard_map/while/body/eval_jaxpr/ppermute | solution.py:18
  521.1 4.6 copy-start.20
  523.2 17.8 %collective-permute-start.2 = (bf16[512,8,64]{0,2,1:T(8,128)(2,1)}, bf16[512,8,64]{0,2,1:T(8,128)(2,1)}, u32[]{:S(2)}, u32[]{:S(2)}) collective-permute-start(bf16[512,8,64]{0,2,1:T(8,128)(2,1)} %fusion.134), channel_id=1, source_target_pairs={{0,2},{2,4},{4,6},{6,0},{1,3},{3,5},{5,7},{7,1},{8,10},{10,12},{12... | collective-permute-start | bytes 1572872 | tf_op jit(solution)/shard_map/while/body/eval_jaxpr/ppermute | solution.py:12
  525.7 10.7 %copy-start.5 = (f32[512,8,64]{0,2,1:T(8,128)S(1)}, f32[512,8,64]{0,2,1:T(8,128)}, u32[]{:S(2)}) copy-start(f32[512,8,64]{0,2,1:T(8,128)} %get-tuple-element.576) | copy-start | bytes 3145732 | tf_op jit(solution)/shard_map/while
  528.7 21.0 %collective-permute-start.3 = (bf16[512,8,64]{0,2,1:T(8,128)(2,1)}, bf16[512,8,64]{0,2,1:T(8,128)(2,1)}, u32[]{:S(2)}, u32[]{:S(2)}) collective-permute-start(bf16[512,8,64]{0,2,1:T(8,128)(2,1)} %fusion.135), channel_id=1, source_target_pairs={{0,2},{2,4},{4,6},{6,0},{1,3},{3,5},{5,7},{7,1},{8,10},{10,12},{12... | collective-permute-start | bytes 1572872 | tf_op jit(solution)/shard_map/while/body/eval_jaxpr/ppermute | solution.py:12
  530.2 30.6 %collective-permute-start = (bf16[512,512]{0,1:T(8,128)(2,1)S(1)}, bf16[512,512]{0,1:T(8,128)(2,1)}, u32[]{:S(2)}, u32[]{:S(2)}) collective-permute-start(bf16[512,512]{0,1:T(8,128)(2,1)S(1)} %copy.108), channel_id=1, source_target_pairs={{0,2},{2,4},{4,6},{1,3},{3,5},{5,7},{8,10},{10,12},{12,14},{9,11},... | collective-permute-start | bytes 1572872 | tf_op jit(solution)/shard_map/while/body/eval_jaxpr/ppermute | solution.py:18
  534.4 33.8 %collective-permute-start.1 = (bf16[512,512]{0,1:T(8,128)(2,1)}, bf16[512,512]{0,1:T(8,128)(2,1)}, u32[]{:S(2)}, u32[]{:S(2)}) collective-permute-start(bf16[512,512]{0,1:T(8,128)(2,1)} %copy.109), channel_id=1, source_target_pairs={{0,2},{2,4},{4,6},{1,3},{3,5},{5,7},{8,10},{10,12},{12,14},{9,11},... | collective-permute-start | bytes 1572872 | tf_op jit(solution)/shard_map/while/body/eval_jaxpr/ppermute | solution.py:18
  571.8 3.7 copy-start.17
  575.5 86.5 %reduce-scatter.15.cloned.1.call-start = ((), (), s32[]{:S(2)}) async-start(), calls=%async_computation.16 | async-start | bytes 5242880 | tf_op jit(solution)/shard_map/reduce_scatter | solution.py:294
  582.8 126.2 %reduce-scatter.17.cloned.1.call-start = ((), (), s32[]{:S(2)}) async-start(), calls=%async_computation.17 | async-start | bytes 5242880 | tf_op jit(solution)/shard_map/reduce_scatter | solution.py:300
  592.1 139.3 %reduce-scatter.21.cloned.1.call-start = ((), (), s32[]{:S(2)}) async-start(), calls=%async_computation.19 | async-start | bytes 20480
  593.0 160.2 %reduce-scatter.19.cloned.1.call-start = ((), (), s32[]{:S(2)}) async-start(), calls=%async_computation.18 | async-start | bytes 20480
  593.0 7.9 copy-start.14
  593.0 7.9 copy-start.16
  593.0 7.9 copy-start.18
  602.2 216.8 %all-reduce.21.cloned.1.call-start = ((), (), s32[]{:S(2)}) async-start(), calls=%async_computation.21 | async-start | bytes 4194304 | tf_op jit(solution)/shard_map/psum | solution.py:241
  607.5 336.8 %all-reduce.19.cloned.1.call-start = ((), (), s32[]{:S(2)}) async-start(), calls=%async_computation.20 | async-start | bytes 6291456 | tf_op jit(solution)/shard_map/psum | solution.py:254
  709.1 5.7 copy-start.45
  709.1 113.2 %copy-start.29 = (f32[512]{0:T(512)S(1)}, f32[512]{0:T(512)}, u32[]{:S(2)}) copy-start(f32[512]{0:T(512)} %copy-done.28) | copy-start | bytes 6148
  819.1 3.3 copy-start.7
  944.3 2.9 copy-start.19
  947.2 2.8 copy-start.23
  (30 other events, 44.4 us)
Sparse Core Ops, SparseCore 0:
  10.2 31.6 all-gather.13
  48.5 45.9 all-gather.23
  96.1 45.0 all-gather.15
  142.6 15.5 all-gather.17
  161.3 40.1 all-reduce.14
  202.9 34.4 all-gather.19
  239.0 35.0 all-gather.21
  287.6 40.0 all-reduce.16
  335.9 24.9 reduce-scatter.12
  575.6 39.2 reduce-scatter.10
  617.4 44.5 reduce-scatter.14
  664.5 44.5 reduce-scatter.16
  712.1 19.2 reduce-scatter.20
  733.8 19.2 reduce-scatter.18
  755.9 63.0 all-reduce.20
  821.7 122.5 all-reduce.18
where the time goes:
time: 963 us; the launch traced here: 958 us
  waiting for transfers between devices  576 us (60%)
  matrix products  149 us (15%)
  blocking collectives  73.5 us (8%)
  other arithmetic  63.6 us (7%)
  starting transfers between devices  42.1 us (4%)
  local copies, waits for them, and re-layouts  37.6 us (4%)
  between operations  15.4 us (2%)
    psum x1, waiting for transfers between devices, local(): lax.psum(grad_attn_in.astype(jnp.bfloat16), 'ctx').astype(jnp.float32)  79.8 us
    ppermute x8, waiting for transfers between devices, from_behind(): lax.ppermute(value, axis, [(source, source + steps) for source in range(i...  68.9 us
    psum x1, waiting for transfers between devices, local(): lax.psum(jnp.einsum('tch,dch->td', grad_mixed, back_in, preferred_element...  65.1 us
    reduce_scatter x1, waiting for transfers between devices, local(): lax.psum_scatter(summed_e.astype(jnp.bfloat16), 'dp', scatter_dimension=0...  47.1 us
    reduce_scatter x1, waiting for transfers between devices, local(): lax.psum_scatter(summed_g.astype(jnp.bfloat16), 'dp', scatter_dimension=1...  47.1 us
    unnamed x18, waiting for transfers between devices  38.3 us
    psum x1, waiting for transfers between devices, local(): lax.psum(jnp.einsum('tf,df->td', grad_pre, back_up, preferred_element_typ...  38 us
    all_gather x1, waiting for transfers between devices, local(): lax.all_gather(keys, 'ctx', axis=0, tiled=True).reshape(-1, heads, HEAD_DIM)  35.1 us
  transfers between devices with their start and end apart: 32, of which 27 were waited for; matrix products, arithmetic and copies ran while one was open for 21% of the time, Pallas kernels for 0%

commit v1 on v0

v1 whole, which is shorter than its diff:
```python
import jax
import jax.numpy as jnp
from jax import lax
from jax.experimental import pallas as pl
from jax.experimental.pallas import tpu as pltpu
from jax.sharding import PartitionSpec as P

HEAD_DIM = 64
F32 = jnp.float32
BF16 = jnp.bfloat16
ROWS_BY_ROWS = (((0,), (0,)), ((), ()))
LAST_BY_LAST = (((1,), (1,)), ((), ()))


def ahead(value, axis, steps):
    count = lax.axis_size(axis)
    first, last = (max(0, -steps), min(count, count - steps))
    return lax.ppermute(value, axis, [(source, source + steps) for source in range(first, last)])


def pair_sum(value):
    low = value.astype(BF16)
    if lax.axis_size("tensor") == 2:
        other = lax.ppermute(low, "tensor", [(0, 1), (1, 0)])
        return low.astype(F32) + other.astype(F32)
    return lax.psum(low, "tensor").astype(F32)


def norm_parts(values):
    center = values - jnp.mean(values, axis=-1, keepdims=True)
    scale = lax.rsqrt(jnp.mean(center * center, axis=-1, keepdims=True) + 1e-05)
    return center * scale, scale


def norm_back(grad, xhat, scale, gain):
    scaled = grad * gain
    return scale * (
        scaled
        - jnp.mean(scaled, axis=-1, keepdims=True)
        - xhat * jnp.mean(scaled * xhat, axis=-1, keepdims=True)
    )


def causal(scores):
    key_pos = lax.broadcasted_iota(jnp.int32, scores.shape, 0)
    query_pos = lax.broadcasted_iota(jnp.int32, scores.shape, 1)
    return jnp.where(key_pos <= query_pos, scores, -1e30)


def scores_of(q_ref, k_ref):
    scaled = q_ref[...] * jnp.asarray(0.125, BF16)
    return lax.dot_general(k_ref[...], scaled, ROWS_BY_ROWS, preferred_element_type=F32)


def first_tile(q_ref, k_ref, v_ref, peak_ref, total_ref, accum_ref):
    scores = causal(scores_of(q_ref, k_ref))
    peak = jnp.max(scores, axis=0, keepdims=True)
    weights = jnp.exp(scores - peak)
    peak_ref[0] = peak
    total_ref[0] = jnp.sum(weights, axis=0, keepdims=True)
    accum_ref[...] = jnp.dot(v_ref[...], weights.astype(BF16), preferred_element_type=F32)


def next_tile(distance, place_ref, q_ref, k_ref, v_ref, p_ref, t_ref, a_ref, peak_ref, total_ref, accum_ref):
    valid = place_ref[0] >= distance

    @pl.when(valid)
    def run():
        scores = scores_of(q_ref, k_ref)
        old = p_ref[0]
        peak = jnp.maximum(old, jnp.max(scores, axis=0, keepdims=True))
        weights = jnp.exp(scores - peak)
        fade = jnp.exp(old - peak)
        peak_ref[0] = peak
        total_ref[0] = t_ref[0] * fade + jnp.sum(weights, axis=0, keepdims=True)
        accum_ref[...] = a_ref[...] * fade + jnp.dot(
            v_ref[...], weights.astype(BF16), preferred_element_type=F32
        )

    @pl.when(jnp.logical_not(valid))
    def keep():
        peak_ref[...] = p_ref[...]
        total_ref[...] = t_ref[...]
        accum_ref[...] = a_ref[...]


def back_tile(distance, place_ref, q_ref, k_ref, v_ref, g_ref, lse_ref, delta_ref, dq_ref, dk_ref, dv_ref):
    valid = place_ref[0] >= distance

    @pl.when(valid)
    def run():
        scores = scores_of(q_ref, k_ref)
        if distance == 0:
            scores = causal(scores)
        probs = jnp.exp(scores - lse_ref[0])
        grad_probs = lax.dot_general(
            v_ref[...], g_ref[...], ROWS_BY_ROWS, preferred_element_type=F32
        )
        grad_scores = (probs * (grad_probs - delta_ref[0])).astype(BF16)
        dv_ref[...] = lax.dot_general(
            g_ref[...], probs.astype(BF16), LAST_BY_LAST, preferred_element_type=F32
        )
        dk_ref[...] = 0.125 * lax.dot_general(
            q_ref[...], grad_scores, LAST_BY_LAST, preferred_element_type=F32
        )
        dq_ref[...] = 0.125 * jnp.dot(k_ref[...], grad_scores, preferred_element_type=F32)

    @pl.when(jnp.logical_not(valid))
    def clear():
        dq_ref[...] = jnp.zeros_like(dq_ref)
        dk_ref[...] = jnp.zeros_like(dk_ref)
        dv_ref[...] = jnp.zeros_like(dv_ref)


def tile_call(kernel, place, wide, stats, flops, order):
    width, count = wide[0].shape
    heads = width // HEAD_DIM
    wide_spec = pl.BlockSpec((HEAD_DIM, count), lambda h: (h, 0))
    stat_spec = pl.BlockSpec((1, 1, count), lambda h: (h, 0, 0))
    specs = {"w": wide_spec, "s": stat_spec}
    scalars = [] if place is None else [place]
    scalar_specs = [] if place is None else [pl.BlockSpec(memory_space=pltpu.SMEM)]
    wide_shape = jax.ShapeDtypeStruct((width, count), F32)
    stat_shape = jax.ShapeDtypeStruct((heads, 1, count), F32)
    ins, outs = order
    wide, stats = (list(wide), list(stats))
    args = [wide.pop(0) if kind == "w" else stats.pop(0) for kind in ins]
    return pl.pallas_call(
        kernel,
        grid=(heads,),
        in_specs=scalar_specs + [specs[kind] for kind in ins],
        out_specs=[specs[kind] for kind in outs],
        out_shape=[wide_shape if kind == "w" else stat_shape for kind in outs],
        compiler_params=pltpu.CompilerParams(vmem_limit_bytes=32 * 1024 * 1024),
        cost_estimate=pl.CostEstimate(
            flops=flops * 2 * width * count * count,
            bytes_accessed=6 * width * count * 4,
            transcendentals=heads * count * count,
        ),
    )(*scalars, *args)


def local(
    inputs,
    qkv_weight,
    qv_bias,
    out_weight,
    out_bias,
    up_weight,
    up_bias,
    down_weight,
    down_bias,
    first_gain,
    first_shift,
    second_gain,
    second_shift,
    grad_output,
):
    shape = inputs.shape
    width = shape[-1]
    rows = inputs.reshape(-1, width).astype(F32)
    count = rows.shape[0]
    ctx_size = lax.axis_size("ctx")
    dp_size = lax.axis_size("dp")
    dp_place = lax.axis_index("dp")
    place = lax.axis_index("ctx").astype(jnp.int32).reshape(1)

    attn_in = lax.all_gather(jnp.swapaxes(qkv_weight, 0, 1), "dp", axis=1, tiled=True)
    small = (
        first_gain,
        first_shift,
        second_gain,
        second_shift,
        out_bias,
        down_bias,
        qv_bias,
        up_bias,
    )
    packed = lax.all_gather(jnp.concatenate([item.reshape(-1) for item in small]), "dp")
    packed = packed.astype(F32)
    parts = []
    start = 0
    for item in small:
        part = packed[:, start : start + item.size].reshape((dp_size,) + item.shape)
        start += item.size
        parts.append(jnp.moveaxis(part, 0, -2).reshape(item.shape[:-1] + (-1,)))
    gain_one, shift_one, gain_two, shift_two, bias_out, bias_down, bias_in, bias_up = parts
    attn_out = lax.all_gather(out_weight, "dp", axis=1, tiled=True)
    mlp_up = lax.all_gather(up_weight, "dp", axis=0, tiled=True)
    mlp_down = lax.all_gather(down_weight, "dp", axis=1, tiled=True)

    half_width = attn_in.shape[2]
    heads = half_width // HEAD_DIM
    xhat_one, scale_one = norm_parts(rows)
    normed_low = (xhat_one * gain_one + shift_one).astype(BF16)
    bias_in = bias_in.reshape(2, half_width, 1)
    mixed = jnp.einsum("td,cdh->cht", normed_low, attn_in, preferred_element_type=F32)
    query = (mixed[0] + bias_in[0]).astype(BF16)
    keys = mixed[1].astype(BF16)
    values = (mixed[2] + bias_in[1]).astype(BF16)

    blocks = [jnp.concatenate([keys, values], axis=0)]
    for distance in range(1, ctx_size):
        blocks.append(ahead(blocks[-1], "ctx", 1))
    peak, total, accum = tile_call(
        first_tile, None, (query, keys, values), (), 2, ("www", "ssw")
    )
    pairs = [(keys, values)]
    for distance in range(1, ctx_size):
        block = blocks[distance]
        pairs.append((block[:half_width], block[half_width:]))

        def step(*refs, distance=distance):
            next_tile(distance, *refs)

        peak, total, accum = tile_call(
            step,
            place,
            (query, *pairs[distance], accum),
            (peak, total),
            2,
            ("wwwssw", "ssw"),
        )
    attn_heads = accum.reshape(heads, HEAD_DIM, count) / total
    log_total = peak + jnp.log(total)
    attended_low = attn_heads.reshape(half_width, count).astype(BF16)

    branch = pair_sum(jnp.einsum("ht,hd->td", attended_low, attn_out, preferred_element_type=F32))
    resid = rows + branch + bias_out
    xhat_two, scale_two = norm_parts(resid)
    normed_two_low = (xhat_two * gain_two + shift_two).astype(BF16)
    hidden_pre = jnp.dot(normed_two_low, mlp_up, preferred_element_type=F32) + bias_up.reshape(-1)
    hidden_act, gelu_pull = jax.vjp(lambda pre: jax.nn.gelu(pre, approximate=True), hidden_pre)
    hidden_act = hidden_act.astype(BF16)

    grad_rows = grad_output.reshape(count, width)
    grad_float = grad_rows.astype(F32)
    grad_bias_down = jnp.sum(grad_float, axis=0)
    grad_act = jnp.einsum("td,fd->tf", grad_rows, mlp_down, preferred_element_type=F32)
    grad_pre = gelu_pull(grad_act)[0].astype(BF16)
    grad_normed_two = pair_sum(
        jnp.einsum("tf,df->td", grad_pre, mlp_up, preferred_element_type=F32)
    )
    mlp_part = pair_sum(jnp.dot(hidden_act, mlp_down, preferred_element_type=F32))
    output = (resid + mlp_part + bias_down).astype(BF16).reshape(shape)

    def scattered(value, dimension):
        return lax.psum_scatter(
            value.astype(BF16), "dp", scatter_dimension=dimension, tiled=True
        )

    grad_down = scattered(
        jnp.einsum("tf,td->fd", hidden_act, grad_rows, preferred_element_type=F32), 1
    )
    grad_bias_up = jnp.sum(grad_pre, axis=0, dtype=F32)
    grad_up = scattered(
        jnp.einsum("td,tf->df", normed_two_low, grad_pre, preferred_element_type=F32), 0
    )

    grad_gain_two = jnp.sum(grad_normed_two * xhat_two, axis=0)
    grad_shift_two = jnp.sum(grad_normed_two, axis=0)
    grad_resid = grad_float + norm_back(grad_normed_two, xhat_two, scale_two, gain_two)
    grad_branch = grad_resid.astype(BF16)
    grad_bias_out = jnp.sum(grad_branch, axis=0, dtype=F32)
    grad_attended = jnp.einsum(
        "td,hd->ht", grad_branch, attn_out, preferred_element_type=F32
    ).astype(BF16)
    grad_heads = grad_attended.astype(F32).reshape(heads, HEAD_DIM, count)
    delta = jnp.sum(grad_heads * attn_heads, axis=1, keepdims=True)
    grad_out = scattered(
        jnp.einsum("ht,td->hd", attended_low, grad_branch, preferred_element_type=F32), 1
    )

    grad_query = 0.0
    arrived = None
    for distance in range(ctx_size - 1, -1, -1):

        def back_step(*refs, distance=distance):
            back_tile(distance, *refs)

        part_query, part_keys, part_values = tile_call(
            back_step,
            place,
            (query, *pairs[distance], grad_attended),
            (log_total, delta),
            5,
            ("wwwwss", "www"),
        )
        grad_query = grad_query + part_query
        block = jnp.concatenate([part_keys, part_values], axis=0)
        if arrived is not None:
            block = block + arrived.astype(F32)
        block = block.astype(BF16)
        if distance > 0:
            arrived = ahead(block, "ctx", -1)
    grad_mixed = jnp.concatenate([grad_query.astype(BF16), block], axis=0)
    grad_mixed = grad_mixed.reshape(3, half_width, count)
    grad_bias_in = jnp.sum(grad_mixed[0::2], axis=2, dtype=F32)
    grad_normed_one = pair_sum(
        jnp.einsum("cht,cdh->td", grad_mixed, attn_in, preferred_element_type=F32)
    )
    grad_attn_in = scattered(
        jnp.einsum("td,cht->cdh", normed_low, grad_mixed, preferred_element_type=F32), 1
    )
    grad_gain_one = jnp.sum(grad_normed_one * xhat_one, axis=0)
    grad_shift_one = jnp.sum(grad_normed_one, axis=0)
    grad_inputs = grad_resid + norm_back(grad_normed_one, xhat_one, scale_one, gain_one)
    grad_inputs = grad_inputs.astype(BF16).reshape(shape)

    grad_up, grad_down = [lax.psum(item, "ctx").astype(F32) for item in (grad_up, grad_down)]
    grad_out, grad_attn_in = [
        lax.psum(item, "ctx").astype(F32) for item in (grad_out, grad_attn_in)
    ]
    grad_attn_in = jnp.swapaxes(grad_attn_in, 0, 1)

    grads_small = (
        grad_gain_one,
        grad_shift_one,
        grad_gain_two,
        grad_shift_two,
        grad_bias_out,
        grad_bias_down,
        grad_bias_in,
        grad_bias_up,
    )
    summed = lax.psum(jnp.concatenate([item.reshape(-1) for item in grads_small]), ("dp", "ctx"))
    small_out = []
    start = 0
    for item in small:
        whole = summed[start : start + item.size * dp_size]
        start += item.size * dp_size
        whole = whole.reshape(item.shape[:-1] + (dp_size, item.shape[-1]))
        small_out.append(lax.dynamic_index_in_dim(whole, dp_place, whole.ndim - 2, False))
    (
        grad_gain_one,
        grad_shift_one,
        grad_gain_two,
        grad_shift_two,
        grad_bias_out,
        grad_bias_down,
        grad_bias_in,
        grad_bias_up,
    ) = small_out
    return (
        output,
        grad_inputs,
        grad_attn_in,
        grad_bias_in,
        grad_out,
        grad_bias_out,
        grad_up,
        grad_bias_up,
        grad_down,
        grad_bias_down,
        grad_gain_one,
        grad_shift_one,
        grad_gain_two,
        grad_shift_two,
    )


def solution(mesh):
    in_specs = (
        P("dp", "ctx", None),
        P("dp", None, "tensor"),
        P(None, "tensor", "dp"),
        P("tensor", "dp"),
        P("dp"),
        P("dp", "tensor"),
        P("tensor", "dp"),
        P("tensor", "dp"),
        P("dp"),
        P("dp"),
        P("dp"),
        P("dp"),
        P("dp"),
        P("dp", "ctx", None),
    )
    out_specs = (
        P("dp", "ctx", None),
        P("dp", "ctx", None),
        P("dp", None, "tensor"),
        P(None, "tensor", "dp"),
        P("tensor", "dp"),
        P("dp"),
        P("dp", "tensor"),
        P("tensor", "dp"),
        P("tensor", "dp"),
        P("dp"),
        P("dp"),
        P("dp"),
        P("dp"),
        P("dp"),
    )
    return jax.shard_map(local, mesh=mesh, in_specs=in_specs, out_specs=out_specs, check_vma=False)
```

time: 963 us -> 540 us (0.56)
  waiting for transfers between devices: 576 us -> 312 us
  matrix products: 149 us -> 55.7 us
  other arithmetic: 63.6 us -> 21.7 us
  starting transfers between devices: 42.1 us -> 24.8 us
  local copies, waits for them, and re-layouts: 37.6 us -> 20.8 us
  Pallas kernels: 0 us -> 13.5 us
    psum x4 -> x1, waiting for transfers between devices: 201 us -> 50.9 us  [local(): lax.psum(item, 'ctx').astype(F32)]
    all_gather x6 -> x4, waiting for transfers between devices: 135 us -> 21.4 us  [the longest x1 21.4 us: local(): lax.all_gather(jnp.swapaxes(qkv_weight, 0, 1), 'dp', axis=1, tiled=True)]
    dot_general x33 -> x11, matrix products: 143 us -> 48.9 us  [the longest x1 8.67 us: local(): jnp.einsum('td,fd->tf', grad_rows, mlp_down, preferred_element_type=F32)]
    ppermute x16 -> x10, waiting for transfers between devices: 100 us -> 180 us  [the longest x6 122 us: ahead(): lax.ppermute(value, axis, [(source, source + steps) for source in range(f...]
    psum x1, blocking collectives: 19.8 us -> 64.6 us  [local(): lax.psum(jnp.concatenate([item.reshape(-1) for item in grads_small]), ('d...]
    reduce_scatter x4, waiting for transfers between devices: 102 us -> 58.2 us  [scattered(): lax.psum_scatter(value.astype(BF16), 'dp', scatter_dimension=dimension, t...]
    unnamed x18 -> x9, waiting for transfers between devices: 38.3 us -> 1.49 us
    all_gather x8 -> x1, blocking collectives: 42.1 us -> 6.18 us  [local(): lax.all_gather(jnp.concatenate([item.reshape(-1) for item in small]), 'dp')]
  transfers between devices with their start and end apart: 32 -> 19, of which waited for: 27 -> 13; matrix products, arithmetic and copies ran while one was open for 21% -> 13% of each run, Pallas kernels for 0% -> 3%
where the time goes in v1:
time: 540 us; the launch traced here: 534 us
  waiting for transfers between devices  312 us (58%)
  blocking collectives  70.8 us (13%)
  matrix products  55.7 us (10%)
  starting transfers between devices  24.8 us (5%)
  other arithmetic  21.7 us (4%)
  local copies, waits for them, and re-layouts  20.8 us (4%)
  between operations  15.1 us (3%)
  Pallas kernels  13.5 us (2%)
    ppermute x6, waiting for transfers between devices, ahead(): lax.ppermute(value, axis, [(source, source + steps) for source in range(f...  122 us
    psum x1, blocking collectives, local(): lax.psum(jnp.concatenate([item.reshape(-1) for item in grads_small]), ('d...  64.6 us
    reduce_scatter x4, waiting for transfers between devices, scattered(): lax.psum_scatter(value.astype(BF16), 'dp', scatter_dimension=dimension, t...  58.2 us
    ppermute x4, waiting for transfers between devices, pair_sum(): other = lax.ppermute(low, 'tensor', [(0, 1), (1, 0)])  57.9 us
    psum x1, waiting for transfers between devices, local(): lax.psum(item, 'ctx').astype(F32)  50.9 us
    all_gather x1, waiting for transfers between devices, local(): lax.all_gather(jnp.swapaxes(qkv_weight, 0, 1), 'dp', axis=1, tiled=True)  21.4 us
    ppermute x6, starting transfers between devices, ahead(): lax.ppermute(value, axis, [(source, source + steps) for source in range(f...  18.2 us
    pallas_call x8, Pallas kernels, tile_call(): pl.pallas_call(kernel, grid=(heads,), in_specs=scalar_specs + [specs[kind...  13.5 us
  transfers between devices with their start and end apart: 19, of which 13 were waited for; matrix products, arithmetic and copies ran while one was open for 13% of the time, Pallas kernels for 3%

profile of v1, /device:TPU:0, one launch (start us, length us, event | category | flops | bytes accessed | tf_op | source)
XLA Modules:
  0.0 533.9 jit_solution(11379746581014279903)
XLA Ops:
  7.3 2.4 copy.48
  9.8 0.7 all-gather.9.cloned.1.call-update
  10.5 0.7 all-gather.11.cloned.1.call-update
  13.3 6.2 %all-gather.1 = bf16[4,1,2304]{2,1,0:T(2,128)(2,1)S(1)} all-gather(bf16[1,1,2304]{2,1,0:T(2,128)(2,1)S(1)} %reshape.247), channel_id=2, replica_groups=mesh['dp'=4,'ctx'=4,'tensor'=2] {'dp'}, dimensions={0}, use_global_device_ids=true | all-gather | bytes 23040 | tf_op jit(solution)/shard_map/all_gather | solution.py:179
  20.5 21.4 %all-gather.7.cloned.1.call-done = bf16[3,1024,512]{1,2,0:T(8,128)(2,1)} async-done(((bf16[3,256,512]{1,2,0:T(8,128)(2,1)}), bf16[3,1024,512]{1,2,0:T(8,128)(2,1)}) %all-gather.7.cloned.1.call-update) | async-done | bytes 3145744 | tf_op jit(solution)/shard_map/all_gather | solution.py:168
  41.9 3.9 convolution_bitcast_fusion
  46.2 4.4 collective-permute-start
  50.7 21.8 %collective-permute-done = bf16[1024,512]{1,0:T(8,128)(2,1)} collective-permute-done((bf16[1024,512]{1,0:T(8,128)(2,1)S(1)}, bf16[1024,512]{1,0:T(8,128)(2,1)}, u32[]{:S(2)}, u32[]{:S(2)}) %collective-permute-start) | collective-permute-done | bytes 1048608 | tf_op jit(solution)/shard_map/ppermute | solution.py:18
  72.4 4.5 collective-permute-start.1
  77.0 22.3 %collective-permute-done.1 = bf16[1024,512]{1,0:T(8,128)(2,1)S(1)} collective-permute-done((bf16[1024,512]{1,0:T(8,128)(2,1)}, bf16[1024,512]{1,0:T(8,128)(2,1)S(1)}, u32[]{:S(2)}, u32[]{:S(2)}) %collective-permute-start.1) | collective-permute-done | bytes 1048608 | tf_op jit(solution)/shard_map/ppermute | solution.py:18
  99.2 5.3 collective-permute-start.2
  104.5 4.6 shard_map.245
  109.1 1.3 fusion.69
  111.4 13.2 %collective-permute-done.2 = bf16[1024,512]{1,0:T(8,128)(2,1)} collective-permute-done((bf16[1024,512]{1,0:T(8,128)(2,1)S(1)}, bf16[1024,512]{1,0:T(8,128)(2,1)}, u32[]{:S(2)}, u32[]{:S(2)}) %collective-permute-start.2) | collective-permute-done | bytes 1048608 | tf_op jit(solution)/shard_map/ppermute | solution.py:18
  124.6 1.3 fusion.71
  126.7 0.8 copy-done.6
  127.5 0.9 fusion.53
  128.4 3.1 convolution_convert_fusion.3
  131.5 1.5 collective-permute-start.3
  133.2 21.2 %collective-permute-done.3 = bf16[512,1024]{1,0:T(8,128)(2,1)} collective-permute-done((bf16[512,1024]{1,0:T(8,128)(2,1)}, bf16[512,1024]{1,0:T(8,128)(2,1)}, u32[]{:S(2)}, u32[]{:S(2)}) %collective-permute-start.3) | collective-permute-done | bytes 1048608 | tf_op jit(solution)/shard_map/ppermute | solution.py:24
  154.5 2.4 fusion.67
  156.9 1.3 copy-done.12
  158.6 7.3 %fusion.66 = f32[512,2048]{1,0:T(8,128)} fusion(bf16[1024,2048]{1,0:T(8,128)(2,1)} %all-gather.11.cloned.1.call-done, f32[512,1024]{1,0:T(8,128)} %copy-done.12, f32[1024]{0:T(1024)S(1)} %bitcast.194, f32[1024]{0:T(1024)S(1)} %bitcast.178, f32[512]{0:T(512)S(1)} %add_rsqrt_fusion, f32[512]{0:T(512)S(1)} %broadcast_multiply_fusion.4), kind=kOutput, calls=%fused_computation.137 | convolution fusion | flops 2150105088 | bytes 10498048 | tf_op jit(solution)/shard_map/dot_general | solution.py:232
  165.9 8.7 %convert_reduce_fusion = (f32[2048]{0:T(1024)S(1)}, bf16[512,2048]{1,0:T(8,128)(2,1)S(1)}) fusion(f32[512,2048]{1,0:T(8,128)} %fusion.66, f32[2048]{0:T(1024)S(1)} %add.193, bf16[2048,1024]{1,0:T(8,128)(2,1)} %all-gather.13.cloned.1.call-done, bf16[1,512,1024]{2,1,0:T(8,128)(2,1)} %param.27), kind=kOutput, calls=%fused_computation.9 | convolution fusion | flops 2171598848 | bytes 11550720 | tf_op jit(solution)/shard_map/td,fd->tf/dot_general | solution.py:239
  174.6 2.4 convolution_convert_fusion.4
  177.0 1.6 collective-permute-start.5
  178.8 3.1 convolution_convert_fusion.5
  181.9 1.6 collective-permute-start.4
  183.4 19.7 %collective-permute-done.5 = bf16[512,1024]{1,0:T(8,128)(2,1)S(1)} collective-permute-done((bf16[512,1024]{1,0:T(8,128)(2,1)S(1)}, bf16[512,1024]{1,0:T(8,128)(2,1)S(1)}, u32[]{:S(2)}, u32[]{:S(2)}) %collective-permute-start.5) | collective-permute-done | bytes 1048608 | tf_op jit(solution)/shard_map/ppermute | solution.py:24
  203.2 1.1 multiply_reduce_fusion
  204.3 17.0 %collective-permute-done.4 = bf16[512,1024]{1,0:T(8,128)(2,1)S(1)} collective-permute-done((bf16[512,1024]{1,0:T(8,128)(2,1)S(1)}, bf16[512,1024]{1,0:T(8,128)(2,1)S(1)}, u32[]{:S(2)}, u32[]{:S(2)}) %collective-permute-start.4) | collective-permute-done | bytes 1048608 | tf_op jit(solution)/shard_map/ppermute | solution.py:24
  221.2 2.4 convert_reduce_fusion.4
  223.7 1.3 copy-done.10
  225.0 1.7 convolution_convert_fusion.2
  226.7 7.7 %convolution_convert_fusion = bf16[2048,1024]{1,0:T(8,128)(2,1)} fusion(bf16[1,512,1024]{2,1,0:T(8,128)(2,1)} %param.27, f32[512,2048]{1,0:T(8,128)} %fusion.66, f32[2048]{0:T(1024)S(1)} %add.193), kind=kOutput, calls=%fused_computation.11 | convolution fusion | flops 2160066560 | bytes 9445376 | tf_op jit(solution)/shard_map/tf,td->fd/dot_general | solution.py:253
  234.6 6.8 %convolution_convert_fusion.1 = bf16[1024,2048]{1,0:T(8,128)(2,1)} fusion(bf16[512,2048]{1,0:T(8,128)(2,1)} %copy-done.31, f32[512,1024]{1,0:T(8,128)} %copy-done.12, f32[1024]{0:T(1024)S(1)} %bitcast.195, f32[1024]{0:T(1024)S(1)} %bitcast.181, f32[512]{0:T(512)S(1)} %add_rsqrt_fusion, f32[512]{0:T(512)S(1)} %broadcast_multiply_fusion.4), kind=kOutput, calls=%fused_computation.12 | convolution fusion | flops 2152202240 | bytes 8400896 | tf_op jit(solution)/shard_map/td,tf->df/dot_general | solution.py:257
  241.4 2.7 fusion.47
  244.8 1.4 collective-permute-start.6
  246.7 21.9 %collective-permute-done.6 = bf16[1024,512]{1,0:T(8,128)(2,1)S(1)} collective-permute-done((bf16[1024,512]{1,0:T(8,128)(2,1)S(1)}, bf16[1024,512]{1,0:T(8,128)(2,1)S(1)}, u32[]{:S(2)}, u32[]{:S(2)}) %collective-permute-start.6) | collective-permute-done | bytes 1048608 | tf_op jit(solution)/shard_map/ppermute | solution.py:18
  269.0 1.3 collective-permute-start.7
  270.3 0.6 shard_map.251
  271.0 20.1 %collective-permute-done.7 = bf16[1024,512]{1,0:T(8,128)(2,1)S(1)} collective-permute-done((bf16[1024,512]{1,0:T(8,128)(2,1)S(1)}, bf16[1024,512]{1,0:T(8,128)(2,1)S(1)}, u32[]{:S(2)}, u32[]{:S(2)}) %collective-permute-start.7) | collective-permute-done | bytes 1048608 | tf_op jit(solution)/shard_map/ppermute | solution.py:18
  291.5 1.3 collective-permute-start.8
  292.8 6.6 %shard_map.252 = (f32[512,512]{1,0:T(8,128)S(1)}, f32[512,512]{1,0:T(8,128)S(1)}, f32[512,512]{1,0:T(8,128)S(1)}) custom-call(s32[1]{0:T(128)} %bitcast.1.refs_0_, bf16[512,512]{1,0:T(8,128)(2,1)S(1)} %get-tuple-element.135.q_ref.refs_1_, bf16[512,512]{1,0:T(8,128)(2,1)S(1)} %fusion.63.k_ref.refs_2_, bf16[512,512]{1,0:T(8,128)(2,1)S(1)} %get-tuple-element.134.v_ref.refs_3_, ...), custom_call_target="tpu_custom_call" | custom-call | flops 1342177280 | bytes 6291456 | tf_op jit(solution)/shard_map/pallas_call | solution.py:128
  300.0 22.4 %collective-permute-done.8 = bf16[1024,512]{1,0:T(8,128)(2,1)S(1)} collective-permute-done((bf16[1024,512]{1,0:T(8,128)(2,1)S(1)}, bf16[1024,512]{1,0:T(8,128)(2,1)S(1)}, u32[]{:S(2)}, u32[]{:S(2)}) %collective-permute-start.8) | collective-permute-done | bytes 1048608 | tf_op jit(solution)/shard_map/ppermute | solution.py:18
  323.0 1.1 copy-done.15
  324.1 3.7 convert_bitcast_fusion
  327.8 4.7 bitcast_convert_fusion
  332.5 1.6 collective-permute-start.9
  334.4 17.5 %reduce-scatter.9.cloned.1.call-done = bf16[256,2048]{1,0:T(8,128)(2,1)} async-done(((bf16[1024,2048]{1,0:T(8,128)(2,1)}), bf16[256,2048]{1,0:T(8,128)(2,1)}) %reduce-scatter.9.cloned.1.call-update) | async-done | bytes 1048592 | tf_op jit(solution)/shard_map/reduce_scatter | solution.py:248
  351.9 40.7 %reduce-scatter.5.cloned.1.call-done = bf16[3,256,512]{1,2,0:T(8,128)(2,1)} async-done(((bf16[3,1024,512]{1,2,0:T(8,128)(2,1)}), bf16[3,256,512]{1,2,0:T(8,128)(2,1)}) %reduce-scatter.5.cloned.1.call-update) | async-done | bytes 786448 | tf_op jit(solution)/shard_map/reduce_scatter | solution.py:248
  392.6 2.8 fusion.22
  395.5 64.6 %psum.36 = f32[9216]{0:T(1024)S(1)} all-reduce(f32[9216]{0:T(1024)S(1)} %constant_dynamic-update-slice_fusion), channel_id=1, replica_groups=mesh['dp'=4,'ctx'=4,'tensor'=2] {'dp','ctx'}, use_global_device_ids=true, to_apply=%region_19.0 | all-reduce | flops 9216 | bytes 73728 | tf_op jit(solution)/shard_map/psum | solution.py:326
  460.4 0.7 copy.53
  461.1 0.6 constant_dynamic-slice_fusion
  462.2 0.6 constant_dynamic-slice_fusion.2
  462.8 0.6 constant_dynamic-slice_fusion.3
  464.5 0.6 constant_dynamic-slice_fusion.7
  465.1 3.5 fusion.62
  468.6 50.9 %all-reduce.3.cloned.1.call-done = (bf16[256,3,512]{0,2,1:T(8,128)(2,1)}, bf16[512,256]{1,0:T(8,128)(2,1)}, bf16[256,2048]{1,0:T(8,128)(2,1)}, bf16[2048,256]{1,0:T(8,128)(2,1)}) async-done(((bf16[256,3,512]{0,2,1:T(8,128)(2,1)}, bf16[512,256]{1,0:T(8,128)(2,1)}, bf16[256,2048]{1,0:T(8,128)(2,1)}, bf16[2048,256]{1,0:T(8,128)(2,1)}), (bf16[256,3,512]{0,2,1:T(8,128)(2,1)}, bf16[512,256]{1,0:T(8,128)(2,1)}, ...) | async-done | bytes 3145744 | tf_op jit(solution)/shard_map/psum | solution.py:312
  519.5 1.9 convert_element_type.193
  521.4 2.6 copy.54
  523.9 1.6 convert_element_type.195
  525.5 1.5 convert_element_type.197
  (166 shorter events, 11.7 us)
Async XLA Ops:
  7.2 4.1 copy-start.21
  7.2 4.2 copy-start.20
  7.2 4.3 copy-start.22
  7.2 4.6 copy-start.23
  7.2 4.8 copy-start.24
  7.2 5.0 copy-start.25
  7.2 5.2 copy-start.26
  7.3 5.4 %copy-start.27 = (bf16[256]{0:T(256)(128)(2,1)S(1)}, bf16[256]{0:T(256)(128)(2,1)}, u32[]{:S(2)}) copy-start(bf16[256]{0:T(256)(128)(2,1)} %param.22) | copy-start | bytes 1540
  7.3 12.6 %copy-start.14 = (bf16[1,512,1024]{2,1,0:T(8,128)(2,1)S(1)}, bf16[1,512,1024]{2,1,0:T(8,128)(2,1)}, u32[]{:S(2)}) copy-start(bf16[1,512,1024]{2,1,0:T(8,128)(2,1)} %param.14) | copy-start | bytes 3145732
  7.3 34.6 %all-gather.7.cloned.1.call-start = ((), (), s32[]{:S(2)}) async-start(), calls=%async_computation.4 | async-start | bytes 3932160 | tf_op jit(solution)/shard_map/all_gather | solution.py:168
  9.7 118.7 %all-gather.9.cloned.1.call-start = ((), (), s32[]{:S(2)}) async-start(), calls=%async_computation.5 | async-start | bytes 1310720 | tf_op jit(solution)/shard_map/all_gather | solution.py:188
  10.5 148.1 %all-gather.11.cloned.1.call-start = ((), (), s32[]{:S(2)}) async-start(), calls=%async_computation.6 | async-start | bytes 5242880 | tf_op jit(solution)/shard_map/all_gather | solution.py:189
  11.2 154.6 %all-gather.13.cloned.1.call-start = ((), (), s32[]{:S(2)}) async-start(), calls=%async_computation.7 | async-start | bytes 5242880 | tf_op jit(solution)/shard_map/all_gather | solution.py:190
  46.2 26.2 %collective-permute-start = (bf16[1024,512]{1,0:T(8,128)(2,1)S(1)}, bf16[1024,512]{1,0:T(8,128)(2,1)}, u32[]{:S(2)}, u32[]{:S(2)}) collective-permute-start(bf16[1024,512]{1,0:T(8,128)(2,1)S(1)} %pad_maximum_fusion.1), channel_id=1, source_target_pairs={{0,2},{2,4},{4,6},{1,3},{3,5},{5,7},{8,10},{10,12},{12,14},{9,11},... | collective-permute-start | bytes 3145736 | tf_op jit(solution)/shard_map/ppermute | solution.py:18
  50.6 283.7 %reduce-scatter.7.cloned.1.call-start = ((), (), s32[]{:S(2)}) async-start(), calls=%async_computation.9 | async-start | bytes 1310720 | tf_op jit(solution)/shard_map/reduce_scatter | solution.py:248
  72.4 26.8 %collective-permute-start.1 = (bf16[1024,512]{1,0:T(8,128)(2,1)}, bf16[1024,512]{1,0:T(8,128)(2,1)S(1)}, u32[]{:S(2)}, u32[]{:S(2)}) collective-permute-start(bf16[1024,512]{1,0:T(8,128)(2,1)} %collective-permute-done), channel_id=1, source_target_pairs={{0,2},{2,4},{4,6},{1,3},{3,5},{5,7},{8,10},{10,12},{12,14},{9,11},... | collective-permute-start | bytes 3145736 | tf_op jit(solution)/shard_map/ppermute | solution.py:18
  99.2 25.4 %collective-permute-start.2 = (bf16[1024,512]{1,0:T(8,128)(2,1)S(1)}, bf16[1024,512]{1,0:T(8,128)(2,1)}, u32[]{:S(2)}, u32[]{:S(2)}) collective-permute-start(bf16[1024,512]{1,0:T(8,128)(2,1)S(1)} %collective-permute-done.1), channel_id=1, source_target_pairs={{0,2},{2,4},{4,6},{1,3},{3,5},{5,7},{8,10},{10,12},{12,14},{9,11},... | collective-permute-start | bytes 3145736 | tf_op jit(solution)/shard_map/ppermute | solution.py:18
  110.4 0.8 copy-start
  111.2 14.7 %copy-start.2 = (bf16[512,512]{1,0:T(8,128)(2,1)}, bf16[512,512]{1,0:T(8,128)(2,1)S(1)}, u32[]{:S(2)}) copy-start(bf16[512,512]{1,0:T(8,128)(2,1)S(1)} %get-tuple-element.140.refs_3_) | copy-start | bytes 1572868
  111.2 14.7 %copy-start.4 = (bf16[512,512]{1,0:T(8,128)(2,1)}, bf16[512,512]{1,0:T(8,128)(2,1)S(1)}, u32[]{:S(2)}) copy-start(bf16[512,512]{1,0:T(8,128)(2,1)S(1)} %get-tuple-element.141.refs_2_) | copy-start | bytes 1572868
  125.9 0.8 copy-start.8
  126.7 0.8 copy-start.6
  131.5 23.0 %collective-permute-start.3 = (bf16[512,1024]{1,0:T(8,128)(2,1)}, bf16[512,1024]{1,0:T(8,128)(2,1)}, u32[]{:S(2)}, u32[]{:S(2)}) collective-permute-start(bf16[512,1024]{1,0:T(8,128)(2,1)} %convolution_convert_fusion.3), channel_id=1, source_target_pairs={{0,1},{1,0},{2,3},{3,2},{4,5},{5,4},{6,7},{7,6},{8,9},{9,8},{10,11... | collective-permute-start | bytes 3145736 | tf_op jit(solution)/shard_map/ppermute | solution.py:24
  156.9 1.3 copy-start.12
  165.9 8.7 %copy-start.28 = (bf16[1024,2048]{1,0:T(8,128)(2,1)S(1)}, bf16[1024,2048]{1,0:T(8,128)(2,1)}, u32[]{:S(2)}) copy-start(bf16[1024,2048]{1,0:T(8,128)(2,1)} %all-gather.11.cloned.1.call-done) | copy-start | bytes 12582916
  174.5 2.4 copy-start.31
  174.6 4.0 copy-start.29
  174.6 4.2 copy-start.30
  177.0 26.2 %copy-start.13 = (f32[512,1024]{1,0:T(8,128)S(1)}, f32[512,1024]{1,0:T(8,128)}, u32[]{:S(2)}) copy-start(f32[512,1024]{1,0:T(8,128)} %copy-done.12) | copy-start | bytes 6291460
  177.0 26.2 %collective-permute-start.5 = (bf16[512,1024]{1,0:T(8,128)(2,1)S(1)}, bf16[512,1024]{1,0:T(8,128)(2,1)S(1)}, u32[]{:S(2)}, u32[]{:S(2)}) collective-permute-start(bf16[512,1024]{1,0:T(8,128)(2,1)S(1)} %convolution_convert_fusion.4), channel_id=1, source_target_pairs={{0,1},{1,0},{2,3},{3,2},{4,5},{5,4},{6,7},{7,6},{8,9},{9,8},{10,11... | collective-permute-start | bytes 3145736 | tf_op jit(solution)/shard_map/ppermute | solution.py:24
  181.9 39.4 %collective-permute-start.4 = (bf16[512,1024]{1,0:T(8,128)(2,1)S(1)}, bf16[512,1024]{1,0:T(8,128)(2,1)S(1)}, u32[]{:S(2)}, u32[]{:S(2)}) collective-permute-start(bf16[512,1024]{1,0:T(8,128)(2,1)S(1)} %convolution_convert_fusion.5), channel_id=1, source_target_pairs={{0,1},{1,0},{2,3},{3,2},{4,5},{5,4},{6,7},{7,6},{8,9},{9,8},{10,11... | collective-permute-start | bytes 3145736 | tf_op jit(solution)/shard_map/ppermute | solution.py:24
  183.4 37.8 %copy-start.17 = (bf16[1,512,1024]{2,1,0:T(8,128)(2,1)S(1)}, bf16[1,512,1024]{2,1,0:T(8,128)(2,1)}, u32[]{:S(2)}) copy-start(bf16[1,512,1024]{2,1,0:T(8,128)(2,1)} %param.27) | copy-start | bytes 3145732
  221.2 3.8 copy-start.16
  223.7 1.3 copy-start.10
  226.7 107.7 %reduce-scatter.11.cloned.1.call-start = ((), (), s32[]{:S(2)}) async-start(), calls=%async_computation.11 | async-start | bytes 5242880 | tf_op jit(solution)/shard_map/reduce_scatter | solution.py:248
  234.5 117.4 %reduce-scatter.9.cloned.1.call-start = ((), (), s32[]{:S(2)}) async-start(), calls=%async_computation.10 | async-start | bytes 5242880 | tf_op jit(solution)/shard_map/reduce_scatter | solution.py:248
  241.4 151.2 %reduce-scatter.5.cloned.1.call-start = ((), (), s32[]{:S(2)}) async-start(), calls=%async_computation.8 | async-start | bytes 3932160 | tf_op jit(solution)/shard_map/reduce_scatter | solution.py:248
  241.4 2.8 copy-start.7
  241.4 2.8 copy-start.9
  244.7 1.6 copy-start.3
  244.7 1.6 copy-start.5
  244.8 23.7 %collective-permute-start.6 = (bf16[1024,512]{1,0:T(8,128)(2,1)S(1)}, bf16[1024,512]{1,0:T(8,128)(2,1)S(1)}, u32[]{:S(2)}, u32[]{:S(2)}) collective-permute-start(bf16[1024,512]{1,0:T(8,128)(2,1)S(1)} %pad_maximum_fusion.2), channel_id=1, source_target_pairs={{2,0},{4,2},{6,4},{3,1},{5,3},{7,5},{10,8},{12,10},{14,12},{11,9},... | collective-permute-start | bytes 3145736 | tf_op jit(solution)/shard_map/ppermute | solution.py:18
  268.6 1.7 copy-start.1
  269.0 22.1 %collective-permute-start.7 = (bf16[1024,512]{1,0:T(8,128)(2,1)S(1)}, bf16[1024,512]{1,0:T(8,128)(2,1)S(1)}, u32[]{:S(2)}, u32[]{:S(2)}) collective-permute-start(bf16[1024,512]{1,0:T(8,128)(2,1)S(1)} %fusion.31), channel_id=1, source_target_pairs={{2,0},{4,2},{6,4},{3,1},{5,3},{7,5},{10,8},{12,10},{14,12},{11,9},... | collective-permute-start | bytes 3145736 | tf_op jit(solution)/shard_map/ppermute | solution.py:18
  291.5 30.9 %collective-permute-start.8 = (bf16[1024,512]{1,0:T(8,128)(2,1)S(1)}, bf16[1024,512]{1,0:T(8,128)(2,1)S(1)}, u32[]{:S(2)}, u32[]{:S(2)}) collective-permute-start(bf16[1024,512]{1,0:T(8,128)(2,1)S(1)} %fusion.30), channel_id=1, source_target_pairs={{2,0},{4,2},{6,4},{3,1},{5,3},{7,5},{10,8},{12,10},{14,12},{11,9},... | collective-permute-start | bytes 3145736 | tf_op jit(solution)/shard_map/ppermute | solution.py:18
  322.8 1.2 copy-start.15
  327.8 191.8 %all-reduce.3.cloned.1.call-start = ((), (), s32[]{:S(2)}) async-start(), calls=%async_computation.12 | async-start | bytes 6291456 | tf_op jit(solution)/shard_map/psum | solution.py:312
  332.5 60.1 %collective-permute-start.9 = (bf16[512,1024]{1,0:T(8,128)(2,1)}, bf16[512,1024]{1,0:T(8,128)(2,1)}, u32[]{:S(2)}, u32[]{:S(2)}) collective-permute-start(bf16[512,1024]{1,0:T(8,128)(2,1)} %bitcast_convert_fusion), channel_id=1, source_target_pairs={{0,1},{1,0},{2,3},{3,2},{4,5},{5,4},{6,7},{7,6},{8,9},{9,8},{10,11... | collective-permute-start | bytes 3145736 | tf_op jit(solution)/shard_map/ppermute | solution.py:24
  392.6 72.5 %copy-start.11 = (f32[512,1024]{1,0:T(8,128)S(1)}, f32[512,1024]{1,0:T(8,128)}, u32[]{:S(2)}) copy-start(f32[512,1024]{1,0:T(8,128)} %copy-done.10) | copy-start | bytes 6291460
  519.5 4.4 copy-start.19
  523.9 1.6 copy-start.18
Sparse Core Ops, SparseCore 0:
  10.2 31.6 all-gather.6
  43.4 16.8 all-gather.8
  61.9 34.4 all-gather.10
  97.8 35.0 all-gather.12
  226.8 30.8 reduce-scatter.6
  260.2 44.4 reduce-scatter.10
  307.3 44.5 reduce-scatter.8
  354.6 37.9 reduce-scatter.4
  395.2 124.2 all-reduce.2

commit v2 on v1

--- a/solution.py
+++ b/solution.py
@@ -24,6 +24,64 @@
         other = lax.ppermute(low, "tensor", [(0, 1), (1, 0)])
         return low.astype(F32) + other.astype(F32)
     return lax.psum(low, "tensor").astype(F32)
+
+
+def flipped(value, axis, bit):
+    count = lax.axis_size(axis)
+    return lax.ppermute(value, axis, [(source, source ^ bit) for source in range(count)])
+
+
+def gather_shards(shard):
+    mine = lax.axis_index("dp")
+    beside = flipped(shard, "dp", 1)
+    across = flipped(shard, "dp", 2)
+    corner = flipped(across, "dp", 1)
+    whole = jnp.zeros((4,) + shard.shape, shard.dtype)
+    for bit, item in enumerate((shard, beside, across, corner)):
+        whole = lax.dynamic_update_index_in_dim(whole, item, mine ^ bit, 0)
+    return whole
+
+
+def shard_columns(rows, core, high):
+    size = rows.shape[1] // 4
+    return lax.dynamic_slice_in_dim(rows, (2 * high + core) * size, size, 1)
+
+
+def scatter_product(rows, product):
+    mine = lax.axis_index("dp")
+    core, high = mine % 2, mine // 2
+    sent = [product(shard_columns(rows, 1 - core, bit)).astype(BF16) for bit in (1 - high, high)]
+    sent = [flipped(item, "dp", 1) for item in sent]
+    kept = [product(shard_columns(rows, core, bit)) for bit in (1 - high, high)]
+    away, home = [own + other.astype(F32) for own, other in zip(kept, sent)]
+    return home + flipped(away.astype(BF16), "dp", 2).astype(F32)
+
+
+def ctx_total(value):
+    count = lax.axis_size("ctx")
+    mine = lax.axis_index("ctx")
+    chunks = value.astype(BF16).reshape((count, -1) + value.shape[1:])
+    total = lax.dynamic_index_in_dim(chunks, mine, 0, False).astype(F32)
+    for step in range(1, count):
+        chunk = lax.dynamic_index_in_dim(chunks, (mine + step) % count, 0, False)
+        pairs = [(source, (source + step) % count) for source in range(count)]
+        total = total + lax.ppermute(chunk, "ctx", pairs).astype(F32)
+    total = total.astype(BF16)
+    whole = lax.dynamic_update_index_in_dim(jnp.zeros_like(chunks), total, mine, 0)
+    for step in range(1, count):
+        pairs = [(source, (source + step) % count) for source in range(count)]
+        other = lax.ppermute(total, "ctx", pairs)
+        whole = lax.dynamic_update_index_in_dim(whole, other, (mine + count - step) % count, 0)
+    return whole.reshape(value.shape).astype(F32)
+
+
+def small_total(value):
+    for axis in ("dp", "ctx"):
+        bit = 1
+        while bit < lax.axis_size(axis):
+            value = value + flipped(value, axis, bit)
+            bit *= 2
+    return value
 
 
 def norm_parts(values):
@@ -165,7 +223,9 @@
     dp_place = lax.axis_index("dp")
     place = lax.axis_index("ctx").astype(jnp.int32).reshape(1)
 
-    attn_in = lax.all_gather(jnp.swapaxes(qkv_weight, 0, 1), "dp", axis=1, tiled=True)
+    kv_in = gather_shards(jnp.swapaxes(qkv_weight[:, 1:], 0, 1))
+    kv_in = jnp.swapaxes(kv_in, 0, 1).reshape(2, width, -1)
+    q_in = lax.all_gather(qkv_weight[:, 0], "dp", axis=0, tiled=True)
     small = (
         first_gain,
         first_shift,
@@ -189,17 +249,18 @@
     mlp_up = lax.all_gather(up_weight, "dp", axis=0, tiled=True)
     mlp_down = lax.all_gather(down_weight, "dp", axis=1, tiled=True)
 
-    half_width = attn_in.shape[2]
+    half_width = q_in.shape[1]
     heads = half_width // HEAD_DIM
     xhat_one, scale_one = norm_parts(rows)
     normed_low = (xhat_one * gain_one + shift_one).astype(BF16)
     bias_in = bias_in.reshape(2, half_width, 1)
-    mixed = jnp.einsum("td,cdh->cht", normed_low, attn_in, preferred_element_type=F32)
-    query = (mixed[0] + bias_in[0]).astype(BF16)
-    keys = mixed[1].astype(BF16)
-    values = (mixed[2] + bias_in[1]).astype(BF16)
+    mixed = jnp.einsum("td,cdh->cht", normed_low, kv_in, preferred_element_type=F32)
+    keys = mixed[0].astype(BF16)
+    values = (mixed[1] + bias_in[1]).astype(BF16)
 
     blocks = [jnp.concatenate([keys, values], axis=0)]
+    query = jnp.einsum("td,dh->ht", normed_low, q_in, preferred_element_type=F32)
+    query = (query + bias_in[0]).astype(BF16)
     for distance in range(1, ctx_size):
         blocks.append(ahead(blocks[-1], "ctx", 1))
     peak, total, accum = tile_call(
@@ -241,20 +302,18 @@
     grad_normed_two = pair_sum(
         jnp.einsum("tf,df->td", grad_pre, mlp_up, preferred_element_type=F32)
     )
-    mlp_part = pair_sum(jnp.dot(hidden_act, mlp_down, preferred_element_type=F32))
+    later_act, grad_normed_two = lax.optimization_barrier((hidden_act, grad_normed_two))
+    mlp_part = pair_sum(jnp.dot(later_act, mlp_down, preferred_element_type=F32))
     output = (resid + mlp_part + bias_down).astype(BF16).reshape(shape)
 
-    def scattered(value, dimension):
-        return lax.psum_scatter(
-            value.astype(BF16), "dp", scatter_dimension=dimension, tiled=True
-        )
-
-    grad_down = scattered(
-        jnp.einsum("tf,td->fd", hidden_act, grad_rows, preferred_element_type=F32), 1
+    grad_down = scatter_product(
+        grad_rows,
+        lambda part: jnp.einsum("tf,td->fd", hidden_act, part, preferred_element_type=F32),
     )
     grad_bias_up = jnp.sum(grad_pre, axis=0, dtype=F32)
-    grad_up = scattered(
-        jnp.einsum("td,tf->df", normed_two_low, grad_pre, preferred_element_type=F32), 0
+    grad_up = scatter_product(
+        normed_two_low,
+        lambda part: jnp.einsum("td,tf->df", part, grad_pre, preferred_element_type=F32),
     )
 
     grad_gain_two = jnp.sum(grad_normed_two * xhat_two, axis=0)
@@ -267,8 +326,9 @@
     ).astype(BF16)
     grad_heads = grad_attended.astype(F32).reshape(heads, HEAD_DIM, count)
     delta = jnp.sum(grad_heads * attn_heads, axis=1, keepdims=True)
-    grad_out = scattered(
-        jnp.einsum("ht,td->hd", attended_low, grad_branch, preferred_element_type=F32), 1
+    grad_out = scatter_product(
+        grad_branch,
+        lambda part: jnp.einsum("ht,td->hd", attended_low, part, preferred_element_type=F32),
     )
 
     grad_query = 0.0
@@ -297,21 +357,24 @@
     grad_mixed = grad_mixed.reshape(3, half_width, count)
     grad_bias_in = jnp.sum(grad_mixed[0::2], axis=2, dtype=F32)
     grad_normed_one = pair_sum(
-        jnp.einsum("cht,cdh->td", grad_mixed, attn_in, preferred_element_type=F32)
-    )
-    grad_attn_in = scattered(
-        jnp.einsum("td,cht->cdh", normed_low, grad_mixed, preferred_element_type=F32), 1
+        jnp.einsum("ht,dh->td", grad_mixed[0], q_in, preferred_element_type=F32)
+        + jnp.einsum("cht,cdh->td", grad_mixed[1:], kv_in, preferred_element_type=F32)
+    )
+    grad_attn_in = scatter_product(
+        normed_low,
+        lambda part: jnp.einsum(
+            "td,rt->dr", part, grad_mixed.reshape(-1, count), preferred_element_type=F32
+        ),
     )
     grad_gain_one = jnp.sum(grad_normed_one * xhat_one, axis=0)
     grad_shift_one = jnp.sum(grad_normed_one, axis=0)
     grad_inputs = grad_resid + norm_back(grad_normed_one, xhat_one, scale_one, gain_one)
     grad_inputs = grad_inputs.astype(BF16).reshape(shape)
 
-    grad_up, grad_down = [lax.psum(item, "ctx").astype(F32) for item in (grad_up, grad_down)]
-    grad_out, grad_attn_in = [
-        lax.psum(item, "ctx").astype(F32) for item in (grad_out, grad_attn_in)
+    grad_up, grad_down, grad_out = [
+        lax.psum(item.astype(BF16), "ctx").astype(F32) for item in (grad_up, grad_down, grad_out)
     ]
-    grad_attn_in = jnp.swapaxes(grad_attn_in, 0, 1)
+    grad_attn_in = ctx_total(grad_attn_in).reshape(-1, 3, half_width)
 
     grads_small = (
         grad_gain_one,
@@ -323,7 +386,7 @@
         grad_bias_in,
         grad_bias_up,
     )
-    summed = lax.psum(jnp.concatenate([item.reshape(-1) for item in grads_small]), ("dp", "ctx"))
+    summed = small_total(jnp.concatenate([item.reshape(-1) for item in grads_small]))
     small_out = []
     start = 0
     for item in small:

time: 540 us -> 490 us (0.907)
  blocking collectives: 70.8 us -> 15.6 us
  waiting for transfers between devices: 312 us -> 271 us
  starting transfers between devices: 24.8 us -> 49.6 us
  other arithmetic: 21.7 us -> 32.5 us
  local copies, waits for them, and re-layouts: 20.8 us -> 27.6 us
    psum x1 -> x0, blocking collectives: 64.6 us -> none  [local(): lax.psum(jnp.concatenate([item.reshape(-1) for item in grads_small]), ('d...]
    reduce_scatter x4 -> x0, waiting for transfers between devices: 58.2 us -> none  [scattered(): lax.psum_scatter(value.astype(BF16), 'dp', scatter_dimension=dimension, t...]
    ppermute x0 -> x25, waiting for transfers between devices: none -> 35.1 us  [the longest x19 14.6 us: flipped(): lax.ppermute(value, axis, [(source, source ^ bit) for source in range(cou...]
    ppermute x6, waiting for transfers between devices: 122 us -> 148 us  [ahead(): lax.ppermute(value, axis, [(source, source + steps) for source in range(f...]
    ppermute x0 -> x25, starting transfers between devices: none -> 25.2 us  [the longest x19 14.6 us: flipped(): lax.ppermute(value, axis, [(source, source ^ bit) for source in range(cou...]
    all_gather x1, waiting for transfers between devices: 21.4 us -> 0.01 us  [local(): q_in = lax.all_gather(qkv_weight[:, 0], 'dp', axis=0, tiled=True)]
    ppermute x4, waiting for transfers between devices: 57.9 us -> 40.2 us  [pair_sum(): other = lax.ppermute(low, 'tensor', [(0, 1), (1, 0)])]
    all_gather x1, blocking collectives: 6.18 us -> 15.6 us  [local(): lax.all_gather(jnp.concatenate([item.reshape(-1) for item in small]), 'dp')]
  transfers between devices with their start and end apart: 19 -> 40, of which waited for: 13 -> 19; matrix products, arithmetic and copies ran while one was open for 13% -> 19% of each run, Pallas kernels for 3% -> 3%
where the time goes in v2:
time: 490 us; the launch traced here: 481 us
  waiting for transfers between devices  271 us (55%)
  matrix products  55.2 us (11%)
  starting transfers between devices  49.6 us (10%)
  other arithmetic  32.5 us (7%)
  local copies, waits for them, and re-layouts  27.6 us (6%)
  blocking collectives  15.6 us (3%)
  between operations  15.4 us (3%)
  Pallas kernels  13.6 us (3%)
    ppermute x6, waiting for transfers between devices, ahead(): lax.ppermute(value, axis, [(source, source + steps) for source in range(f...  148 us
    psum x1, waiting for transfers between devices, local(): lax.psum(item.astype(BF16), 'ctx').astype(F32)  46.5 us
    ppermute x4, waiting for transfers between devices, pair_sum(): other = lax.ppermute(low, 'tensor', [(0, 1), (1, 0)])  40.2 us
    ppermute x6, starting transfers between devices, ahead(): lax.ppermute(value, axis, [(source, source + steps) for source in range(f...  19.3 us
    all_gather x1, blocking collectives, local(): lax.all_gather(jnp.concatenate([item.reshape(-1) for item in small]), 'dp')  15.6 us
    ppermute x19, starting transfers between devices, flipped(): lax.ppermute(value, axis, [(source, source ^ bit) for source in range(cou...  14.6 us
    ppermute x19, waiting for transfers between devices, flipped(): lax.ppermute(value, axis, [(source, source ^ bit) for source in range(cou...  14.6 us
    dot_general x4, matrix products, local(): jnp.einsum('tf,td->fd', hidden_act, part, preferred_element_type=F32)  13.9 us
  transfers between devices with their start and end apart: 40, of which 19 were waited for; matrix products, arithmetic and copies ran while one was open for 19% of the time, Pallas kernels for 3%

profile of v2, /device:TPU:0, one launch (start us, length us, event | category | flops | bytes accessed | tf_op | source)
XLA Modules:
  0.0 480.8 jit_solution(15724319567743497149)
XLA Ops:
  7.3 1.8 slice.178
  11.2 2.6 collective-permute-start.1
  15.9 15.6 %all-gather.2 = bf16[4,1,2304]{2,1,0:T(2,128)(2,1)S(1)} all-gather(bf16[1,1,2304]{2,1,0:T(2,128)(2,1)S(1)} %reshape.266), channel_id=2, replica_groups=mesh['dp'=4,'ctx'=4,'tensor'=2] {'dp'}, dimensions={0}, use_global_device_ids=true | all-gather | bytes 23040 | tf_op jit(solution)/shard_map/all_gather | solution.py:239
  32.2 1.5 broadcast_in_dim.43
  35.0 1.9 bitcast_dynamic-update-slice_fusion.3
  37.7 1.8 copy.55
  39.5 1.5 fusion.40
  42.3 4.3 collective-permute-start.3
  46.7 22.9 %collective-permute-done.3 = bf16[1024,512]{1,0:T(8,128)(2,1)S(1)} collective-permute-done((bf16[1024,512]{1,0:T(8,128)(2,1)}, bf16[1024,512]{1,0:T(8,128)(2,1)S(1)}, u32[]{:S(2)}, u32[]{:S(2)}) %collective-permute-start.3) | collective-permute-done | bytes 1048608 | tf_op jit(solution)/shard_map/ppermute | solution.py:18
  69.6 5.2 %collective-permute-start.4 = (bf16[1024,512]{1,0:T(8,128)(2,1)S(1)}, bf16[1024,512]{1,0:T(8,128)(2,1)}, u32[]{:S(2)}, u32[]{:S(2)}) collective-permute-start(bf16[1024,512]{1,0:T(8,128)(2,1)S(1)} %collective-permute-done.3), channel_id=1, source_target_pairs={{0,2},{2,4},{4,6},{1,3},{3,5},{5,7},{8,10},{10,12},{12,14},{9,11},... | collective-permute-start | bytes 3145736 | tf_op jit(solution)/shard_map/ppermute | solution.py:18
  74.9 21.1 %collective-permute-done.4 = bf16[1024,512]{1,0:T(8,128)(2,1)} collective-permute-done((bf16[1024,512]{1,0:T(8,128)(2,1)S(1)}, bf16[1024,512]{1,0:T(8,128)(2,1)}, u32[]{:S(2)}, u32[]{:S(2)}) %collective-permute-start.4) | collective-permute-done | bytes 1048608 | tf_op jit(solution)/shard_map/ppermute | solution.py:18
  95.9 5.5 %collective-permute-start.5 = (bf16[1024,512]{1,0:T(8,128)(2,1)}, bf16[1024,512]{1,0:T(8,128)(2,1)}, u32[]{:S(2)}, u32[]{:S(2)}) collective-permute-start(bf16[1024,512]{1,0:T(8,128)(2,1)} %collective-permute-done.4), channel_id=1, source_target_pairs={{0,2},{2,4},{4,6},{1,3},{3,5},{5,7},{8,10},{10,12},{12,14},{9,11},... | collective-permute-start | bytes 3145736 | tf_op jit(solution)/shard_map/ppermute | solution.py:18
  102.0 2.3 fusion.37.q_ref.refs_1_
  104.3 4.6 shard_map.245
  110.9 10.9 %collective-permute-done.5 = bf16[1024,512]{1,0:T(8,128)(2,1)} collective-permute-done((bf16[1024,512]{1,0:T(8,128)(2,1)}, bf16[1024,512]{1,0:T(8,128)(2,1)}, u32[]{:S(2)}, u32[]{:S(2)}) %collective-permute-start.5) | collective-permute-done | bytes 1048608 | tf_op jit(solution)/shard_map/ppermute | solution.py:18
  124.6 3.2 convolution_convert_fusion.6
  127.8 1.6 collective-permute-start.6
  129.7 21.0 %collective-permute-done.6 = bf16[512,1024]{1,0:T(8,128)(2,1)} collective-permute-done((bf16[512,1024]{1,0:T(8,128)(2,1)}, bf16[512,1024]{1,0:T(8,128)(2,1)}, u32[]{:S(2)}, u32[]{:S(2)}) %collective-permute-start.6) | collective-permute-done | bytes 1048608 | tf_op jit(solution)/shard_map/ppermute | solution.py:24
  150.7 2.4 fusion.115
  154.4 1.4 add_convert_fusion.5
  155.8 8.4 %multiply_convert_fusion = (bf16[512,2048]{1,0:T(8,128)(2,1)}, f32[512,2048]{1,0:T(8,128)}) fusion(f32[2048]{0:T(1024)S(1)} %add.366, bf16[512,1024]{1,0:T(8,128)(2,1)} %add_convert_fusion.5, bf16[1024,2048]{1,0:T(8,128)(2,1)} %all-gather.10.cloned.1.call-done), kind=kOutput, calls=%fused_computation.10 | convolution fusion | flops 2157969408 | bytes 11542528 | tf_op jit(solution)/shard_map/dot_general | solution.py:293
  164.2 8.7 %convert_reduce_fusion = (f32[2048]{0:T(1024)S(1)}, bf16[512,2048]{1,0:T(8,128)(2,1)S(1)}) fusion(f32[512,2048]{1,0:T(8,128)} %get-tuple-element.154, f32[2048]{0:T(1024)S(1)} %add.366, bf16[2048,1024]{1,0:T(8,128)(2,1)} %all-gather.12.cloned.1.call-done, bf16[1,512,1024]{2,1,0:T(8,128)(2,1)} %param.27), kind=kOutput, calls=%fused_computation.9 | convolution fusion | flops 2171598848 | bytes 11550720 | tf_op jit(solution)/shard_map/td,fd->tf/dot_general | solution.py:300
  172.9 2.4 convolution_convert_fusion.8
  175.3 1.7 collective-permute-start.7
  177.7 11.6 %convolution_convert_fusion = bf16[2048,256]{1,0:T(8,128)(2,1)S(1)} fusion(bf16[512,2048]{1,0:T(8,128)(2,1)S(1)} %copy-done.23, bf16[1,512,1024]{2,1,0:T(8,128)(2,1)S(1)} %copy-done.28, s32[]{:T(128)S(6)} %select_n.113), kind=kOutput, calls=%fused_computation.18 | convolution fusion | flops 537395200 | bytes 3407876 | tf_op jit(solution)/shard_map/tf,td->fd/dot_general | solution.py:311
  193.5 3.5 collective-permute-done.7
  197.4 2.4 convolution_convert_fusion.7
  199.8 1.7 collective-permute-start.8
  202.3 2.8 collective-permute-start.34
  207.0 15.7 %collective-permute-done.8 = bf16[512,1024]{1,0:T(8,128)(2,1)S(1)} collective-permute-done((bf16[512,1024]{1,0:T(8,128)(2,1)S(1)}, bf16[512,1024]{1,0:T(8,128)(2,1)S(1)}, u32[]{:S(2)}, u32[]{:S(2)}) %collective-permute-start.8) | collective-permute-done | bytes 1048608 | tf_op jit(solution)/shard_map/ppermute | solution.py:24
  222.7 2.7 convert_reduce_fusion.4
  227.0 1.4 collective-permute-start.9
  230.1 1.4 add_convert_fusion
  231.5 20.0 %collective-permute-done.9 = bf16[1024,512]{1,0:T(8,128)(2,1)S(1)} collective-permute-done((bf16[1024,512]{1,0:T(8,128)(2,1)S(1)}, bf16[1024,512]{1,0:T(8,128)(2,1)S(1)}, u32[]{:S(2)}, u32[]{:S(2)}) %collective-permute-start.9) | collective-permute-done | bytes 1048608 | tf_op jit(solution)/shard_map/ppermute | solution.py:18
  251.5 1.4 fusion.31
  252.9 1.4 collective-permute-start.10
  254.4 1.4 add_convert_fusion.2
  256.1 2.5 collective-permute-start.28
  263.8 12.6 %collective-permute-done.10 = bf16[1024,512]{1,0:T(8,128)(2,1)} collective-permute-done((bf16[1024,512]{1,0:T(8,128)(2,1)}, bf16[1024,512]{1,0:T(8,128)(2,1)}, u32[]{:S(2)}, u32[]{:S(2)}) %collective-permute-start.10) | collective-permute-done | bytes 1048608 | tf_op jit(solution)/shard_map/ppermute | solution.py:18
  276.4 2.3 fusion.30
  278.7 1.4 collective-permute-start.11
  280.1 6.8 %shard_map.252 = (f32[512,512]{1,0:T(8,128)S(1)}, f32[512,512]{1,0:T(8,128)S(1)}, f32[512,512]{1,0:T(8,128)S(1)}) custom-call(s32[1]{0:T(128)} %bitcast.1.refs_0_, bf16[512,512]{1,0:T(8,128)(2,1)S(1)} %copy-done.16, bf16[512,512]{1,0:T(8,128)(2,1)S(1)} %fusion.58.k_ref.refs_2_, bf16[512,512]{1,0:T(8,128)(2,1)S(1)} %fusion.43.v_ref.refs_3_, ...), custom_call_target="tpu_custom_call" | custom-call | flops 1342177280 | bytes 6291456 | tf_op jit(solution)/shard_map/pallas_call | solution.py:186
  289.0 60.6 %collective-permute-done.11 = bf16[1024,512]{1,0:T(8,128)(2,1)S(1)} collective-permute-done((bf16[1024,512]{1,0:T(8,128)(2,1)S(1)}, bf16[1024,512]{1,0:T(8,128)(2,1)S(1)}, u32[]{:S(2)}, u32[]{:S(2)}) %collective-permute-start.11) | collective-permute-done | bytes 1048608 | tf_op jit(solution)/shard_map/ppermute | solution.py:18
  352.6 46.5 %all-reduce.3.cloned.1.call-done = (bf16[512,256]{1,0:T(8,128)(2,1)}, bf16[256,2048]{1,0:T(8,128)(2,1)}, bf16[2048,256]{1,0:T(8,128)(2,1)}) async-done(((bf16[512,256]{1,0:T(8,128)(2,1)}, bf16[256,2048]{1,0:T(8,128)(2,1)}, bf16[2048,256]{1,0:T(8,128)(2,1)}), (bf16[512,256]{1,0:T(8,128)(2,1)}, bf16[256,2048]{1,0:T(8,128)(2,1)}, bf16[2048,256]{1,0:T(8,128)(2,1)})) %all-reduce.3.cloned.1.call-update) | async-done | bytes 2359312 | tf_op jit(solution)/shard_map/psum | solution.py:375
  399.2 2.9 convert_element_type.316
  402.0 1.5 convert_element_type.324
  406.3 1.8 fusion.96
  408.1 2.4 fusion.22
  411.1 1.6 convolution_convert_fusion.5
  412.7 1.5 collective-permute-start.23
  414.2 1.5 add_convert_fusion.7
  416.8 3.9 collective-permute-done.24
  422.0 3.2 fusion.57
  426.6 9.2 %collective-permute-done.15 = bf16[256,1536]{1,0:T(8,128)(2,1)} collective-permute-done((bf16[256,1536]{1,0:T(8,128)(2,1)}, bf16[256,1536]{1,0:T(8,128)(2,1)}, u32[]{:S(2)}, u32[]{:S(2)}) %collective-permute-start.15) | collective-permute-done | bytes 786464 | tf_op jit(solution)/shard_map/ppermute | solution.py:31
  435.7 1.4 add_convert_fusion.6
  437.3 1.9 collective-permute-start.17
  439.2 2.4 collective-permute-start.18
  442.7 4.3 collective-permute-done.16
  447.0 6.9 %collective-permute-done.17 = bf16[64,1536]{1,0:T(8,128)(2,1)S(1)} collective-permute-done((bf16[64,1536]{1,0:T(8,128)(2,1)S(1)}, bf16[64,1536]{1,0:T(8,128)(2,1)S(1)}, u32[]{:S(2)}, u32[]{:S(2)}) %collective-permute-start.17) | collective-permute-done | bytes 196640 | tf_op jit(solution)/shard_map/ppermute | solution.py:68
  454.1 3.8 collective-permute-start.19
  461.5 1.9 collective-permute-done.19
  463.5 7.3 %collective-permute-done.20 = bf16[64,1536]{1,0:T(8,128)(2,1)S(1)} collective-permute-done((bf16[64,1536]{1,0:T(8,128)(2,1)S(1)}, bf16[64,1536]{1,0:T(8,128)(2,1)S(1)}, u32[]{:S(2)}, u32[]{:S(2)}) %collective-permute-start.20) | collective-permute-done | bytes 196640 | tf_op jit(solution)/shard_map/ppermute | solution.py:73
  470.8 1.4 reshape.262
  472.2 1.6 copy.61
  (271 shorter events, 48.6 us)
Async XLA Ops:
  7.2 6.6 %copy-start.39 = (bf16[2,8,16]{2,1,0:T(8,128)(2,1)S(1)}, bf16[2,8,16]{2,1,0:T(8,128)(2,1)}, u32[]{:S(2)}) copy-start(bf16[2,8,16]{2,1,0:T(8,128)(2,1)} %param.16) | copy-start | bytes 1540
  7.2 6.7 %copy-start.38 = (bf16[32,16]{0,1:T(8,128)(2,1)S(1)}, bf16[32,16]{0,1:T(8,128)(2,1)}, u32[]{:S(2)}) copy-start(bf16[32,16]{0,1:T(8,128)(2,1)} %param.20) | copy-start | bytes 3076
  7.2 6.9 %copy-start.40 = (bf16[256]{0:T(256)(128)(2,1)S(1)}, bf16[256]{0:T(256)(128)(2,1)}, u32[]{:S(2)}) copy-start(bf16[256]{0:T(256)(128)(2,1)} %param.23) | copy-start | bytes 1540
  7.2 7.1 %copy-start.41 = (bf16[256]{0:T(256)(128)(2,1)S(1)}, bf16[256]{0:T(256)(128)(2,1)}, u32[]{:S(2)}) copy-start(bf16[256]{0:T(256)(128)(2,1)} %param.24) | copy-start | bytes 1540
  7.2 7.3 %copy-start.42 = (bf16[256]{0:T(256)(128)(2,1)S(1)}, bf16[256]{0:T(256)(128)(2,1)}, u32[]{:S(2)}) copy-start(bf16[256]{0:T(256)(128)(2,1)} %param.25) | copy-start | bytes 1540
  7.2 7.5 %copy-start.43 = (bf16[256]{0:T(256)(128)(2,1)S(1)}, bf16[256]{0:T(256)(128)(2,1)}, u32[]{:S(2)}) copy-start(bf16[256]{0:T(256)(128)(2,1)} %param.26) | copy-start | bytes 1540
  7.3 7.8 %copy-start.44 = (bf16[256]{0:T(256)(128)(2,1)S(1)}, bf16[256]{0:T(256)(128)(2,1)}, u32[]{:S(2)}) copy-start(bf16[256]{0:T(256)(128)(2,1)} %param.18) | copy-start | bytes 1540
  7.3 8.0 %copy-start.45 = (bf16[256]{0:T(256)(128)(2,1)S(1)}, bf16[256]{0:T(256)(128)(2,1)}, u32[]{:S(2)}) copy-start(bf16[256]{0:T(256)(128)(2,1)} %param.22) | copy-start | bytes 1540
  7.3 24.3 %copy-start.19 = (bf16[1,512,1024]{2,1,0:T(8,128)(2,1)S(1)}, bf16[1,512,1024]{2,1,0:T(8,128)(2,1)}, u32[]{:S(2)}) copy-start(bf16[1,512,1024]{2,1,0:T(8,128)(2,1)} %param.14) | copy-start | bytes 3145732
  7.3 94.7 %all-gather.14.cloned.1.call-start = ((), (), s32[]{:S(2)}) async-start(), calls=%async_computation.3 | async-start | bytes 1310720 | tf_op jit(solution)/shard_map/all_gather | solution.py:228
  9.1 115.5 %all-gather.8.cloned.1.call-start = ((), (), s32[]{:S(2)}) async-start(), calls=%async_computation | async-start | bytes 1310720 | tf_op jit(solution)/shard_map/all_gather | solution.py:248
  9.9 145.9 %all-gather.10.cloned.1.call-start = ((), (), s32[]{:S(2)}) async-start(), calls=%async_computation.1 | async-start | bytes 5242880 | tf_op jit(solution)/shard_map/all_gather | solution.py:249
  10.6 153.6 %all-gather.12.cloned.1.call-start = ((), (), s32[]{:S(2)}) async-start(), calls=%async_computation.2 | async-start | bytes 5242880 | tf_op jit(solution)/shard_map/all_gather | solution.py:250
  10.7 24.2 %collective-permute-start = (bf16[2,256,512]{2,1,0:T(8,128)(2,1)S(1)}, bf16[2,256,512]{2,1,0:T(8,128)(2,1)}, u32[]{:S(2)}, u32[]{:S(2)}) collective-permute-start(bf16[2,256,512]{2,1,0:T(8,128)(2,1)S(1)} %slice_bitcast_fusion.1), channel_id=1, source_target_pairs={{0,8},{8,0},{16,24},{24,16},{1,9},{9,1},{17,25},{25,17},{2,10},{10... | collective-permute-start | bytes 1572872 | tf_op jit(solution)/shard_map/ppermute | solution.py:31
  11.2 23.3 %collective-permute-start.1 = (bf16[2,256,512]{2,1,0:T(8,128)(2,1)S(1)}, bf16[2,256,512]{2,1,0:T(8,128)(2,1)S(1)}, u32[]{:S(2)}, u32[]{:S(2)}) collective-permute-start(bf16[2,256,512]{2,1,0:T(8,128)(2,1)S(1)} %slice_bitcast_fusion.1), channel_id=1, source_target_pairs={{0,16},{8,24},{16,0},{24,8},{1,17},{9,25},{17,1},{25,9},{2,18},{10... | collective-permute-start | bytes 1572872 | tf_op jit(solution)/shard_map/ppermute | solution.py:31
  34.5 4.9 %collective-permute-start.2 = (bf16[2,256,512]{2,1,0:T(8,128)(2,1)S(1)}, bf16[2,256,512]{2,1,0:T(8,128)(2,1)S(1)}, u32[]{:S(2)}, u32[]{:S(2)}) collective-permute-start(bf16[2,256,512]{2,1,0:T(8,128)(2,1)S(1)} %collective-permute-done.1), channel_id=1, source_target_pairs={{0,8},{8,0},{16,24},{24,16},{1,9},{9,1},{17,25},{25,17},{2,10},{10... | collective-permute-start | bytes 1572872 | tf_op jit(solution)/shard_map/ppermute | solution.py:31
  42.3 27.4 %collective-permute-start.3 = (bf16[1024,512]{1,0:T(8,128)(2,1)}, bf16[1024,512]{1,0:T(8,128)(2,1)S(1)}, u32[]{:S(2)}, u32[]{:S(2)}) collective-permute-start(bf16[1024,512]{1,0:T(8,128)(2,1)} %pad_maximum_fusion.1), channel_id=1, source_target_pairs={{0,2},{2,4},{4,6},{1,3},{3,5},{5,7},{8,10},{10,12},{12,14},{9,11},... | collective-permute-start | bytes 3145736 | tf_op jit(solution)/shard_map/ppermute | solution.py:18
  46.7 352.5 %all-reduce.3.cloned.1.call-start = ((), (), s32[]{:S(2)}) async-start(), calls=%async_computation.4 | async-start | bytes 4718592 | tf_op jit(solution)/shard_map/psum | solution.py:375
  69.6 26.3 %copy-start.35 = (bf16[1024,512]{1,0:T(8,128)(2,1)}, bf16[1024,512]{1,0:T(8,128)(2,1)S(1)}, u32[]{:S(2)}) copy-start(bf16[1024,512]{1,0:T(8,128)(2,1)S(1)} %collective-permute-done.3) | copy-start | bytes 3145732
  69.6 26.3 %collective-permute-start.4 = (bf16[1024,512]{1,0:T(8,128)(2,1)S(1)}, bf16[1024,512]{1,0:T(8,128)(2,1)}, u32[]{:S(2)}, u32[]{:S(2)}) collective-permute-start(bf16[1024,512]{1,0:T(8,128)(2,1)S(1)} %collective-permute-done.3), channel_id=1, source_target_pairs={{0,2},{2,4},{4,6},{1,3},{3,5},{5,7},{8,10},{10,12},{12,14},{9,11},... | collective-permute-start | bytes 3145736 | tf_op jit(solution)/shard_map/ppermute | solution.py:18
  95.9 25.9 %collective-permute-start.5 = (bf16[1024,512]{1,0:T(8,128)(2,1)}, bf16[1024,512]{1,0:T(8,128)(2,1)}, u32[]{:S(2)}, u32[]{:S(2)}) collective-permute-start(bf16[1024,512]{1,0:T(8,128)(2,1)} %collective-permute-done.4), channel_id=1, source_target_pairs={{0,2},{2,4},{4,6},{1,3},{3,5},{5,7},{8,10},{10,12},{12,14},{9,11},... | collective-permute-start | bytes 3145736 | tf_op jit(solution)/shard_map/ppermute | solution.py:18
  101.9 7.0 %copy-start.33 = (bf16[512,1024]{1,0:T(8,128)(2,1)}, bf16[512,1024]{1,0:T(8,128)(2,1)S(1)}, u32[]{:S(2)}) copy-start(bf16[512,1024]{1,0:T(8,128)(2,1)S(1)} %fusion.16) | copy-start | bytes 3145732
  104.3 18.9 %copy-start.14 = (bf16[512,512]{1,0:T(8,128)(2,1)}, bf16[512,512]{1,0:T(8,128)(2,1)S(1)}, u32[]{:S(2)}) copy-start(bf16[512,512]{1,0:T(8,128)(2,1)S(1)} %fusion.37.q_ref.refs_1_) | copy-start | bytes 1572868
  104.3 4.6 copy-start.36
  110.7 12.5 %copy-start.10 = (bf16[512,512]{1,0:T(8,128)(2,1)}, bf16[512,512]{1,0:T(8,128)(2,1)S(1)}, u32[]{:S(2)}) copy-start(bf16[512,512]{1,0:T(8,128)(2,1)S(1)} %get-tuple-element.130.refs_3_) | copy-start | bytes 1572868
  110.7 12.5 %copy-start.12 = (bf16[512,512]{1,0:T(8,128)(2,1)}, bf16[512,512]{1,0:T(8,128)(2,1)S(1)}, u32[]{:S(2)}) copy-start(bf16[512,512]{1,0:T(8,128)(2,1)S(1)} %get-tuple-element.131.refs_2_) | copy-start | bytes 1572868
  127.8 22.9 %collective-permute-start.6 = (bf16[512,1024]{1,0:T(8,128)(2,1)}, bf16[512,1024]{1,0:T(8,128)(2,1)}, u32[]{:S(2)}, u32[]{:S(2)}) collective-permute-start(bf16[512,1024]{1,0:T(8,128)(2,1)} %convolution_convert_fusion.6), channel_id=1, source_target_pairs={{0,1},{1,0},{2,3},{3,2},{4,5},{5,4},{6,7},{7,6},{8,9},{9,8},{10,11... | collective-permute-start | bytes 3145736 | tf_op jit(solution)/shard_map/ppermute | solution.py:24
  164.2 8.7 %copy-start.46 = (bf16[1024,2048]{1,0:T(8,128)(2,1)S(1)}, bf16[1024,2048]{1,0:T(8,128)(2,1)}, u32[]{:S(2)}) copy-start(bf16[1024,2048]{1,0:T(8,128)(2,1)} %all-gather.10.cloned.1.call-done) | copy-start | bytes 12582916
  172.9 4.1 copy-start.24
  175.3 21.7 %collective-permute-start.7 = (bf16[512,1024]{1,0:T(8,128)(2,1)S(1)}, bf16[512,1024]{1,0:T(8,128)(2,1)S(1)}, u32[]{:S(2)}, u32[]{:S(2)}) collective-permute-start(bf16[512,1024]{1,0:T(8,128)(2,1)S(1)} %convolution_convert_fusion.8), channel_id=1, source_target_pairs={{0,1},{1,0},{2,3},{3,2},{4,5},{5,4},{6,7},{7,6},{8,9},{9,8},{10,11... | collective-permute-start | bytes 3145736 | tf_op jit(solution)/shard_map/ppermute | solution.py:24
  189.3 12.2 %collective-permute-start.33 = (bf16[2048,256]{1,0:T(8,128)(2,1)S(1)}, bf16[2048,256]{1,0:T(8,128)(2,1)S(1)}, u32[]{:S(2)}, u32[]{:S(2)}) collective-permute-start(bf16[2048,256]{1,0:T(8,128)(2,1)S(1)} %convolution_convert_fusion), channel_id=1, source_target_pairs={{0,8},{8,0},{16,24},{24,16},{1,9},{9,1},{17,25},{25,17},{2,10},{10... | collective-permute-start | bytes 3145736 | tf_op jit(solution)/shard_map/ppermute | solution.py:31
  192.5 5.0 %copy-start.47 = (bf16[2048,1024]{1,0:T(8,128)(2,1)S(1)}, bf16[2048,1024]{1,0:T(8,128)(2,1)}, u32[]{:S(2)}) copy-start(bf16[2048,1024]{1,0:T(8,128)(2,1)} %all-gather.12.cloned.1.call-done) | copy-start | bytes 12582916
  192.5 37.0 %collective-permute-start.32 = (bf16[2048,256]{1,0:T(8,128)(2,1)S(1)}, bf16[2048,256]{1,0:T(8,128)(2,1)S(1)}, u32[]{:S(2)}, u32[]{:S(2)}) collective-permute-start(bf16[2048,256]{1,0:T(8,128)(2,1)S(1)} %convolution_convert_fusion.1), channel_id=1, source_target_pairs={{0,8},{8,0},{16,24},{24,16},{1,9},{9,1},{17,25},{25,17},{2,10},{10... | collective-permute-start | bytes 3145736 | tf_op jit(solution)/shard_map/ppermute | solution.py:31
  193.0 12.1 %collective-permute-start.30 = (bf16[256,2048]{1,0:T(8,128)(2,1)S(1)}, bf16[256,2048]{1,0:T(8,128)(2,1)S(1)}, u32[]{:S(2)}, u32[]{:S(2)}) collective-permute-start(bf16[256,2048]{1,0:T(8,128)(2,1)S(1)} %convolution_convert_fusion.2), channel_id=1, source_target_pairs={{0,8},{8,0},{16,24},{24,16},{1,9},{9,1},{17,25},{25,17},{2,10},{10... | collective-permute-start | bytes 3145736 | tf_op jit(solution)/shard_map/ppermute | solution.py:31
  193.1 61.2 %collective-permute-start.29 = (bf16[256,2048]{1,0:T(8,128)(2,1)S(1)}, bf16[256,2048]{1,0:T(8,128)(2,1)S(1)}, u32[]{:S(2)}, u32[]{:S(2)}) collective-permute-start(bf16[256,2048]{1,0:T(8,128)(2,1)S(1)} %convolution_convert_fusion.3), channel_id=1, source_target_pairs={{0,8},{8,0},{16,24},{24,16},{1,9},{9,1},{17,25},{25,17},{2,10},{10... | collective-permute-start | bytes 3145736 | tf_op jit(solution)/shard_map/ppermute | solution.py:31
  199.8 22.8 %collective-permute-start.8 = (bf16[512,1024]{1,0:T(8,128)(2,1)S(1)}, bf16[512,1024]{1,0:T(8,128)(2,1)S(1)}, u32[]{:S(2)}, u32[]{:S(2)}) collective-permute-start(bf16[512,1024]{1,0:T(8,128)(2,1)S(1)} %convolution_convert_fusion.7), channel_id=1, source_target_pairs={{0,1},{1,0},{2,3},{3,2},{4,5},{5,4},{6,7},{7,6},{8,9},{9,8},{10,11... | collective-permute-start | bytes 3145736 | tf_op jit(solution)/shard_map/ppermute | solution.py:24
  202.3 27.3 %collective-permute-start.34 = (bf16[2048,256]{1,0:T(8,128)(2,1)S(1)}, bf16[2048,256]{1,0:T(8,128)(2,1)S(1)}, u32[]{:S(2)}, u32[]{:S(2)}) collective-permute-start(bf16[2048,256]{1,0:T(8,128)(2,1)S(1)} %add_convert_fusion.1), channel_id=1, source_target_pairs={{0,16},{8,24},{16,0},{24,8},{1,17},{9,25},{17,1},{25,9},{2,18},{10... | collective-permute-start | bytes 3145736 | tf_op jit(solution)/shard_map/ppermute | solution.py:31
  205.9 48.5 %collective-permute-start.31 = (bf16[256,2048]{1,0:T(8,128)(2,1)S(1)}, bf16[256,2048]{1,0:T(8,128)(2,1)S(1)}, u32[]{:S(2)}, u32[]{:S(2)}) collective-permute-start(bf16[256,2048]{1,0:T(8,128)(2,1)S(1)} %add_convert_fusion.3), channel_id=1, source_target_pairs={{0,16},{8,24},{16,0},{24,8},{1,17},{9,25},{17,1},{25,9},{2,18},{10... | collective-permute-start | bytes 3145736 | tf_op jit(solution)/shard_map/ppermute | solution.py:31
  226.1 32.5 %copy-start.4 = (bf16[512,512]{0,1:T(8,128)(2,1)}, bf16[512,512]{0,1:T(8,128)(2,1)S(1)}, u32[]{:S(2)}) copy-start(bf16[512,512]{0,1:T(8,128)(2,1)S(1)} %get-tuple-element.156) | copy-start | bytes 1572868
  227.0 24.5 %collective-permute-start.9 = (bf16[1024,512]{1,0:T(8,128)(2,1)S(1)}, bf16[1024,512]{1,0:T(8,128)(2,1)S(1)}, u32[]{:S(2)}, u32[]{:S(2)}) collective-permute-start(bf16[1024,512]{1,0:T(8,128)(2,1)S(1)} %pad_maximum_fusion.2), channel_id=1, source_target_pairs={{2,0},{4,2},{6,4},{3,1},{5,3},{7,5},{10,8},{12,10},{14,12},{11,9},... | collective-permute-start | bytes 3145736 | tf_op jit(solution)/shard_map/ppermute | solution.py:18
  229.5 26.3 %collective-permute-start.27 = (bf16[512,256]{1,0:T(8,128)(2,1)S(1)}, bf16[512,256]{1,0:T(8,128)(2,1)S(1)}, u32[]{:S(2)}, u32[]{:S(2)}) collective-permute-start(bf16[512,256]{1,0:T(8,128)(2,1)S(1)} %convolution_convert_fusion.10), channel_id=1, source_target_pairs={{0,8},{8,0},{16,24},{24,16},{1,9},{9,1},{17,25},{25,17},{2,10},{10... | collective-permute-start | bytes 786440 | tf_op jit(solution)/shard_map/ppermute | solution.py:31
  229.6 32.6 %collective-permute-start.26 = (bf16[512,256]{1,0:T(8,128)(2,1)S(1)}, bf16[512,256]{1,0:T(8,128)(2,1)S(1)}, u32[]{:S(2)}, u32[]{:S(2)}) collective-permute-start(bf16[512,256]{1,0:T(8,128)(2,1)S(1)} %convolution_convert_fusion.11), channel_id=1, source_target_pairs={{0,8},{8,0},{16,24},{24,16},{1,9},{9,1},{17,25},{25,17},{2,10},{10... | collective-permute-start | bytes 786440 | tf_op jit(solution)/shard_map/ppermute | solution.py:31
  252.9 5.7 %copy-start.7 = (bf16[512,512]{1,0:T(8,128)(2,1)S(1)}, bf16[512,512]{1,0:T(8,128)(2,1)}, u32[]{:S(2)}) copy-start(bf16[512,512]{1,0:T(8,128)(2,1)} %copy-done.6) | copy-start | bytes 1572868
  252.9 5.7 %copy-start.9 = (bf16[512,512]{1,0:T(8,128)(2,1)S(1)}, bf16[512,512]{1,0:T(8,128)(2,1)}, u32[]{:S(2)}) copy-start(bf16[512,512]{1,0:T(8,128)(2,1)} %copy-done.8) | copy-start | bytes 1572868
  252.9 23.4 %collective-permute-start.10 = (bf16[1024,512]{1,0:T(8,128)(2,1)}, bf16[1024,512]{1,0:T(8,128)(2,1)}, u32[]{:S(2)}, u32[]{:S(2)}) collective-permute-start(bf16[1024,512]{1,0:T(8,128)(2,1)} %fusion.31), channel_id=1, source_target_pairs={{2,0},{4,2},{6,4},{3,1},{5,3},{7,5},{10,8},{12,10},{14,12},{11,9},... | collective-permute-start | bytes 3145736 | tf_op jit(solution)/shard_map/ppermute | solution.py:18
  256.1 6.9 %collective-permute-start.28 = (bf16[512,256]{1,0:T(8,128)(2,1)S(1)}, bf16[512,256]{1,0:T(8,128)(2,1)S(1)}, u32[]{:S(2)}, u32[]{:S(2)}) collective-permute-start(bf16[512,256]{1,0:T(8,128)(2,1)S(1)} %add_convert_fusion.10), channel_id=1, source_target_pairs={{0,16},{8,24},{16,0},{24,8},{1,17},{9,25},{17,1},{25,9},{2,18},{10... | collective-permute-start | bytes 786440 | tf_op jit(solution)/shard_map/ppermute | solution.py:31
  278.7 8.3 %copy-start.1 = (f32[512,512]{1,0:T(8,128)S(1)}, f32[512,512]{1,0:T(8,128)}, u32[]{:S(2)}) copy-start(f32[512,512]{1,0:T(8,128)} %copy-done) | copy-start | bytes 3145732
  278.7 70.9 %collective-permute-start.11 = (bf16[1024,512]{1,0:T(8,128)(2,1)S(1)}, bf16[1024,512]{1,0:T(8,128)(2,1)S(1)}, u32[]{:S(2)}, u32[]{:S(2)}) collective-permute-start(bf16[1024,512]{1,0:T(8,128)(2,1)S(1)} %fusion.30), channel_id=1, source_target_pairs={{2,0},{4,2},{6,4},{3,1},{5,3},{7,5},{10,8},{12,10},{14,12},{11,9},... | collective-permute-start | bytes 3145736 | tf_op jit(solution)/shard_map/ppermute | solution.py:18
  352.5 55.6 %collective-permute-start.12 = (bf16[512,1024]{1,0:T(8,128)(2,1)S(1)}, bf16[512,1024]{1,0:T(8,128)(2,1)}, u32[]{:S(2)}, u32[]{:S(2)}) collective-permute-start(bf16[512,1024]{1,0:T(8,128)(2,1)S(1)} %fusion.32), channel_id=1, source_target_pairs={{0,1},{1,0},{2,3},{3,2},{4,5},{5,4},{6,7},{7,6},{8,9},{9,8},{10,11... | collective-permute-start | bytes 3145736 | tf_op jit(solution)/shard_map/ppermute | solution.py:24
  406.2 8.0 %collective-permute-start.14 = (bf16[256,1536]{1,0:T(8,128)(2,1)S(1)}, bf16[256,1536]{1,0:T(8,128)(2,1)S(1)}, u32[]{:S(2)}, u32[]{:S(2)}) collective-permute-start(bf16[256,1536]{1,0:T(8,128)(2,1)S(1)} %convolution_convert_fusion.4), channel_id=1, source_target_pairs={{0,8},{8,0},{16,24},{24,16},{1,9},{9,1},{17,25},{25,17},{2,10},{10... | collective-permute-start | bytes 2359304 | tf_op jit(solution)/shard_map/ppermute | solution.py:31
  410.5 2.1 collective-permute-start.22
  412.7 13.9 %collective-permute-start.13 = (bf16[256,1536]{1,0:T(8,128)(2,1)}, bf16[256,1536]{1,0:T(8,128)(2,1)S(1)}, u32[]{:S(2)}, u32[]{:S(2)}) collective-permute-start(bf16[256,1536]{1,0:T(8,128)(2,1)} %convolution_convert_fusion.5), channel_id=1, source_target_pairs={{0,8},{8,0},{16,24},{24,16},{1,9},{9,1},{17,25},{25,17},{2,10},{10... | collective-permute-start | bytes 2359304 | tf_op jit(solution)/shard_map/ppermute | solution.py:31
  412.7 9.4 %copy-start.22 = (f32[512,1024]{1,0:T(8,128)S(1)}, f32[512,1024]{1,0:T(8,128)}, u32[]{:S(2)}) copy-start(f32[512,1024]{1,0:T(8,128)} %get-tuple-element.121) | copy-start | bytes 6291460
  412.7 4.0 collective-permute-start.23
  415.8 20.0 %collective-permute-start.15 = (bf16[256,1536]{1,0:T(8,128)(2,1)}, bf16[256,1536]{1,0:T(8,128)(2,1)}, u32[]{:S(2)}, u32[]{:S(2)}) collective-permute-start(bf16[256,1536]{1,0:T(8,128)(2,1)} %add_convert_fusion.7), channel_id=1, source_target_pairs={{0,16},{8,24},{16,0},{24,8},{1,17},{9,25},{17,1},{25,9},{2,18},{10... | collective-permute-start | bytes 2359304 | tf_op jit(solution)/shard_map/ppermute | solution.py:31
  416.7 4.0 collective-permute-start.24
  420.7 4.9 %collective-permute-start.25 = (f32[9216]{0:T(1024)S(1)}, f32[9216]{0:T(1024)S(1)}, u32[]{:S(2)}, u32[]{:S(2)}) collective-permute-start(f32[9216]{0:T(1024)S(1)} %add.415), channel_id=1, source_target_pairs={{0,4},{2,6},{4,0},{6,2},{1,5},{3,7},{5,1},{7,3},{8,12},{10,14},{12... | collective-permute-start | bytes 110600 | tf_op jit(solution)/shard_map/ppermute | solution.py:31
  422.0 13.7 %copy-start.29 = (f32[256,1536]{1,0:T(8,128)S(1)}, f32[256,1536]{1,0:T(8,128)}, u32[]{:S(2)}) copy-start(f32[256,1536]{1,0:T(8,128)} %fusion.96) | copy-start | bytes 4718596
  437.2 9.8 %collective-permute-start.16 = (bf16[64,1536]{1,0:T(8,128)(2,1)S(1)}, bf16[64,1536]{1,0:T(8,128)(2,1)S(1)}, u32[]{:S(2)}, u32[]{:S(2)}) collective-permute-start(bf16[64,1536]{1,0:T(8,128)(2,1)S(1)} %get-tuple-element.134), channel_id=1, source_target_pairs={{0,2},{2,4},{4,6},{6,0},{1,3},{3,5},{5,7},{7,1},{8,10},{10,12},{12... | collective-permute-start | bytes 589832 | tf_op jit(solution)/shard_map/ppermute | solution.py:68
  437.3 16.6 %collective-permute-start.17 = (bf16[64,1536]{1,0:T(8,128)(2,1)S(1)}, bf16[64,1536]{1,0:T(8,128)(2,1)S(1)}, u32[]{:S(2)}, u32[]{:S(2)}) collective-permute-start(bf16[64,1536]{1,0:T(8,128)(2,1)S(1)} %get-tuple-element.136), channel_id=1, source_target_pairs={{0,4},{2,6},{4,0},{6,2},{1,5},{3,7},{5,1},{7,3},{8,12},{10,14},{12... | collective-permute-start | bytes 589832 | tf_op jit(solution)/shard_map/ppermute | solution.py:68
  439.2 14.8 %collective-permute-start.18 = (bf16[64,1536]{1,0:T(8,128)(2,1)S(1)}, bf16[64,1536]{1,0:T(8,128)(2,1)S(1)}, u32[]{:S(2)}, u32[]{:S(2)}) collective-permute-start(bf16[64,1536]{1,0:T(8,128)(2,1)S(1)} %get-tuple-element.135), channel_id=1, source_target_pairs={{0,6},{2,0},{4,2},{6,4},{1,7},{3,1},{5,3},{7,5},{8,14},{10,8},{12,... | collective-permute-start | bytes 589832 | tf_op jit(solution)/shard_map/ppermute | solution.py:68
  454.1 9.3 %collective-permute-start.19 = (bf16[64,1536]{1,0:T(8,128)(2,1)S(1)}, bf16[64,1536]{1,0:T(8,128)(2,1)S(1)}, u32[]{:S(2)}, u32[]{:S(2)}) collective-permute-start(bf16[64,1536]{1,0:T(8,128)(2,1)S(1)} %get-tuple-element.123), channel_id=1, source_target_pairs={{0,2},{2,4},{4,6},{6,0},{1,3},{3,5},{5,7},{7,1},{8,10},{10,12},{12... | collective-permute-start | bytes 589832 | tf_op jit(solution)/shard_map/ppermute | solution.py:73
  459.1 11.7 %collective-permute-start.20 = (bf16[64,1536]{1,0:T(8,128)(2,1)S(1)}, bf16[64,1536]{1,0:T(8,128)(2,1)S(1)}, u32[]{:S(2)}, u32[]{:S(2)}) collective-permute-start(bf16[64,1536]{1,0:T(8,128)(2,1)S(1)} %get-tuple-element.123), channel_id=1, source_target_pairs={{0,4},{2,6},{4,0},{6,2},{1,5},{3,7},{5,1},{7,3},{8,12},{10,14},{12... | collective-permute-start | bytes 589832 | tf_op jit(solution)/shard_map/ppermute | solution.py:73
  460.4 10.5 %collective-permute-start.21 = (bf16[64,1536]{1,0:T(8,128)(2,1)S(1)}, bf16[64,1536]{1,0:T(8,128)(2,1)S(1)}, u32[]{:S(2)}, u32[]{:S(2)}) collective-permute-start(bf16[64,1536]{1,0:T(8,128)(2,1)S(1)} %get-tuple-element.123), channel_id=1, source_target_pairs={{0,6},{2,0},{4,2},{6,4},{1,7},{3,1},{5,3},{7,5},{8,14},{10,8},{12,... | collective-permute-start | bytes 589832 | tf_op jit(solution)/shard_map/ppermute | solution.py:73
  (24 other events, 47.7 us)
Sparse Core Ops, SparseCore 0:
  10.3 23.3 all-gather.13
  35.2 18.2 all-gather.7
  55.1 34.4 all-gather.9
  91.0 35.0 all-gather.11
  263.9 135.1 all-reduce.2

commit v3 on v2

--- a/solution.py
+++ b/solution.py
@@ -73,6 +73,27 @@
         other = lax.ppermute(total, "ctx", pairs)
         whole = lax.dynamic_update_index_in_dim(whole, other, (mine + count - step) % count, 0)
     return whole.reshape(value.shape).astype(F32)
+
+
+def line_total(value):
+    count = lax.axis_size("ctx")
+    if count % 2:
+        return lax.psum(value.astype(BF16), "ctx").astype(F32)
+    mine = lax.axis_index("ctx")
+    half = value.shape[0] // 2
+    first, second = value[:half], value[half:]
+    arrived = 0.0
+    hops = [[(hop, hop + 1), (count - 1 - hop, count - 2 - hop)] for hop in range(count - 1)]
+    for hop, pairs in enumerate(hops):
+        sent = (jnp.where(mine == hop, first, second) + arrived).astype(BF16)
+        arrived = lax.ppermute(sent, "ctx", pairs).astype(F32)
+    held = (jnp.where(mine == count - 1, first, second) + arrived).astype(BF16)
+    total_first, total_second = held, held
+    for hop, pairs in enumerate(hops):
+        held = lax.ppermute(held, "ctx", pairs)
+        total_first = jnp.where(mine == count - 2 - hop, held, total_first)
+        total_second = jnp.where(mine == hop + 1, held, total_second)
+    return jnp.concatenate([total_first, total_second], axis=0).astype(F32)
 
 
 def small_total(value):
@@ -302,9 +323,6 @@
     grad_normed_two = pair_sum(
         jnp.einsum("tf,df->td", grad_pre, mlp_up, preferred_element_type=F32)
     )
-    later_act, grad_normed_two = lax.optimization_barrier((hidden_act, grad_normed_two))
-    mlp_part = pair_sum(jnp.dot(later_act, mlp_down, preferred_element_type=F32))
-    output = (resid + mlp_part + bias_down).astype(BF16).reshape(shape)
 
     grad_down = scatter_product(
         grad_rows,
@@ -331,6 +349,10 @@
         lambda part: jnp.einsum("ht,td->hd", attended_low, part, preferred_element_type=F32),
     )
 
+    later_act, grad_attended = lax.optimization_barrier((hidden_act, grad_attended))
+    mlp_part = jnp.dot(later_act, mlp_down, preferred_element_type=F32)
+    mlp_part = pair_sum(mlp_part)
+
     grad_query = 0.0
     arrived = None
     for distance in range(ctx_size - 1, -1, -1):
@@ -353,6 +375,8 @@
         block = block.astype(BF16)
         if distance > 0:
             arrived = ahead(block, "ctx", -1)
+    mlp_part, block = lax.optimization_barrier((mlp_part, block))
+    output = (resid + mlp_part + bias_down).astype(BF16).reshape(shape)
     grad_mixed = jnp.concatenate([grad_query.astype(BF16), block], axis=0)
     grad_mixed = grad_mixed.reshape(3, half_width, count)
     grad_bias_in = jnp.sum(grad_mixed[0::2], axis=2, dtype=F32)
@@ -371,9 +395,7 @@
     grad_inputs = grad_resid + norm_back(grad_normed_one, xhat_one, scale_one, gain_one)
     grad_inputs = grad_inputs.astype(BF16).reshape(shape)
 
-    grad_up, grad_down, grad_out = [
-        lax.psum(item.astype(BF16), "ctx").astype(F32) for item in (grad_up, grad_down, grad_out)
-    ]
+    grad_down, grad_up, grad_out = [line_total(item) for item in (grad_down, grad_up, grad_out)]
     grad_attn_in = ctx_total(grad_attn_in).reshape(-1, 3, half_width)
 
     grads_small = (

time: 490 us -> 509 us (1.039)
  starting transfers between devices: 49.6 us -> 105 us
  waiting for transfers between devices: 271 us -> 248 us
  other arithmetic: 32.5 us -> 24.5 us
    ppermute x0 -> x18, waiting for transfers between devices: none -> 118 us  [the longest x9 89.5 us: line_total(): arrived = lax.ppermute(sent, 'ctx', pairs).astype(F32)]
    ppermute x6, waiting for transfers between devices: 148 us -> 55.1 us  [ahead(): lax.ppermute(value, axis, [(source, source + steps) for source in range(f...]
    ppermute x0 -> x18, starting transfers between devices: none -> 47.6 us  [the longest x9 36.9 us: line_total(): arrived = lax.ppermute(sent, 'ctx', pairs).astype(F32)]
    psum x1 -> x0, waiting for transfers between devices: 46.5 us -> none  [local(): lax.psum(item.astype(BF16), 'ctx').astype(F32)]
    ppermute x19, starting transfers between devices: 14.6 us -> 22.6 us  [flipped(): lax.ppermute(value, axis, [(source, source ^ bit) for source in range(cou...]
    dot_general x4, matrix products: 13.9 us -> 6.33 us  [local(): jnp.einsum('tf,td->fd', hidden_act, part, preferred_element_type=F32)]
    ppermute x4, waiting for transfers between devices: 40.2 us -> 34.8 us  [pair_sum(): other = lax.ppermute(low, 'tensor', [(0, 1), (1, 0)])]
    convert_element_type x7 -> x15, other arithmetic: 10.2 us -> 5.36 us  [the longest x3 3.86 us: line_total(): return jnp.concatenate([total_first, total_second], axis=0).astype(F32)]
  transfers between devices with their start and end apart: 40 -> 57, of which waited for: 19 -> 22; matrix products, arithmetic and copies ran while one was open for 19% -> 16% of each run, Pallas kernels for 3% -> 3%
where the time goes in v3:
time: 509 us; the launch traced here: 500 us
  waiting for transfers between devices  248 us (49%)
  starting transfers between devices  105 us (21%)
  matrix products  51.1 us (10%)
  local copies, waits for them, and re-layouts  27 us (5%)
  other arithmetic  24.5 us (5%)
  between operations  15.7 us (3%)
  blocking collectives  15.6 us (3%)
  Pallas kernels  13.8 us (3%)
    ppermute x9, waiting for transfers between devices, line_total(): arrived = lax.ppermute(sent, 'ctx', pairs).astype(F32)  89.5 us
    ppermute x6, waiting for transfers between devices, ahead(): lax.ppermute(value, axis, [(source, source + steps) for source in range(f...  55.1 us
    ppermute x9, starting transfers between devices, line_total(): arrived = lax.ppermute(sent, 'ctx', pairs).astype(F32)  36.9 us
    ppermute x4, waiting for transfers between devices, pair_sum(): other = lax.ppermute(low, 'tensor', [(0, 1), (1, 0)])  34.8 us
    ppermute x9, waiting for transfers between devices, line_total(): held = lax.ppermute(held, 'ctx', pairs)  28.9 us
    ppermute x19, starting transfers between devices, flipped(): lax.ppermute(value, axis, [(source, source ^ bit) for source in range(cou...  22.6 us
    ppermute x6, starting transfers between devices, ahead(): lax.ppermute(value, axis, [(source, source + steps) for source in range(f...  19 us
    ppermute x19, waiting for transfers between devices, flipped(): lax.ppermute(value, axis, [(source, source ^ bit) for source in range(cou...  16.7 us
  transfers between devices with their start and end apart: 57, of which 22 were waited for; matrix products, arithmetic and copies ran while one was open for 16% of the time, Pallas kernels for 3%

profile of v3, /device:TPU:0, one launch (start us, length us, event | category | flops | bytes accessed | tf_op | source)
XLA Modules:
  0.0 500.5 jit_solution(9594751265109895379)
XLA Ops:
  7.3 1.8 slice.196
  11.2 2.6 collective-permute-start.1
  15.9 15.6 %all-gather.2 = bf16[4,1,2304]{2,1,0:T(2,128)(2,1)S(1)} all-gather(bf16[1,1,2304]{2,1,0:T(2,128)(2,1)S(1)} %reshape.266), channel_id=2, replica_groups=mesh['dp'=4,'ctx'=4,'tensor'=2] {'dp'}, dimensions={0}, use_global_device_ids=true | all-gather | bytes 23040 | tf_op jit(solution)/shard_map/all_gather | solution.py:260
  35.0 1.9 bitcast_dynamic-update-slice_fusion.3
  37.7 1.8 copy.55
  42.3 4.4 collective-permute-start.3
  46.7 23.0 %collective-permute-done.3 = bf16[1024,512]{1,0:T(8,128)(2,1)S(1)} collective-permute-done((bf16[1024,512]{1,0:T(8,128)(2,1)}, bf16[1024,512]{1,0:T(8,128)(2,1)S(1)}, u32[]{:S(2)}, u32[]{:S(2)}) %collective-permute-start.3) | collective-permute-done | bytes 1048608 | tf_op jit(solution)/shard_map/ppermute | solution.py:18
  69.6 5.3 %collective-permute-start.4 = (bf16[1024,512]{1,0:T(8,128)(2,1)S(1)}, bf16[1024,512]{1,0:T(8,128)(2,1)}, u32[]{:S(2)}, u32[]{:S(2)}) collective-permute-start(bf16[1024,512]{1,0:T(8,128)(2,1)S(1)} %collective-permute-done.3), channel_id=1, source_target_pairs={{0,2},{2,4},{4,6},{1,3},{3,5},{5,7},{8,10},{10,12},{12,14},{9,11},... | collective-permute-start | bytes 3145736 | tf_op jit(solution)/shard_map/ppermute | solution.py:18
  74.9 21.0 %collective-permute-done.4 = bf16[1024,512]{1,0:T(8,128)(2,1)} collective-permute-done((bf16[1024,512]{1,0:T(8,128)(2,1)S(1)}, bf16[1024,512]{1,0:T(8,128)(2,1)}, u32[]{:S(2)}, u32[]{:S(2)}) %collective-permute-start.4) | collective-permute-done | bytes 1048608 | tf_op jit(solution)/shard_map/ppermute | solution.py:18
  96.0 5.5 %collective-permute-start.5 = (bf16[1024,512]{1,0:T(8,128)(2,1)}, bf16[1024,512]{1,0:T(8,128)(2,1)}, u32[]{:S(2)}, u32[]{:S(2)}) collective-permute-start(bf16[1024,512]{1,0:T(8,128)(2,1)} %collective-permute-done.4), channel_id=1, source_target_pairs={{0,2},{2,4},{4,6},{1,3},{3,5},{5,7},{8,10},{10,12},{12,14},{9,11},... | collective-permute-start | bytes 3145736 | tf_op jit(solution)/shard_map/ppermute | solution.py:18
  102.0 2.3 fusion.40.q_ref.refs_1_
  104.3 4.6 shard_map.245
  110.8 11.0 %collective-permute-done.5 = bf16[1024,512]{1,0:T(8,128)(2,1)} collective-permute-done((bf16[1024,512]{1,0:T(8,128)(2,1)}, bf16[1024,512]{1,0:T(8,128)(2,1)}, u32[]{:S(2)}, u32[]{:S(2)}) %collective-permute-start.5) | collective-permute-done | bytes 1048608 | tf_op jit(solution)/shard_map/ppermute | solution.py:18
  125.7 3.1 convolution_convert_fusion.6
  128.8 1.6 collective-permute-start.6
  130.7 21.1 %collective-permute-done.6 = bf16[512,1024]{1,0:T(8,128)(2,1)} collective-permute-done((bf16[512,1024]{1,0:T(8,128)(2,1)}, bf16[512,1024]{1,0:T(8,128)(2,1)}, u32[]{:S(2)}, u32[]{:S(2)}) %collective-permute-start.6) | collective-permute-done | bytes 1048608 | tf_op jit(solution)/shard_map/ppermute | solution.py:24
  151.8 2.4 fusion.120
  156.9 8.4 %multiply_convert_fusion = (bf16[512,2048]{1,0:T(8,128)(2,1)}, f32[512,2048]{1,0:T(8,128)}) fusion(f32[2048]{0:T(1024)S(1)} %add.387, bf16[512,1024]{1,0:T(8,128)(2,1)} %add_convert_fusion.3, bf16[1024,2048]{1,0:T(8,128)(2,1)} %all-gather.10.cloned.1.call-done), kind=kOutput, calls=%fused_computation.10 | convolution fusion | flops 2157969408 | bytes 11542528 | tf_op jit(solution)/shard_map/dot_general | solution.py:314
  165.3 8.7 %convert_reduce_fusion = (f32[2048]{0:T(1024)S(1)}, bf16[512,2048]{1,0:T(8,128)(2,1)S(1)}) fusion(f32[512,2048]{1,0:T(8,128)} %get-tuple-element.160, f32[2048]{0:T(1024)S(1)} %add.387, bf16[2048,1024]{1,0:T(8,128)(2,1)} %all-gather.12.cloned.1.call-done, bf16[1,512,1024]{2,1,0:T(8,128)(2,1)} %param.27), kind=kOutput, calls=%fused_computation.9 | convolution fusion | flops 2171598848 | bytes 11550720 | tf_op jit(solution)/shard_map/td,fd->tf/dot_general | solution.py:321
  174.0 2.4 convolution_convert_fusion.8
  176.3 1.6 collective-permute-start.7
  178.0 1.9 convolution_convert_fusion.2
  179.9 1.7 convolution_convert_fusion.3
  182.1 1.8 convolution_convert_fusion
  183.8 1.8 convolution_convert_fusion.1
  187.2 11.0 %collective-permute-done.7 = bf16[512,1024]{1,0:T(8,128)(2,1)S(1)} collective-permute-done((bf16[512,1024]{1,0:T(8,128)(2,1)S(1)}, bf16[512,1024]{1,0:T(8,128)(2,1)S(1)}, u32[]{:S(2)}, u32[]{:S(2)}) %collective-permute-start.7) | collective-permute-done | bytes 1048608 | tf_op jit(solution)/shard_map/ppermute | solution.py:24
  201.6 6.6 %shard_map.249 = (f32[512,512]{1,0:T(8,128)S(1)}, f32[512,512]{1,0:T(8,128)S(1)}, f32[512,512]{1,0:T(8,128)S(1)}) custom-call(s32[1]{0:T(128)} %bitcast.1.refs_0_, bf16[512,512]{1,0:T(8,128)(2,1)S(1)} %copy-done.9, bf16[512,512]{1,0:T(8,128)(2,1)S(1)} %fusion.61.k_ref.refs_2_, bf16[512,512]{1,0:T(8,128)(2,1)S(1)} %fusion.46.v_ref.refs_3_, ...), custom_call_target="tpu_custom_call" | custom-call | flops 1342177280 | bytes 6291456 | tf_op jit(solution)/shard_map/pallas_call | solution.py:207
  214.2 2.4 convolution_convert_fusion.7
  217.4 2.5 collective-permute-start.28
  220.4 4.9 collective-permute-done.28
  226.7 10.4 %collective-permute-start.29 = (bf16[256,256]{1,0:T(8,128)(2,1)S(1)}, bf16[256,256]{1,0:T(8,128)(2,1)S(1)}, u32[]{:S(2)}, u32[]{:S(2)}) collective-permute-start(bf16[256,256]{1,0:T(8,128)(2,1)S(1)} %select_convert_fusion.2), channel_id=1, source_target_pairs={{0,2},{6,4},{1,3},{7,5},{8,10},{14,12},{9,11},{15,13},{16,18},{22,... | collective-permute-start | bytes 393224 | tf_op jit(solution)/shard_map/ppermute | solution.py:89
  237.2 2.0 add_convert_fusion.1
  239.7 1.7 collective-permute-start.37
  242.3 2.0 add_convert_fusion
  246.4 42.9 %collective-permute-done.31 = bf16[256,256]{1,0:T(8,128)(2,1)S(1)} collective-permute-done((bf16[256,256]{1,0:T(8,128)(2,1)S(1)}, bf16[256,256]{1,0:T(8,128)(2,1)S(1)}, u32[]{:S(2)}, u32[]{:S(2)}) %collective-permute-start.31) | collective-permute-done | bytes 131104 | tf_op jit(solution)/shard_map/ppermute | solution.py:89
  289.3 1.5 collective-permute-start.8
  294.7 1.7 convert_add_fusion.2
  296.5 4.6 collective-permute-start.38
  301.1 10.1 %collective-permute-done.46 = bf16[2048,256]{1,0:T(8,128)(2,1)S(1)} collective-permute-done((bf16[2048,256]{1,0:T(8,128)(2,1)S(1)}, bf16[2048,256]{1,0:T(8,128)(2,1)S(1)}, u32[]{:S(2)}, u32[]{:S(2)}) %collective-permute-start.46) | collective-permute-done | bytes 1048608 | tf_op jit(solution)/shard_map/ppermute | solution.py:31
  312.2 15.8 %collective-permute-start.47 = (bf16[1024,256]{1,0:T(8,128)(2,1)S(1)}, bf16[1024,256]{1,0:T(8,128)(2,1)S(1)}, u32[]{:S(2)}, u32[]{:S(2)}) collective-permute-start(bf16[1024,256]{1,0:T(8,128)(2,1)S(1)} %select_convert_fusion), channel_id=1, source_target_pairs={{0,2},{6,4},{1,3},{7,5},{8,10},{14,12},{9,11},{15,13},{16,18},{22,... | collective-permute-start | bytes 1572872 | tf_op jit(solution)/shard_map/ppermute | solution.py:89
  330.6 4.3 collective-permute-done.34
  342.2 28.9 %collective-permute-done.40 = bf16[128,2048]{1,0:T(8,128)(2,1)S(1)} collective-permute-done((bf16[128,2048]{1,0:T(8,128)(2,1)S(1)}, bf16[128,2048]{1,0:T(8,128)(2,1)S(1)}, u32[]{:S(2)}, u32[]{:S(2)}) %collective-permute-start.40) | collective-permute-done | bytes 524320 | tf_op jit(solution)/shard_map/ppermute | solution.py:89
  372.8 16.3 %collective-permute-done.49 = bf16[1024,256]{1,0:T(8,128)(2,1)S(1)} collective-permute-done((bf16[1024,256]{1,0:T(8,128)(2,1)S(1)}, bf16[1024,256]{1,0:T(8,128)(2,1)S(1)}, u32[]{:S(2)}, u32[]{:S(2)}) %collective-permute-start.49) | collective-permute-done | bytes 524320 | tf_op jit(solution)/shard_map/ppermute | solution.py:89
  389.3 1.7 collective-permute-start.50
  393.9 1.6 collective-permute-start.12
  396.2 1.5 convolution_convert_fusion.5
  404.3 1.5 add_convert_fusion.5
  406.1 2.7 collective-permute-done.12
  410.1 1.9 fusion.60
  412.0 14.0 %collective-permute-done.43 = bf16[128,2048]{1,0:T(8,128)(2,1)S(1)} collective-permute-done((bf16[128,2048]{1,0:T(8,128)(2,1)S(1)}, bf16[128,2048]{1,0:T(8,128)(2,1)S(1)}, u32[]{:S(2)}, u32[]{:S(2)}) %collective-permute-start.43) | collective-permute-done | bytes 524320 | tf_op jit(solution)/shard_map/ppermute | solution.py:93
  426.6 10.7 %collective-permute-done.52 = bf16[1024,256]{1,0:T(8,128)(2,1)S(1)} collective-permute-done((bf16[1024,256]{1,0:T(8,128)(2,1)S(1)}, bf16[1024,256]{1,0:T(8,128)(2,1)S(1)}, u32[]{:S(2)}, u32[]{:S(2)}) %collective-permute-start.52) | collective-permute-done | bytes 524320 | tf_op jit(solution)/shard_map/ppermute | solution.py:93
  437.4 9.8 %collective-permute-start.24 = (f32[9216]{0:T(1024)S(1)}, f32[9216]{0:T(1024)S(1)}, u32[]{:S(2)}, u32[]{:S(2)}) collective-permute-start(f32[9216]{0:T(1024)S(1)} %add.435), channel_id=1, source_target_pairs={{0,2},{2,0},{4,6},{6,4},{1,3},{3,1},{5,7},{7,5},{8,10},{10,8},{12,... | collective-permute-start | bytes 110600 | tf_op jit(solution)/shard_map/ppermute | solution.py:31
  447.2 1.6 maximum_convert_fusion
  449.2 2.1 collective-permute-start.25
  455.0 2.1 add_convert_fusion.4
  457.1 1.6 collective-permute-start.18
  458.7 2.0 collective-permute-start.17
  462.4 3.5 collective-permute-done.18
  465.9 8.3 %collective-permute-done.17 = bf16[64,1536]{1,0:T(8,128)(2,1)S(1)} collective-permute-done((bf16[64,1536]{1,0:T(8,128)(2,1)S(1)}, bf16[64,1536]{1,0:T(8,128)(2,1)S(1)}, u32[]{:S(2)}, u32[]{:S(2)}) %collective-permute-start.17) | collective-permute-done | bytes 196640 | tf_op jit(solution)/shard_map/ppermute | solution.py:68
  475.6 1.9 collective-permute-start.20
  477.5 2.9 collective-permute-start.21
  480.4 3.1 collective-permute-done.19
  483.5 6.9 %collective-permute-done.20 = bf16[64,1536]{1,0:T(8,128)(2,1)S(1)} collective-permute-done((bf16[64,1536]{1,0:T(8,128)(2,1)S(1)}, bf16[64,1536]{1,0:T(8,128)(2,1)S(1)}, u32[]{:S(2)}, u32[]{:S(2)}) %collective-permute-start.20) | collective-permute-done | bytes 196640 | tf_op jit(solution)/shard_map/ppermute | solution.py:73
  491.9 1.6 copy.61
  (299 shorter events, 75.4 us)
Async XLA Ops:
  7.3 24.3 %copy-start.12 = (bf16[1,512,1024]{2,1,0:T(8,128)(2,1)S(1)}, bf16[1,512,1024]{2,1,0:T(8,128)(2,1)}, u32[]{:S(2)}) copy-start(bf16[1,512,1024]{2,1,0:T(8,128)(2,1)} %param.14) | copy-start | bytes 3145732
  7.3 94.7 %all-gather.14.cloned.1.call-start = ((), (), s32[]{:S(2)}) async-start(), calls=%async_computation.3 | async-start | bytes 1310720 | tf_op jit(solution)/shard_map/all_gather | solution.py:249
  9.1 116.5 %all-gather.8.cloned.1.call-start = ((), (), s32[]{:S(2)}) async-start(), calls=%async_computation | async-start | bytes 1310720 | tf_op jit(solution)/shard_map/all_gather | solution.py:269
  9.9 147.0 %all-gather.10.cloned.1.call-start = ((), (), s32[]{:S(2)}) async-start(), calls=%async_computation.1 | async-start | bytes 5242880 | tf_op jit(solution)/shard_map/all_gather | solution.py:270
  10.6 154.6 %all-gather.12.cloned.1.call-start = ((), (), s32[]{:S(2)}) async-start(), calls=%async_computation.2 | async-start | bytes 5242880 | tf_op jit(solution)/shard_map/all_gather | solution.py:271
  10.7 24.2 %collective-permute-start = (bf16[2,256,512]{2,1,0:T(8,128)(2,1)S(1)}, bf16[2,256,512]{2,1,0:T(8,128)(2,1)}, u32[]{:S(2)}, u32[]{:S(2)}) collective-permute-start(bf16[2,256,512]{2,1,0:T(8,128)(2,1)S(1)} %slice_bitcast_fusion.1), channel_id=1, source_target_pairs={{0,8},{8,0},{16,24},{24,16},{1,9},{9,1},{17,25},{25,17},{2,10},{10... | collective-permute-start | bytes 1572872 | tf_op jit(solution)/shard_map/ppermute | solution.py:31
  11.2 23.3 %collective-permute-start.1 = (bf16[2,256,512]{2,1,0:T(8,128)(2,1)S(1)}, bf16[2,256,512]{2,1,0:T(8,128)(2,1)S(1)}, u32[]{:S(2)}, u32[]{:S(2)}) collective-permute-start(bf16[2,256,512]{2,1,0:T(8,128)(2,1)S(1)} %slice_bitcast_fusion.1), channel_id=1, source_target_pairs={{0,16},{8,24},{16,0},{24,8},{1,17},{9,25},{17,1},{25,9},{2,18},{10... | collective-permute-start | bytes 1572872 | tf_op jit(solution)/shard_map/ppermute | solution.py:31
  34.5 4.9 collective-permute-start.2
  42.3 27.4 %collective-permute-start.3 = (bf16[1024,512]{1,0:T(8,128)(2,1)}, bf16[1024,512]{1,0:T(8,128)(2,1)S(1)}, u32[]{:S(2)}, u32[]{:S(2)}) collective-permute-start(bf16[1024,512]{1,0:T(8,128)(2,1)} %pad_maximum_fusion.1), channel_id=1, source_target_pairs={{0,2},{2,4},{4,6},{1,3},{3,5},{5,7},{8,10},{10,12},{12,14},{9,11},... | collective-permute-start | bytes 3145736 | tf_op jit(solution)/shard_map/ppermute | solution.py:18
  69.6 26.3 %copy-start.25 = (bf16[1024,512]{1,0:T(8,128)(2,1)}, bf16[1024,512]{1,0:T(8,128)(2,1)S(1)}, u32[]{:S(2)}) copy-start(bf16[1024,512]{1,0:T(8,128)(2,1)S(1)} %collective-permute-done.3) | copy-start | bytes 3145732
  69.6 26.3 %collective-permute-start.4 = (bf16[1024,512]{1,0:T(8,128)(2,1)S(1)}, bf16[1024,512]{1,0:T(8,128)(2,1)}, u32[]{:S(2)}, u32[]{:S(2)}) collective-permute-start(bf16[1024,512]{1,0:T(8,128)(2,1)S(1)} %collective-permute-done.3), channel_id=1, source_target_pairs={{0,2},{2,4},{4,6},{1,3},{3,5},{5,7},{8,10},{10,12},{12,14},{9,11},... | collective-permute-start | bytes 3145736 | tf_op jit(solution)/shard_map/ppermute | solution.py:18
  96.0 25.9 %collective-permute-start.5 = (bf16[1024,512]{1,0:T(8,128)(2,1)}, bf16[1024,512]{1,0:T(8,128)(2,1)}, u32[]{:S(2)}, u32[]{:S(2)}) collective-permute-start(bf16[1024,512]{1,0:T(8,128)(2,1)} %collective-permute-done.4), channel_id=1, source_target_pairs={{0,2},{2,4},{4,6},{1,3},{3,5},{5,7},{8,10},{10,12},{12,14},{9,11},... | collective-permute-start | bytes 3145736 | tf_op jit(solution)/shard_map/ppermute | solution.py:18
  104.3 18.9 %copy-start.8 = (bf16[512,512]{1,0:T(8,128)(2,1)}, bf16[512,512]{1,0:T(8,128)(2,1)S(1)}, u32[]{:S(2)}) copy-start(bf16[512,512]{1,0:T(8,128)(2,1)S(1)} %fusion.40.q_ref.refs_1_) | copy-start | bytes 1572868
  110.5 12.6 %copy-start = (bf16[512,512]{1,0:T(8,128)(2,1)}, bf16[512,512]{1,0:T(8,128)(2,1)S(1)}, u32[]{:S(2)}) copy-start(bf16[512,512]{1,0:T(8,128)(2,1)S(1)} %get-tuple-element.134.refs_3_) | copy-start | bytes 1572868
  110.6 12.6 %copy-start.2 = (bf16[512,512]{1,0:T(8,128)(2,1)}, bf16[512,512]{1,0:T(8,128)(2,1)S(1)}, u32[]{:S(2)}) copy-start(bf16[512,512]{1,0:T(8,128)(2,1)S(1)} %get-tuple-element.135.refs_2_) | copy-start | bytes 1572868
  128.8 23.0 %collective-permute-start.6 = (bf16[512,1024]{1,0:T(8,128)(2,1)}, bf16[512,1024]{1,0:T(8,128)(2,1)}, u32[]{:S(2)}, u32[]{:S(2)}) collective-permute-start(bf16[512,1024]{1,0:T(8,128)(2,1)} %convolution_convert_fusion.6), channel_id=1, source_target_pairs={{0,1},{1,0},{2,3},{3,2},{4,5},{5,4},{6,7},{7,6},{8,9},{9,8},{10,11... | collective-permute-start | bytes 3145736 | tf_op jit(solution)/shard_map/ppermute | solution.py:24
  165.3 8.7 %copy-start.35 = (bf16[1024,2048]{1,0:T(8,128)(2,1)S(1)}, bf16[1024,2048]{1,0:T(8,128)(2,1)}, u32[]{:S(2)}) copy-start(bf16[1024,2048]{1,0:T(8,128)(2,1)} %all-gather.10.cloned.1.call-done) | copy-start | bytes 12582916
  176.3 21.8 %collective-permute-start.7 = (bf16[512,1024]{1,0:T(8,128)(2,1)S(1)}, bf16[512,1024]{1,0:T(8,128)(2,1)S(1)}, u32[]{:S(2)}, u32[]{:S(2)}) collective-permute-start(bf16[512,1024]{1,0:T(8,128)(2,1)S(1)} %convolution_convert_fusion.8), channel_id=1, source_target_pairs={{0,1},{1,0},{2,3},{3,2},{4,5},{5,4},{6,7},{7,6},{8,9},{9,8},{10,11... | collective-permute-start | bytes 3145736 | tf_op jit(solution)/shard_map/ppermute | solution.py:24
  179.8 46.9 %collective-permute-start.36 = (bf16[256,2048]{1,0:T(8,128)(2,1)}, bf16[256,2048]{1,0:T(8,128)(2,1)}, u32[]{:S(2)}, u32[]{:S(2)}) collective-permute-start(bf16[256,2048]{1,0:T(8,128)(2,1)} %convolution_convert_fusion.2), channel_id=1, source_target_pairs={{0,8},{8,0},{16,24},{24,16},{1,9},{9,1},{17,25},{25,17},{2,10},{10... | collective-permute-start | bytes 3145736 | tf_op jit(solution)/shard_map/ppermute | solution.py:31
  181.6 110.3 %collective-permute-start.35 = (bf16[256,2048]{1,0:T(8,128)(2,1)}, bf16[256,2048]{1,0:T(8,128)(2,1)}, u32[]{:S(2)}, u32[]{:S(2)}) collective-permute-start(bf16[256,2048]{1,0:T(8,128)(2,1)} %convolution_convert_fusion.3), channel_id=1, source_target_pairs={{0,8},{8,0},{16,24},{24,16},{1,9},{9,1},{17,25},{25,17},{2,10},{10... | collective-permute-start | bytes 3145736 | tf_op jit(solution)/shard_map/ppermute | solution.py:31
  183.8 57.6 %collective-permute-start.45 = (bf16[2048,256]{1,0:T(8,128)(2,1)}, bf16[2048,256]{1,0:T(8,128)(2,1)}, u32[]{:S(2)}, u32[]{:S(2)}) collective-permute-start(bf16[2048,256]{1,0:T(8,128)(2,1)} %convolution_convert_fusion), channel_id=1, source_target_pairs={{0,8},{8,0},{16,24},{24,16},{1,9},{9,1},{17,25},{25,17},{2,10},{10... | collective-permute-start | bytes 3145736 | tf_op jit(solution)/shard_map/ppermute | solution.py:31
  186.4 11.8 %copy-start.11 = (f32[512,1024]{1,0:T(8,128)S(1)}, f32[512,1024]{1,0:T(8,128)}, u32[]{:S(2)}) copy-start(f32[512,1024]{1,0:T(8,128)} %copy-done.10) | copy-start | bytes 6291460
  212.4 4.6 collective-permute-start.27
  212.5 7.8 %collective-permute-start.26 = (bf16[512,256]{1,0:T(8,128)(2,1)S(1)}, bf16[512,256]{1,0:T(8,128)(2,1)S(1)}, u32[]{:S(2)}, u32[]{:S(2)}) collective-permute-start(bf16[512,256]{1,0:T(8,128)(2,1)S(1)} %convolution_convert_fusion.11), channel_id=1, source_target_pairs={{0,8},{8,0},{16,24},{24,16},{1,9},{9,1},{17,25},{25,17},{2,10},{10... | collective-permute-start | bytes 786440 | tf_op jit(solution)/shard_map/ppermute | solution.py:31
  217.4 7.9 %collective-permute-start.28 = (bf16[512,256]{1,0:T(8,128)(2,1)S(1)}, bf16[512,256]{1,0:T(8,128)(2,1)S(1)}, u32[]{:S(2)}, u32[]{:S(2)}) collective-permute-start(bf16[512,256]{1,0:T(8,128)(2,1)S(1)} %add_convert_fusion.13), channel_id=1, source_target_pairs={{0,16},{8,24},{16,0},{24,8},{1,17},{9,25},{17,1},{25,9},{2,18},{10... | collective-permute-start | bytes 786440 | tf_op jit(solution)/shard_map/ppermute | solution.py:31
  220.3 76.2 %collective-permute-start.44 = (bf16[2048,256]{1,0:T(8,128)(2,1)S(1)}, bf16[2048,256]{1,0:T(8,128)(2,1)S(1)}, u32[]{:S(2)}, u32[]{:S(2)}) collective-permute-start(bf16[2048,256]{1,0:T(8,128)(2,1)S(1)} %copy-done.37), channel_id=1, source_target_pairs={{0,8},{8,0},{16,24},{24,16},{1,9},{9,1},{17,25},{25,17},{2,10},{10... | collective-permute-start | bytes 3145736 | tf_op jit(solution)/shard_map/ppermute | solution.py:31
  225.3 65.6 %collective-permute-start.9 = (bf16[1024,512]{1,0:T(8,128)(2,1)S(1)}, bf16[1024,512]{1,0:T(8,128)(2,1)S(1)}, u32[]{:S(2)}, u32[]{:S(2)}) collective-permute-start(bf16[1024,512]{1,0:T(8,128)(2,1)S(1)} %pad_maximum_fusion.2), channel_id=1, source_target_pairs={{2,0},{4,2},{6,4},{3,1},{5,3},{7,5},{10,8},{12,10},{14,12},{11,9},... | collective-permute-start | bytes 3145736 | tf_op jit(solution)/shard_map/ppermute | solution.py:18
  226.7 12.9 %collective-permute-start.29 = (bf16[256,256]{1,0:T(8,128)(2,1)S(1)}, bf16[256,256]{1,0:T(8,128)(2,1)S(1)}, u32[]{:S(2)}, u32[]{:S(2)}) collective-permute-start(bf16[256,256]{1,0:T(8,128)(2,1)S(1)} %select_convert_fusion.2), channel_id=1, source_target_pairs={{0,2},{6,4},{1,3},{7,5},{8,10},{14,12},{9,11},{15,13},{16,18},{22,... | collective-permute-start | bytes 393224 | tf_op jit(solution)/shard_map/ppermute | solution.py:89
  239.7 53.7 %collective-permute-start.37 = (bf16[256,2048]{1,0:T(8,128)(2,1)S(1)}, bf16[256,2048]{1,0:T(8,128)(2,1)S(1)}, u32[]{:S(2)}, u32[]{:S(2)}) collective-permute-start(bf16[256,2048]{1,0:T(8,128)(2,1)S(1)} %add_convert_fusion.1), channel_id=1, source_target_pairs={{0,16},{8,24},{16,0},{24,8},{1,17},{9,25},{17,1},{25,9},{2,18},{10... | collective-permute-start | bytes 3145736 | tf_op jit(solution)/shard_map/ppermute | solution.py:31
  241.5 2.8 collective-permute-start.30
  244.3 45.0 %collective-permute-start.31 = (bf16[256,256]{1,0:T(8,128)(2,1)S(1)}, bf16[256,256]{1,0:T(8,128)(2,1)S(1)}, u32[]{:S(2)}, u32[]{:S(2)}) collective-permute-start(bf16[256,256]{1,0:T(8,128)(2,1)S(1)} %add_convert_fusion.15), channel_id=1, source_target_pairs={{4,6},{2,0},{5,7},{3,1},{12,14},{10,8},{13,15},{11,9},{20,22},{18,... | collective-permute-start | bytes 393224 | tf_op jit(solution)/shard_map/ppermute | solution.py:89
  289.3 40.9 %collective-permute-start.8 = (bf16[512,1024]{1,0:T(8,128)(2,1)S(1)}, bf16[512,1024]{1,0:T(8,128)(2,1)S(1)}, u32[]{:S(2)}, u32[]{:S(2)}) collective-permute-start(bf16[512,1024]{1,0:T(8,128)(2,1)S(1)} %convolution_convert_fusion.7), channel_id=1, source_target_pairs={{0,1},{1,0},{2,3},{3,2},{4,5},{5,4},{6,7},{7,6},{8,9},{9,8},{10,11... | collective-permute-start | bytes 3145736 | tf_op jit(solution)/shard_map/ppermute | solution.py:24
  290.9 20.2 %collective-permute-start.46 = (bf16[2048,256]{1,0:T(8,128)(2,1)S(1)}, bf16[2048,256]{1,0:T(8,128)(2,1)S(1)}, u32[]{:S(2)}, u32[]{:S(2)}) collective-permute-start(bf16[2048,256]{1,0:T(8,128)(2,1)S(1)} %add_convert_fusion), channel_id=1, source_target_pairs={{0,16},{8,24},{16,0},{24,8},{1,17},{9,25},{17,1},{25,9},{2,18},{10... | collective-permute-start | bytes 3145736 | tf_op jit(solution)/shard_map/ppermute | solution.py:31
  291.9 19.5 %collective-permute-start.32 = (bf16[256,256]{1,0:T(8,128)(2,1)S(1)}, bf16[256,256]{1,0:T(8,128)(2,1)S(1)}, u32[]{:S(2)}, u32[]{:S(2)}) collective-permute-start(bf16[256,256]{1,0:T(8,128)(2,1)S(1)} %add_convert_fusion.14), channel_id=1, source_target_pairs={{0,2},{6,4},{1,3},{7,5},{8,10},{14,12},{9,11},{15,13},{16,18},{22,... | collective-permute-start | bytes 393224 | tf_op jit(solution)/shard_map/ppermute | solution.py:93
  293.4 44.8 %collective-permute-start.10 = (bf16[1024,512]{1,0:T(8,128)(2,1)S(1)}, bf16[1024,512]{1,0:T(8,128)(2,1)S(1)}, u32[]{:S(2)}, u32[]{:S(2)}) collective-permute-start(bf16[1024,512]{1,0:T(8,128)(2,1)S(1)} %fusion.31), channel_id=1, source_target_pairs={{2,0},{4,2},{6,4},{3,1},{5,3},{7,5},{10,8},{12,10},{14,12},{11,9},... | collective-permute-start | bytes 3145736 | tf_op jit(solution)/shard_map/ppermute | solution.py:18
  296.5 32.8 %collective-permute-start.38 = (bf16[128,2048]{1,0:T(8,128)(2,1)S(1)}, bf16[128,2048]{1,0:T(8,128)(2,1)S(1)}, u32[]{:S(2)}, u32[]{:S(2)}) collective-permute-start(bf16[128,2048]{1,0:T(8,128)(2,1)S(1)} %select_convert_fusion.1), channel_id=1, source_target_pairs={{0,2},{6,4},{1,3},{7,5},{8,10},{14,12},{9,11},{15,13},{16,18},{22,... | collective-permute-start | bytes 1572872 | tf_op jit(solution)/shard_map/ppermute | solution.py:89
  311.4 16.6 %collective-permute-start.33 = (bf16[256,256]{1,0:T(8,128)(2,1)S(1)}, bf16[256,256]{1,0:T(8,128)(2,1)S(1)}, u32[]{:S(2)}, u32[]{:S(2)}) collective-permute-start(bf16[256,256]{1,0:T(8,128)(2,1)S(1)} %collective-permute-done.32), channel_id=1, source_target_pairs={{2,4},{4,2},{3,5},{5,3},{10,12},{12,10},{11,13},{13,11},{18,20},{2... | collective-permute-start | bytes 393224 | tf_op jit(solution)/shard_map/ppermute | solution.py:93
  312.2 23.6 %collective-permute-start.47 = (bf16[1024,256]{1,0:T(8,128)(2,1)S(1)}, bf16[1024,256]{1,0:T(8,128)(2,1)S(1)}, u32[]{:S(2)}, u32[]{:S(2)}) collective-permute-start(bf16[1024,256]{1,0:T(8,128)(2,1)S(1)} %select_convert_fusion), channel_id=1, source_target_pairs={{0,2},{6,4},{1,3},{7,5},{8,10},{14,12},{9,11},{15,13},{16,18},{22,... | collective-permute-start | bytes 1572872 | tf_op jit(solution)/shard_map/ppermute | solution.py:89
  328.0 6.9 %collective-permute-start.34 = (bf16[256,256]{1,0:T(8,128)(2,1)S(1)}, bf16[256,256]{1,0:T(8,128)(2,1)S(1)}, u32[]{:S(2)}, u32[]{:S(2)}) collective-permute-start(bf16[256,256]{1,0:T(8,128)(2,1)S(1)} %collective-permute-done.33), channel_id=1, source_target_pairs={{4,6},{2,0},{5,7},{3,1},{12,14},{10,8},{13,15},{11,9},{20,22},{18,... | collective-permute-start | bytes 393224 | tf_op jit(solution)/shard_map/ppermute | solution.py:93
  329.5 7.1 %collective-permute-start.39 = (bf16[128,2048]{1,0:T(8,128)(2,1)S(1)}, bf16[128,2048]{1,0:T(8,128)(2,1)S(1)}, u32[]{:S(2)}, u32[]{:S(2)}) collective-permute-start(bf16[128,2048]{1,0:T(8,128)(2,1)S(1)} %add_convert_fusion.11), channel_id=1, source_target_pairs={{2,4},{4,2},{3,5},{5,3},{10,12},{12,10},{11,13},{13,11},{18,20},{2... | collective-permute-start | bytes 1572872 | tf_op jit(solution)/shard_map/ppermute | solution.py:89
  336.0 3.9 collective-permute-start.48
  336.9 34.2 %collective-permute-start.40 = (bf16[128,2048]{1,0:T(8,128)(2,1)S(1)}, bf16[128,2048]{1,0:T(8,128)(2,1)S(1)}, u32[]{:S(2)}, u32[]{:S(2)}) collective-permute-start(bf16[128,2048]{1,0:T(8,128)(2,1)S(1)} %add_convert_fusion.10), channel_id=1, source_target_pairs={{4,6},{2,0},{5,7},{3,1},{12,14},{10,8},{13,15},{11,9},{20,22},{18,... | collective-permute-start | bytes 1572872 | tf_op jit(solution)/shard_map/ppermute | solution.py:89
  338.6 52.4 %collective-permute-start.11 = (bf16[1024,512]{1,0:T(8,128)(2,1)S(1)}, bf16[1024,512]{1,0:T(8,128)(2,1)S(1)}, u32[]{:S(2)}, u32[]{:S(2)}) collective-permute-start(bf16[1024,512]{1,0:T(8,128)(2,1)S(1)} %fusion.30), channel_id=1, source_target_pairs={{2,0},{4,2},{6,4},{3,1},{5,3},{7,5},{10,8},{12,10},{14,12},{11,9},... | collective-permute-start | bytes 3145736 | tf_op jit(solution)/shard_map/ppermute | solution.py:18
  340.1 49.0 %collective-permute-start.49 = (bf16[1024,256]{1,0:T(8,128)(2,1)S(1)}, bf16[1024,256]{1,0:T(8,128)(2,1)S(1)}, u32[]{:S(2)}, u32[]{:S(2)}) collective-permute-start(bf16[1024,256]{1,0:T(8,128)(2,1)S(1)} %add_convert_fusion.7), channel_id=1, source_target_pairs={{4,6},{2,0},{5,7},{3,1},{12,14},{10,8},{13,15},{11,9},{20,22},{18,... | collective-permute-start | bytes 1572872 | tf_op jit(solution)/shard_map/ppermute | solution.py:89
  371.3 27.1 %collective-permute-start.41 = (bf16[128,2048]{1,0:T(8,128)(2,1)S(1)}, bf16[128,2048]{1,0:T(8,128)(2,1)S(1)}, u32[]{:S(2)}, u32[]{:S(2)}) collective-permute-start(bf16[128,2048]{1,0:T(8,128)(2,1)S(1)} %add_convert_fusion.9), channel_id=1, source_target_pairs={{0,2},{6,4},{1,3},{7,5},{8,10},{14,12},{9,11},{15,13},{16,18},{22,... | collective-permute-start | bytes 1572872 | tf_op jit(solution)/shard_map/ppermute | solution.py:93
  389.3 9.8 %collective-permute-start.50 = (bf16[1024,256]{1,0:T(8,128)(2,1)S(1)}, bf16[1024,256]{1,0:T(8,128)(2,1)S(1)}, u32[]{:S(2)}, u32[]{:S(2)}) collective-permute-start(bf16[1024,256]{1,0:T(8,128)(2,1)S(1)} %add_convert_fusion.6), channel_id=1, source_target_pairs={{0,2},{6,4},{1,3},{7,5},{8,10},{14,12},{9,11},{15,13},{16,18},{22,... | collective-permute-start | bytes 1572872 | tf_op jit(solution)/shard_map/ppermute | solution.py:93
  393.9 14.9 %collective-permute-start.12 = (bf16[512,1024]{1,0:T(8,128)(2,1)S(1)}, bf16[512,1024]{1,0:T(8,128)(2,1)S(1)}, u32[]{:S(2)}, u32[]{:S(2)}) collective-permute-start(bf16[512,1024]{1,0:T(8,128)(2,1)S(1)} %fusion.32), channel_id=1, source_target_pairs={{0,1},{1,0},{2,3},{3,2},{4,5},{5,4},{6,7},{7,6},{8,9},{9,8},{10,11... | collective-permute-start | bytes 3145736 | tf_op jit(solution)/shard_map/ppermute | solution.py:24
  396.2 8.1 %collective-permute-start.14 = (bf16[256,1536]{1,0:T(8,128)(2,1)S(1)}, bf16[256,1536]{1,0:T(8,128)(2,1)S(1)}, u32[]{:S(2)}, u32[]{:S(2)}) collective-permute-start(bf16[256,1536]{1,0:T(8,128)(2,1)S(1)} %convolution_convert_fusion.4), channel_id=1, source_target_pairs={{0,8},{8,0},{16,24},{24,16},{1,9},{9,1},{17,25},{25,17},{2,10},{10... | collective-permute-start | bytes 2359304 | tf_op jit(solution)/shard_map/ppermute | solution.py:31
  397.8 57.2 %collective-permute-start.13 = (bf16[256,1536]{1,0:T(8,128)(2,1)}, bf16[256,1536]{1,0:T(8,128)(2,1)}, u32[]{:S(2)}, u32[]{:S(2)}) collective-permute-start(bf16[256,1536]{1,0:T(8,128)(2,1)} %convolution_convert_fusion.5), channel_id=1, source_target_pairs={{0,8},{8,0},{16,24},{24,16},{1,9},{9,1},{17,25},{25,17},{2,10},{10... | collective-permute-start | bytes 2359304 | tf_op jit(solution)/shard_map/ppermute | solution.py:31
  398.4 3.1 collective-permute-start.42
  399.1 3.8 collective-permute-start.51
  401.5 24.5 %collective-permute-start.43 = (bf16[128,2048]{1,0:T(8,128)(2,1)S(1)}, bf16[128,2048]{1,0:T(8,128)(2,1)S(1)}, u32[]{:S(2)}, u32[]{:S(2)}) collective-permute-start(bf16[128,2048]{1,0:T(8,128)(2,1)S(1)} %collective-permute-done.42), channel_id=1, source_target_pairs={{4,6},{2,0},{5,7},{3,1},{12,14},{10,8},{13,15},{11,9},{20,22},{18,... | collective-permute-start | bytes 1572872 | tf_op jit(solution)/shard_map/ppermute | solution.py:93
  403.0 34.3 %collective-permute-start.52 = (bf16[1024,256]{1,0:T(8,128)(2,1)S(1)}, bf16[1024,256]{1,0:T(8,128)(2,1)S(1)}, u32[]{:S(2)}, u32[]{:S(2)}) collective-permute-start(bf16[1024,256]{1,0:T(8,128)(2,1)S(1)} %collective-permute-done.51), channel_id=1, source_target_pairs={{4,6},{2,0},{5,7},{3,1},{12,14},{10,8},{13,15},{11,9},{20,22},{18,... | collective-permute-start | bytes 1572872 | tf_op jit(solution)/shard_map/ppermute | solution.py:93
  405.8 49.2 %collective-permute-start.15 = (bf16[256,1536]{1,0:T(8,128)(2,1)}, bf16[256,1536]{1,0:T(8,128)(2,1)}, u32[]{:S(2)}, u32[]{:S(2)}) collective-permute-start(bf16[256,1536]{1,0:T(8,128)(2,1)} %add_convert_fusion.5), channel_id=1, source_target_pairs={{0,16},{8,24},{16,0},{24,8},{1,17},{9,25},{17,1},{25,9},{2,18},{10... | collective-permute-start | bytes 2359304 | tf_op jit(solution)/shard_map/ppermute | solution.py:31
  410.0 16.1 %collective-permute-start.22 = (f32[9216]{0:T(1024)S(1)}, f32[9216]{0:T(1024)S(1)}, u32[]{:S(2)}, u32[]{:S(2)}) collective-permute-start(f32[9216]{0:T(1024)S(1)} %constant_dynamic-update-slice_fusion), channel_id=1, source_target_pairs={{0,8},{8,0},{16,24},{24,16},{1,9},{9,1},{17,25},{25,17},{2,10},{10... | collective-permute-start | bytes 110600 | tf_op jit(solution)/shard_map/ppermute | solution.py:31
  426.2 11.2 %collective-permute-start.23 = (f32[9216]{0:T(1024)S(1)}, f32[9216]{0:T(1024)S(1)}, u32[]{:S(2)}, u32[]{:S(2)}) collective-permute-start(f32[9216]{0:T(1024)S(1)} %add.434), channel_id=1, source_target_pairs={{0,16},{8,24},{16,0},{24,8},{1,17},{9,25},{17,1},{25,9},{2,18},{10... | collective-permute-start | bytes 110600 | tf_op jit(solution)/shard_map/ppermute | solution.py:31
  437.4 11.7 %collective-permute-start.24 = (f32[9216]{0:T(1024)S(1)}, f32[9216]{0:T(1024)S(1)}, u32[]{:S(2)}, u32[]{:S(2)}) collective-permute-start(f32[9216]{0:T(1024)S(1)} %add.435), channel_id=1, source_target_pairs={{0,2},{2,0},{4,6},{6,4},{1,3},{3,1},{5,7},{7,5},{8,10},{10,8},{12,... | collective-permute-start | bytes 110600 | tf_op jit(solution)/shard_map/ppermute | solution.py:31
  449.2 4.9 collective-permute-start.25
  457.1 8.8 %collective-permute-start.18 = (bf16[64,1536]{1,0:T(8,128)(2,1)S(1)}, bf16[64,1536]{1,0:T(8,128)(2,1)S(1)}, u32[]{:S(2)}, u32[]{:S(2)}) collective-permute-start(bf16[64,1536]{1,0:T(8,128)(2,1)S(1)} %get-tuple-element.139), channel_id=1, source_target_pairs={{0,6},{2,0},{4,2},{6,4},{1,7},{3,1},{5,3},{7,5},{8,14},{10,8},{12,... | collective-permute-start | bytes 589832 | tf_op jit(solution)/shard_map/ppermute | solution.py:68
  458.7 15.5 %collective-permute-start.17 = (bf16[64,1536]{1,0:T(8,128)(2,1)S(1)}, bf16[64,1536]{1,0:T(8,128)(2,1)S(1)}, u32[]{:S(2)}, u32[]{:S(2)}) collective-permute-start(bf16[64,1536]{1,0:T(8,128)(2,1)S(1)} %get-tuple-element.140), channel_id=1, source_target_pairs={{0,4},{2,6},{4,0},{6,2},{1,5},{3,7},{5,1},{7,3},{8,12},{10,14},{12... | collective-permute-start | bytes 589832 | tf_op jit(solution)/shard_map/ppermute | solution.py:68
  460.6 13.5 %collective-permute-start.16 = (bf16[64,1536]{1,0:T(8,128)(2,1)S(1)}, bf16[64,1536]{1,0:T(8,128)(2,1)S(1)}, u32[]{:S(2)}, u32[]{:S(2)}) collective-permute-start(bf16[64,1536]{1,0:T(8,128)(2,1)S(1)} %get-tuple-element.138), channel_id=1, source_target_pairs={{0,2},{2,4},{4,6},{6,0},{1,3},{3,5},{5,7},{7,1},{8,10},{10,12},{12... | collective-permute-start | bytes 589832 | tf_op jit(solution)/shard_map/ppermute | solution.py:68
  474.3 9.2 %collective-permute-start.19 = (bf16[64,1536]{1,0:T(8,128)(2,1)S(1)}, bf16[64,1536]{1,0:T(8,128)(2,1)S(1)}, u32[]{:S(2)}, u32[]{:S(2)}) collective-permute-start(bf16[64,1536]{1,0:T(8,128)(2,1)S(1)} %get-tuple-element.124), channel_id=1, source_target_pairs={{0,2},{2,4},{4,6},{6,0},{1,3},{3,5},{5,7},{7,1},{8,10},{10,12},{12... | collective-permute-start | bytes 589832 | tf_op jit(solution)/shard_map/ppermute | solution.py:73
  475.6 14.9 %collective-permute-start.20 = (bf16[64,1536]{1,0:T(8,128)(2,1)S(1)}, bf16[64,1536]{1,0:T(8,128)(2,1)S(1)}, u32[]{:S(2)}, u32[]{:S(2)}) collective-permute-start(bf16[64,1536]{1,0:T(8,128)(2,1)S(1)} %get-tuple-element.124), channel_id=1, source_target_pairs={{0,4},{2,6},{4,0},{6,2},{1,5},{3,7},{5,1},{7,3},{8,12},{10,14},{12... | collective-permute-start | bytes 589832 | tf_op jit(solution)/shard_map/ppermute | solution.py:73
  477.5 13.0 %collective-permute-start.21 = (bf16[64,1536]{1,0:T(8,128)(2,1)S(1)}, bf16[64,1536]{1,0:T(8,128)(2,1)S(1)}, u32[]{:S(2)}, u32[]{:S(2)}) collective-permute-start(bf16[64,1536]{1,0:T(8,128)(2,1)S(1)} %get-tuple-element.124), channel_id=1, source_target_pairs={{0,6},{2,0},{4,2},{6,4},{1,7},{3,1},{5,3},{7,5},{8,14},{10,8},{12,... | collective-permute-start | bytes 589832 | tf_op jit(solution)/shard_map/ppermute | solution.py:73
  (31 other events, 115.3 us)
Sparse Core Ops, SparseCore 0:
  10.3 23.3 all-gather.13
  35.2 18.2 all-gather.7
  55.1 34.4 all-gather.9
  91.0 35.0 all-gather.11

commit v4 on v2

--- a/solution.py
+++ b/solution.py
@@ -304,7 +304,6 @@
     )
     later_act, grad_normed_two = lax.optimization_barrier((hidden_act, grad_normed_two))
     mlp_part = pair_sum(jnp.dot(later_act, mlp_down, preferred_element_type=F32))
-    output = (resid + mlp_part + bias_down).astype(BF16).reshape(shape)
 
     grad_down = scatter_product(
         grad_rows,
@@ -353,6 +352,8 @@
         block = block.astype(BF16)
         if distance > 0:
             arrived = ahead(block, "ctx", -1)
+    mlp_part, block = lax.optimization_barrier((mlp_part, block))
+    output = (resid + mlp_part + bias_down).astype(BF16).reshape(shape)
     grad_mixed = jnp.concatenate([grad_query.astype(BF16), block], axis=0)
     grad_mixed = grad_mixed.reshape(3, half_width, count)
     grad_bias_in = jnp.sum(grad_mixed[0::2], axis=2, dtype=F32)
@@ -371,10 +372,11 @@
     grad_inputs = grad_resid + norm_back(grad_normed_one, xhat_one, scale_one, gain_one)
     grad_inputs = grad_inputs.astype(BF16).reshape(shape)
 
-    grad_up, grad_down, grad_out = [
-        lax.psum(item.astype(BF16), "ctx").astype(F32) for item in (grad_up, grad_down, grad_out)
-    ]
-    grad_attn_in = ctx_total(grad_attn_in).reshape(-1, 3, half_width)
+    sums = [lax.psum(item.astype(BF16), "ctx") for item in (grad_up, grad_down, grad_out)]
+    grad_attn_in = ctx_total(grad_attn_in)
+    sums, grad_attn_in = lax.optimization_barrier((sums, grad_attn_in))
+    grad_up, grad_down, grad_out = [item.astype(F32) for item in sums]
+    grad_attn_in = grad_attn_in.reshape(-1, 3, half_width)
 
     grads_small = (
         grad_gain_one,

time: 490 us -> 460 us (0.939)
  waiting for transfers between devices: 271 us -> 228 us
  starting transfers between devices: 49.6 us -> 66.1 us
    psum x1, waiting for transfers between devices: 46.5 us -> 10.7 us  [local(): lax.psum(item.astype(BF16), 'ctx')]
    ppermute x6, waiting for transfers between devices: 148 us -> 116 us  [ahead(): lax.ppermute(value, axis, [(source, source + steps) for source in range(f...]
    ppermute x3, waiting for transfers between devices: 11.2 us -> 31.5 us  [ctx_total(): total = total + lax.ppermute(chunk, 'ctx', pairs).astype(F32)]
    dot_general x4, matrix products: 2.99 us -> 14.5 us  [local(): jnp.einsum('td,tf->df', part, grad_pre, preferred_element_type=F32)]
    dot_general x4, matrix products: 13.9 us -> 5.29 us  [local(): jnp.einsum('tf,td->fd', hidden_act, part, preferred_element_type=F32)]
    ppermute x3, waiting for transfers between devices: 9.27 us -> 17.8 us  [ctx_total(): other = lax.ppermute(total, 'ctx', pairs)]
    ppermute x19, starting transfers between devices: 14.6 us -> 22 us  [flipped(): lax.ppermute(value, axis, [(source, source ^ bit) for source in range(cou...]
    unnamed x123 -> x121, local copies, waits for them, and re-layouts: 10.4 us -> 9.15 us
  transfers between devices with their start and end apart: 40 -> 40, of which waited for: 19 -> 19; matrix products, arithmetic and copies ran while one was open for 19% -> 20% of each run, Pallas kernels for 3% -> 3%
where the time goes in v4:
time: 460 us; the launch traced here: 453 us
  waiting for transfers between devices  228 us (50%)
  starting transfers between devices  66.1 us (14%)
  matrix products  59.8 us (13%)
  other arithmetic  28.9 us (6%)
  local copies, waits for them, and re-layouts  25.4 us (6%)
  blocking collectives  15.6 us (3%)
  between operations  15.4 us (3%)
  Pallas kernels  13.4 us (3%)
    ppermute x6, waiting for transfers between devices, ahead(): lax.ppermute(value, axis, [(source, source + steps) for source in range(f...  116 us
    ppermute x4, waiting for transfers between devices, pair_sum(): other = lax.ppermute(low, 'tensor', [(0, 1), (1, 0)])  37.3 us
    ppermute x3, waiting for transfers between devices, ctx_total(): total = total + lax.ppermute(chunk, 'ctx', pairs).astype(F32)  31.5 us
    ppermute x19, starting transfers between devices, flipped(): lax.ppermute(value, axis, [(source, source ^ bit) for source in range(cou...  22 us
    ppermute x6, starting transfers between devices, ahead(): lax.ppermute(value, axis, [(source, source + steps) for source in range(f...  19.3 us
    ppermute x3, waiting for transfers between devices, ctx_total(): other = lax.ppermute(total, 'ctx', pairs)  17.8 us
    all_gather x1, blocking collectives, local(): lax.all_gather(jnp.concatenate([item.reshape(-1) for item in small]), 'dp')  15.6 us
    dot_general x4, matrix products, local(): jnp.einsum('td,tf->df', part, grad_pre, preferred_element_type=F32)  14.5 us
  transfers between devices with their start and end apart: 40, of which 19 were waited for; matrix products, arithmetic and copies ran while one was open for 20% of the time, Pallas kernels for 3%

profile of v4, /device:TPU:0, one launch (start us, length us, event | category | flops | bytes accessed | tf_op | source)
XLA Modules:
  0.0 452.7 jit_solution(5131343718362609093)
XLA Ops:
  7.3 1.8 slice.178
  11.2 2.6 collective-permute-start.1
  15.9 15.6 %all-gather.2 = bf16[4,1,2304]{2,1,0:T(2,128)(2,1)S(1)} all-gather(bf16[1,1,2304]{2,1,0:T(2,128)(2,1)S(1)} %reshape.268), channel_id=2, replica_groups=mesh['dp'=4,'ctx'=4,'tensor'=2] {'dp'}, dimensions={0}, use_global_device_ids=true | all-gather | bytes 23040 | tf_op jit(solution)/shard_map/all_gather | solution.py:239
  32.2 1.5 broadcast_in_dim.43
  35.0 1.9 bitcast_dynamic-update-slice_fusion.3
  37.7 1.8 copy.60
  42.3 4.3 collective-permute-start.3
  46.7 22.9 %collective-permute-done.3 = bf16[1024,512]{1,0:T(8,128)(2,1)S(1)} collective-permute-done((bf16[1024,512]{1,0:T(8,128)(2,1)}, bf16[1024,512]{1,0:T(8,128)(2,1)S(1)}, u32[]{:S(2)}, u32[]{:S(2)}) %collective-permute-start.3) | collective-permute-done | bytes 1048608 | tf_op jit(solution)/shard_map/ppermute | solution.py:18
  69.6 5.2 %collective-permute-start.4 = (bf16[1024,512]{1,0:T(8,128)(2,1)S(1)}, bf16[1024,512]{1,0:T(8,128)(2,1)}, u32[]{:S(2)}, u32[]{:S(2)}) collective-permute-start(bf16[1024,512]{1,0:T(8,128)(2,1)S(1)} %collective-permute-done.3), channel_id=1, source_target_pairs={{0,2},{2,4},{4,6},{1,3},{3,5},{5,7},{8,10},{10,12},{12,14},{9,11},... | collective-permute-start | bytes 3145736 | tf_op jit(solution)/shard_map/ppermute | solution.py:18
  74.9 21.1 %collective-permute-done.4 = bf16[1024,512]{1,0:T(8,128)(2,1)} collective-permute-done((bf16[1024,512]{1,0:T(8,128)(2,1)S(1)}, bf16[1024,512]{1,0:T(8,128)(2,1)}, u32[]{:S(2)}, u32[]{:S(2)}) %collective-permute-start.4) | collective-permute-done | bytes 1048608 | tf_op jit(solution)/shard_map/ppermute | solution.py:18
  95.9 5.5 %collective-permute-start.5 = (bf16[1024,512]{1,0:T(8,128)(2,1)}, bf16[1024,512]{1,0:T(8,128)(2,1)}, u32[]{:S(2)}, u32[]{:S(2)}) collective-permute-start(bf16[1024,512]{1,0:T(8,128)(2,1)} %collective-permute-done.4), channel_id=1, source_target_pairs={{0,2},{2,4},{4,6},{1,3},{3,5},{5,7},{8,10},{10,12},{12,14},{9,11},... | collective-permute-start | bytes 3145736 | tf_op jit(solution)/shard_map/ppermute | solution.py:18
  102.0 2.3 fusion.37.q_ref.refs_1_
  104.3 4.6 %shard_map.245 = (f32[8,1,512]{2,1,0:T(1,128)S(1)}, f32[8,1,512]{2,1,0:T(1,128)S(1)}, f32[512,512]{1,0:T(8,128)S(1)}) custom-call(bf16[512,512]{1,0:T(8,128)(2,1)S(1)} %fusion.37.q_ref.refs_1_, bf16[512,512]{1,0:T(8,128)(2,1)S(1)} %fusion.58.k_ref.refs_2_, bf16[512,512]{1,0:T(8,128)(2,1)S(1)} %fusion.43.v_ref.refs_3_), custom_call_target="tpu_custom_call" | custom-call | flops 536870912 | bytes 6291456 | tf_op jit(solution)/shard_map/pallas_call | solution.py:186
  110.9 10.9 %collective-permute-done.5 = bf16[1024,512]{1,0:T(8,128)(2,1)} collective-permute-done((bf16[1024,512]{1,0:T(8,128)(2,1)}, bf16[1024,512]{1,0:T(8,128)(2,1)}, u32[]{:S(2)}, u32[]{:S(2)}) %collective-permute-start.5) | collective-permute-done | bytes 1048608 | tf_op jit(solution)/shard_map/ppermute | solution.py:18
  125.7 3.1 convolution_convert_fusion.6
  128.7 1.6 collective-permute-start.6
  130.7 21.1 %collective-permute-done.6 = bf16[512,1024]{1,0:T(8,128)(2,1)} collective-permute-done((bf16[512,1024]{1,0:T(8,128)(2,1)}, bf16[512,1024]{1,0:T(8,128)(2,1)}, u32[]{:S(2)}, u32[]{:S(2)}) %collective-permute-start.6) | collective-permute-done | bytes 1048608 | tf_op jit(solution)/shard_map/ppermute | solution.py:24
  151.8 2.4 fusion.117
  156.9 8.4 %multiply_convert_fusion = (bf16[512,2048]{1,0:T(8,128)(2,1)}, f32[512,2048]{1,0:T(8,128)}) fusion(f32[2048]{0:T(1024)S(1)} %add.366, bf16[512,1024]{1,0:T(8,128)(2,1)} %add_convert_fusion.5, bf16[1024,2048]{1,0:T(8,128)(2,1)} %all-gather.10.cloned.1.call-done), kind=kOutput, calls=%fused_computation.10 | convolution fusion | flops 2157969408 | bytes 11542528 | tf_op jit(solution)/shard_map/dot_general | solution.py:293
  165.3 8.7 %convert_reduce_fusion = (f32[2048]{0:T(1024)S(1)}, bf16[512,2048]{1,0:T(8,128)(2,1)S(1)}) fusion(f32[512,2048]{1,0:T(8,128)} %get-tuple-element.165, f32[2048]{0:T(1024)S(1)} %add.366, bf16[2048,1024]{1,0:T(8,128)(2,1)} %all-gather.12.cloned.1.call-done, bf16[1,512,1024]{2,1,0:T(8,128)(2,1)} %param.27), kind=kOutput, calls=%fused_computation.9 | convolution fusion | flops 2171598848 | bytes 11550720 | tf_op jit(solution)/shard_map/td,fd->tf/dot_general | solution.py:300
  174.0 2.4 convolution_convert_fusion.8
  176.4 1.7 collective-permute-start.7
  178.0 12.3 %convolution_convert_fusion.2 = bf16[256,2048]{1,0:T(8,128)(2,1)S(1)} fusion(bf16[512,2048]{1,0:T(8,128)(2,1)S(1)} %get-tuple-element.169, bf16[512,1024]{1,0:T(8,128)(2,1)S(1)} %copy-done.20, s32[]{:T(128)S(6)} %select_n.113), kind=kOutput, calls=%fused_computation.20 | convolution fusion | flops 537395200 | bytes 3407876 | tf_op jit(solution)/shard_map/td,tf->df/dot_general | solution.py:315
  192.2 1.7 convolution_convert_fusion
  196.2 2.0 collective-permute-done.7
  198.6 2.3 convolution_convert_fusion.7
  200.9 1.7 collective-permute-start.8
  203.5 2.3 convert_reduce_fusion.4
  209.2 6.6 %shard_map.249 = (f32[512,512]{1,0:T(8,128)S(1)}, f32[512,512]{1,0:T(8,128)S(1)}, f32[512,512]{1,0:T(8,128)S(1)}) custom-call(s32[1]{0:T(128)} %bitcast.1.refs_0_, bf16[512,512]{1,0:T(8,128)(2,1)S(1)} %copy-done.9, bf16[512,512]{1,0:T(8,128)(2,1)S(1)} %fusion.58.k_ref.refs_2_, bf16[512,512]{1,0:T(8,128)(2,1)S(1)} %fusion.43.v_ref.refs_3_, ...), custom_call_target="tpu_custom_call" | custom-call | flops 1342177280 | bytes 6291456 | tf_op jit(solution)/shard_map/pallas_call | solution.py:186
  217.1 2.5 collective-permute-start.15
  220.3 2.0 add_convert_fusion.1
  222.9 11.8 %collective-permute-done.9 = bf16[1024,512]{1,0:T(8,128)(2,1)S(1)} collective-permute-done((bf16[1024,512]{1,0:T(8,128)(2,1)S(1)}, bf16[1024,512]{1,0:T(8,128)(2,1)S(1)}, u32[]{:S(2)}, u32[]{:S(2)}) %collective-permute-start.9) | collective-permute-done | bytes 1048608 | tf_op jit(solution)/shard_map/ppermute | solution.py:18
  238.1 22.0 %collective-permute-done.10 = bf16[1024,512]{1,0:T(8,128)(2,1)S(1)} collective-permute-done((bf16[1024,512]{1,0:T(8,128)(2,1)S(1)}, bf16[1024,512]{1,0:T(8,128)(2,1)S(1)}, u32[]{:S(2)}, u32[]{:S(2)}) %collective-permute-start.10) | collective-permute-done | bytes 1048608 | tf_op jit(solution)/shard_map/ppermute | solution.py:18
  260.1 2.5 collective-permute-start.21
  263.0 3.9 collective-permute-done.21
  266.9 1.5 collective-permute-start.11
  269.2 2.0 collective-permute-start.18
  271.3 1.5 add_convert_fusion.2
  273.2 27.7 %collective-permute-done.11 = bf16[1024,512]{1,0:T(8,128)(2,1)S(1)} collective-permute-done((bf16[1024,512]{1,0:T(8,128)(2,1)S(1)}, bf16[1024,512]{1,0:T(8,128)(2,1)S(1)}, u32[]{:S(2)}, u32[]{:S(2)}) %collective-permute-start.11) | collective-permute-done | bytes 1048608 | tf_op jit(solution)/shard_map/ppermute | solution.py:18
  301.3 1.6 copy-done.26
  302.9 2.3 fusion.32
  305.2 4.9 %collective-permute-start.12 = (bf16[512,1024]{1,0:T(8,128)(2,1)}, bf16[512,1024]{1,0:T(8,128)(2,1)}, u32[]{:S(2)}, u32[]{:S(2)}) collective-permute-start(bf16[512,1024]{1,0:T(8,128)(2,1)} %fusion.32), channel_id=1, source_target_pairs={{0,1},{1,0},{2,3},{3,2},{4,5},{5,4},{6,7},{7,6},{8,9},{9,8},{10,11... | collective-permute-start | bytes 3145736 | tf_op jit(solution)/shard_map/ppermute | solution.py:24
  312.4 2.1 convolution_convert_fusion.4
  314.6 1.6 convolution_convert_fusion.5
  317.0 14.2 %collective-permute-done.12 = bf16[512,1024]{1,0:T(8,128)(2,1)} collective-permute-done((bf16[512,1024]{1,0:T(8,128)(2,1)}, bf16[512,1024]{1,0:T(8,128)(2,1)}, u32[]{:S(2)}, u32[]{:S(2)}) %collective-permute-start.12) | collective-permute-done | bytes 1048608 | tf_op jit(solution)/shard_map/ppermute | solution.py:24
  331.2 2.7 fusion.22
  339.6 6.9 %collective-permute-start.33 = (f32[9216]{0:T(1024)S(1)}, f32[9216]{0:T(1024)S(1)}, u32[]{:S(2)}, u32[]{:S(2)}) collective-permute-start(f32[9216]{0:T(1024)S(1)} %add.423), channel_id=1, source_target_pairs={{0,2},{2,0},{4,6},{6,4},{1,3},{3,1},{5,7},{7,5},{8,10},{10,8},{12,... | collective-permute-start | bytes 110600 | tf_op jit(solution)/shard_map/ppermute | solution.py:31
  346.6 4.7 %collective-permute-done.33 = f32[9216]{0:T(1024)S(1)} collective-permute-done((f32[9216]{0:T(1024)S(1)}, f32[9216]{0:T(1024)S(1)}, u32[]{:S(2)}, u32[]{:S(2)}) %collective-permute-start.33) | collective-permute-done | bytes 36896 | tf_op jit(solution)/shard_map/ppermute | solution.py:31
  352.3 3.5 fusion.57
  355.8 3.4 collective-permute-done.34
  360.2 1.9 add_convert_fusion.6
  362.2 3.4 collective-permute-start.27
  365.7 1.6 collective-permute-start.26
  369.9 2.6 collective-permute-done.27
  372.5 28.9 %collective-permute-done.26 = bf16[64,1536]{1,0:T(8,128)(2,1)S(1)} collective-permute-done((bf16[64,1536]{1,0:T(8,128)(2,1)S(1)}, bf16[64,1536]{1,0:T(8,128)(2,1)S(1)}, u32[]{:S(2)}, u32[]{:S(2)}) %collective-permute-start.26) | collective-permute-done | bytes 196640 | tf_op jit(solution)/shard_map/ppermute | solution.py:68
  401.6 3.4 collective-permute-start.28
  406.2 1.9 collective-permute-start.29
  408.2 2.9 collective-permute-start.30
  411.1 3.3 collective-permute-done.28
  414.4 13.9 %collective-permute-done.29 = bf16[64,1536]{1,0:T(8,128)(2,1)S(1)} collective-permute-done((bf16[64,1536]{1,0:T(8,128)(2,1)S(1)}, bf16[64,1536]{1,0:T(8,128)(2,1)S(1)}, u32[]{:S(2)}, u32[]{:S(2)}) %collective-permute-start.29) | collective-permute-done | bytes 196640 | tf_op jit(solution)/shard_map/ppermute | solution.py:73
  429.2 10.7 %all-reduce.3.cloned.1.call-done = (bf16[256,2048]{1,0:T(8,128)(2,1)}, bf16[2048,256]{1,0:T(8,128)(2,1)}, bf16[512,256]{1,0:T(8,128)(2,1)}) async-done(((bf16[256,2048]{1,0:T(8,128)(2,1)}, bf16[2048,256]{1,0:T(8,128)(2,1)}, bf16[512,256]{1,0:T(8,128)(2,1)}), (bf16[256,2048]{1,0:T(8,128)(2,1)}, bf16[2048,256]{1,0:T(8,128)(2,1)}, bf16[512,256]{1,0:T(8,128)(2,1)})) %all-reduce.3.cloned.1.call-update) | async-done | bytes 2359312 | tf_op jit(solution)/shard_map/psum | solution.py:375
  440.3 1.6 copy.67
  442.8 1.6 convert_element_type.322
  444.3 1.5 convert_element_type.323
  (271 shorter events, 52.5 us)
Async XLA Ops:
  7.2 6.6 %copy-start.38 = (bf16[2,8,16]{2,1,0:T(8,128)(2,1)S(1)}, bf16[2,8,16]{2,1,0:T(8,128)(2,1)}, u32[]{:S(2)}) copy-start(bf16[2,8,16]{2,1,0:T(8,128)(2,1)} %param.16) | copy-start | bytes 1540
  7.2 6.7 %copy-start.37 = (bf16[32,16]{0,1:T(8,128)(2,1)S(1)}, bf16[32,16]{0,1:T(8,128)(2,1)}, u32[]{:S(2)}) copy-start(bf16[32,16]{0,1:T(8,128)(2,1)} %param.20) | copy-start | bytes 3076
  7.2 6.9 %copy-start.39 = (bf16[256]{0:T(256)(128)(2,1)S(1)}, bf16[256]{0:T(256)(128)(2,1)}, u32[]{:S(2)}) copy-start(bf16[256]{0:T(256)(128)(2,1)} %param.23) | copy-start | bytes 1540
  7.2 7.1 %copy-start.40 = (bf16[256]{0:T(256)(128)(2,1)S(1)}, bf16[256]{0:T(256)(128)(2,1)}, u32[]{:S(2)}) copy-start(bf16[256]{0:T(256)(128)(2,1)} %param.24) | copy-start | bytes 1540
  7.2 7.3 %copy-start.41 = (bf16[256]{0:T(256)(128)(2,1)S(1)}, bf16[256]{0:T(256)(128)(2,1)}, u32[]{:S(2)}) copy-start(bf16[256]{0:T(256)(128)(2,1)} %param.25) | copy-start | bytes 1540
  7.2 7.5 %copy-start.42 = (bf16[256]{0:T(256)(128)(2,1)S(1)}, bf16[256]{0:T(256)(128)(2,1)}, u32[]{:S(2)}) copy-start(bf16[256]{0:T(256)(128)(2,1)} %param.26) | copy-start | bytes 1540
  7.3 7.8 %copy-start.43 = (bf16[256]{0:T(256)(128)(2,1)S(1)}, bf16[256]{0:T(256)(128)(2,1)}, u32[]{:S(2)}) copy-start(bf16[256]{0:T(256)(128)(2,1)} %param.18) | copy-start | bytes 1540
  7.3 8.0 %copy-start.44 = (bf16[256]{0:T(256)(128)(2,1)S(1)}, bf16[256]{0:T(256)(128)(2,1)}, u32[]{:S(2)}) copy-start(bf16[256]{0:T(256)(128)(2,1)} %param.22) | copy-start | bytes 1540
  7.3 24.3 %copy-start.13 = (bf16[1,512,1024]{2,1,0:T(8,128)(2,1)S(1)}, bf16[1,512,1024]{2,1,0:T(8,128)(2,1)}, u32[]{:S(2)}) copy-start(bf16[1,512,1024]{2,1,0:T(8,128)(2,1)} %param.14) | copy-start | bytes 3145732
  7.3 94.7 %all-gather.14.cloned.1.call-start = ((), (), s32[]{:S(2)}) async-start(), calls=%async_computation.3 | async-start | bytes 1310720 | tf_op jit(solution)/shard_map/all_gather | solution.py:228
  9.1 116.5 %all-gather.8.cloned.1.call-start = ((), (), s32[]{:S(2)}) async-start(), calls=%async_computation | async-start | bytes 1310720 | tf_op jit(solution)/shard_map/all_gather | solution.py:248
  9.9 147.0 %all-gather.10.cloned.1.call-start = ((), (), s32[]{:S(2)}) async-start(), calls=%async_computation.1 | async-start | bytes 5242880 | tf_op jit(solution)/shard_map/all_gather | solution.py:249
  10.6 154.6 %all-gather.12.cloned.1.call-start = ((), (), s32[]{:S(2)}) async-start(), calls=%async_computation.2 | async-start | bytes 5242880 | tf_op jit(solution)/shard_map/all_gather | solution.py:250
  10.7 24.2 %collective-permute-start = (bf16[2,256,512]{2,1,0:T(8,128)(2,1)S(1)}, bf16[2,256,512]{2,1,0:T(8,128)(2,1)}, u32[]{:S(2)}, u32[]{:S(2)}) collective-permute-start(bf16[2,256,512]{2,1,0:T(8,128)(2,1)S(1)} %slice_bitcast_fusion.1), channel_id=1, source_target_pairs={{0,8},{8,0},{16,24},{24,16},{1,9},{9,1},{17,25},{25,17},{2,10},{10... | collective-permute-start | bytes 1572872 | tf_op jit(solution)/shard_map/ppermute | solution.py:31
  11.2 23.3 %collective-permute-start.1 = (bf16[2,256,512]{2,1,0:T(8,128)(2,1)S(1)}, bf16[2,256,512]{2,1,0:T(8,128)(2,1)S(1)}, u32[]{:S(2)}, u32[]{:S(2)}) collective-permute-start(bf16[2,256,512]{2,1,0:T(8,128)(2,1)S(1)} %slice_bitcast_fusion.1), channel_id=1, source_target_pairs={{0,16},{8,24},{16,0},{24,8},{1,17},{9,25},{17,1},{25,9},{2,18},{10... | collective-permute-start | bytes 1572872 | tf_op jit(solution)/shard_map/ppermute | solution.py:31
  34.5 4.9 %collective-permute-start.2 = (bf16[2,256,512]{2,1,0:T(8,128)(2,1)S(1)}, bf16[2,256,512]{2,1,0:T(8,128)(2,1)S(1)}, u32[]{:S(2)}, u32[]{:S(2)}) collective-permute-start(bf16[2,256,512]{2,1,0:T(8,128)(2,1)S(1)} %collective-permute-done.1), channel_id=1, source_target_pairs={{0,8},{8,0},{16,24},{24,16},{1,9},{9,1},{17,25},{25,17},{2,10},{10... | collective-permute-start | bytes 1572872 | tf_op jit(solution)/shard_map/ppermute | solution.py:31
  42.3 27.4 %collective-permute-start.3 = (bf16[1024,512]{1,0:T(8,128)(2,1)}, bf16[1024,512]{1,0:T(8,128)(2,1)S(1)}, u32[]{:S(2)}, u32[]{:S(2)}) collective-permute-start(bf16[1024,512]{1,0:T(8,128)(2,1)} %pad_maximum_fusion.1), channel_id=1, source_target_pairs={{0,2},{2,4},{4,6},{1,3},{3,5},{5,7},{8,10},{10,12},{12,14},{9,11},... | collective-permute-start | bytes 3145736 | tf_op jit(solution)/shard_map/ppermute | solution.py:18
  46.7 393.2 %all-reduce.3.cloned.1.call-start = ((), (), s32[]{:S(2)}) async-start(), calls=%async_computation.4 | async-start | bytes 4718592 | tf_op jit(solution)/shard_map/psum | solution.py:375
  69.6 26.3 %copy-start.34 = (bf16[1024,512]{1,0:T(8,128)(2,1)}, bf16[1024,512]{1,0:T(8,128)(2,1)S(1)}, u32[]{:S(2)}) copy-start(bf16[1024,512]{1,0:T(8,128)(2,1)S(1)} %collective-permute-done.3) | copy-start | bytes 3145732
  69.6 26.3 %collective-permute-start.4 = (bf16[1024,512]{1,0:T(8,128)(2,1)S(1)}, bf16[1024,512]{1,0:T(8,128)(2,1)}, u32[]{:S(2)}, u32[]{:S(2)}) collective-permute-start(bf16[1024,512]{1,0:T(8,128)(2,1)S(1)} %collective-permute-done.3), channel_id=1, source_target_pairs={{0,2},{2,4},{4,6},{1,3},{3,5},{5,7},{8,10},{10,12},{12,14},{9,11},... | collective-permute-start | bytes 3145736 | tf_op jit(solution)/shard_map/ppermute | solution.py:18
  95.9 25.9 %collective-permute-start.5 = (bf16[1024,512]{1,0:T(8,128)(2,1)}, bf16[1024,512]{1,0:T(8,128)(2,1)}, u32[]{:S(2)}, u32[]{:S(2)}) collective-permute-start(bf16[1024,512]{1,0:T(8,128)(2,1)} %collective-permute-done.4), channel_id=1, source_target_pairs={{0,2},{2,4},{4,6},{1,3},{3,5},{5,7},{8,10},{10,12},{12,14},{9,11},... | collective-permute-start | bytes 3145736 | tf_op jit(solution)/shard_map/ppermute | solution.py:18
  101.9 7.0 %copy-start.32 = (bf16[512,1024]{1,0:T(8,128)(2,1)}, bf16[512,1024]{1,0:T(8,128)(2,1)S(1)}, u32[]{:S(2)}) copy-start(bf16[512,1024]{1,0:T(8,128)(2,1)S(1)} %fusion.16) | copy-start | bytes 3145732
  104.3 18.9 %copy-start.8 = (bf16[512,512]{1,0:T(8,128)(2,1)}, bf16[512,512]{1,0:T(8,128)(2,1)S(1)}, u32[]{:S(2)}) copy-start(bf16[512,512]{1,0:T(8,128)(2,1)S(1)} %fusion.37.q_ref.refs_1_) | copy-start | bytes 1572868
  104.3 4.6 %copy-start.35 = (bf16[1024,512]{1,0:T(8,128)(2,1)S(1)}, bf16[1024,512]{1,0:T(8,128)(2,1)}, u32[]{:S(2)}) copy-start(bf16[1024,512]{1,0:T(8,128)(2,1)} %copy-done.34) | copy-start | bytes 3145732
  128.7 23.0 %collective-permute-start.6 = (bf16[512,1024]{1,0:T(8,128)(2,1)}, bf16[512,1024]{1,0:T(8,128)(2,1)}, u32[]{:S(2)}, u32[]{:S(2)}) collective-permute-start(bf16[512,1024]{1,0:T(8,128)(2,1)} %convolution_convert_fusion.6), channel_id=1, source_target_pairs={{0,1},{1,0},{2,3},{3,2},{4,5},{5,4},{6,7},{7,6},{8,9},{9,8},{10,11... | collective-permute-start | bytes 3145736 | tf_op jit(solution)/shard_map/ppermute | solution.py:24
  165.3 8.7 %copy-start.45 = (bf16[1024,2048]{1,0:T(8,128)(2,1)S(1)}, bf16[1024,2048]{1,0:T(8,128)(2,1)}, u32[]{:S(2)}) copy-start(bf16[1024,2048]{1,0:T(8,128)(2,1)} %all-gather.10.cloned.1.call-done) | copy-start | bytes 12582916
  174.0 4.1 copy-start.20
  176.4 21.8 %collective-permute-start.7 = (bf16[512,1024]{1,0:T(8,128)(2,1)S(1)}, bf16[512,1024]{1,0:T(8,128)(2,1)S(1)}, u32[]{:S(2)}, u32[]{:S(2)}) collective-permute-start(bf16[512,1024]{1,0:T(8,128)(2,1)S(1)} %convolution_convert_fusion.8), channel_id=1, source_target_pairs={{0,1},{1,0},{2,3},{3,2},{4,5},{5,4},{6,7},{7,6},{8,9},{9,8},{10,11... | collective-permute-start | bytes 3145736 | tf_op jit(solution)/shard_map/ppermute | solution.py:24
  190.3 26.0 %collective-permute-start.14 = (bf16[256,2048]{1,0:T(8,128)(2,1)S(1)}, bf16[256,2048]{1,0:T(8,128)(2,1)S(1)}, u32[]{:S(2)}, u32[]{:S(2)}) collective-permute-start(bf16[256,2048]{1,0:T(8,128)(2,1)S(1)} %convolution_convert_fusion.2), channel_id=1, source_target_pairs={{0,8},{8,0},{16,24},{24,16},{1,9},{9,1},{17,25},{25,17},{2,10},{10... | collective-permute-start | bytes 3145736 | tf_op jit(solution)/shard_map/ppermute | solution.py:31
  191.2 78.1 %collective-permute-start.13 = (bf16[256,2048]{1,0:T(8,128)(2,1)S(1)}, bf16[256,2048]{1,0:T(8,128)(2,1)S(1)}, u32[]{:S(2)}, u32[]{:S(2)}) collective-permute-start(bf16[256,2048]{1,0:T(8,128)(2,1)S(1)} %convolution_convert_fusion.3), channel_id=1, source_target_pairs={{0,8},{8,0},{16,24},{24,16},{1,9},{9,1},{17,25},{25,17},{2,10},{10... | collective-permute-start | bytes 3145736 | tf_op jit(solution)/shard_map/ppermute | solution.py:31
  193.9 26.3 %collective-permute-start.17 = (bf16[2048,256]{1,0:T(8,128)(2,1)}, bf16[2048,256]{1,0:T(8,128)(2,1)}, u32[]{:S(2)}, u32[]{:S(2)}) collective-permute-start(bf16[2048,256]{1,0:T(8,128)(2,1)} %convolution_convert_fusion), channel_id=1, source_target_pairs={{0,8},{8,0},{16,24},{24,16},{1,9},{9,1},{17,25},{25,17},{2,10},{10... | collective-permute-start | bytes 3145736 | tf_op jit(solution)/shard_map/ppermute | solution.py:31
  198.6 4.0 copy-start.11
  200.9 71.8 %collective-permute-start.8 = (bf16[512,1024]{1,0:T(8,128)(2,1)S(1)}, bf16[512,1024]{1,0:T(8,128)(2,1)S(1)}, u32[]{:S(2)}, u32[]{:S(2)}) collective-permute-start(bf16[512,1024]{1,0:T(8,128)(2,1)S(1)} %convolution_convert_fusion.7), channel_id=1, source_target_pairs={{0,1},{1,0},{2,3},{3,2},{4,5},{5,4},{6,7},{7,6},{8,9},{9,8},{10,11... | collective-permute-start | bytes 3145736 | tf_op jit(solution)/shard_map/ppermute | solution.py:24
  207.8 8.1 %copy-start.1 = (bf16[512,512]{1,0:T(8,128)(2,1)S(1)}, bf16[512,512]{1,0:T(8,128)(2,1)}, u32[]{:S(2)}) copy-start(bf16[512,512]{1,0:T(8,128)(2,1)} %copy-done) | copy-start | bytes 1572868
  207.8 8.1 %copy-start.3 = (bf16[512,512]{1,0:T(8,128)(2,1)S(1)}, bf16[512,512]{1,0:T(8,128)(2,1)}, u32[]{:S(2)}) copy-start(bf16[512,512]{1,0:T(8,128)(2,1)} %copy-done.2) | copy-start | bytes 1572868
  207.8 26.8 %collective-permute-start.9 = (bf16[1024,512]{1,0:T(8,128)(2,1)S(1)}, bf16[1024,512]{1,0:T(8,128)(2,1)S(1)}, u32[]{:S(2)}, u32[]{:S(2)}) collective-permute-start(bf16[1024,512]{1,0:T(8,128)(2,1)S(1)} %pad_maximum_fusion.2), channel_id=1, source_target_pairs={{2,0},{4,2},{6,4},{3,1},{5,3},{7,5},{10,8},{12,10},{14,12},{11,9},... | collective-permute-start | bytes 3145736 | tf_op jit(solution)/shard_map/ppermute | solution.py:18
  217.1 54.2 %collective-permute-start.15 = (bf16[256,2048]{1,0:T(8,128)(2,1)S(1)}, bf16[256,2048]{1,0:T(8,128)(2,1)S(1)}, u32[]{:S(2)}, u32[]{:S(2)}) collective-permute-start(bf16[256,2048]{1,0:T(8,128)(2,1)S(1)} %add_convert_fusion.3), channel_id=1, source_target_pairs={{0,16},{8,24},{16,0},{24,8},{1,17},{9,25},{17,1},{25,9},{2,18},{10... | collective-permute-start | bytes 3145736 | tf_op jit(solution)/shard_map/ppermute | solution.py:31
  220.2 17.5 %collective-permute-start.20 = (bf16[512,256]{1,0:T(8,128)(2,1)S(1)}, bf16[512,256]{1,0:T(8,128)(2,1)S(1)}, u32[]{:S(2)}, u32[]{:S(2)}) collective-permute-start(bf16[512,256]{1,0:T(8,128)(2,1)S(1)} %convolution_convert_fusion.10), channel_id=1, source_target_pairs={{0,8},{8,0},{16,24},{24,16},{1,9},{9,1},{17,25},{25,17},{2,10},{10... | collective-permute-start | bytes 786440 | tf_op jit(solution)/shard_map/ppermute | solution.py:31
  222.9 13.4 %copy-start.18 = (bf16[512,512]{1,0:T(8,128)(2,1)}, bf16[512,512]{1,0:T(8,128)(2,1)S(1)}, u32[]{:S(2)}) copy-start(bf16[512,512]{1,0:T(8,128)(2,1)S(1)} %add_convert_fusion.8) | copy-start | bytes 1572868
  235.0 25.1 %collective-permute-start.10 = (bf16[1024,512]{1,0:T(8,128)(2,1)S(1)}, bf16[1024,512]{1,0:T(8,128)(2,1)S(1)}, u32[]{:S(2)}, u32[]{:S(2)}) collective-permute-start(bf16[1024,512]{1,0:T(8,128)(2,1)S(1)} %fusion.31), channel_id=1, source_target_pairs={{2,0},{4,2},{6,4},{3,1},{5,3},{7,5},{10,8},{12,10},{14,12},{11,9},... | collective-permute-start | bytes 3145736 | tf_op jit(solution)/shard_map/ppermute | solution.py:18
  237.7 25.2 %collective-permute-start.19 = (bf16[512,256]{1,0:T(8,128)(2,1)S(1)}, bf16[512,256]{1,0:T(8,128)(2,1)S(1)}, u32[]{:S(2)}, u32[]{:S(2)}) collective-permute-start(bf16[512,256]{1,0:T(8,128)(2,1)S(1)} %convolution_convert_fusion.11), channel_id=1, source_target_pairs={{0,8},{8,0},{16,24},{24,16},{1,9},{9,1},{17,25},{25,17},{2,10},{10... | collective-permute-start | bytes 786440 | tf_op jit(solution)/shard_map/ppermute | solution.py:31
  260.1 6.8 %collective-permute-start.21 = (bf16[512,256]{1,0:T(8,128)(2,1)S(1)}, bf16[512,256]{1,0:T(8,128)(2,1)S(1)}, u32[]{:S(2)}, u32[]{:S(2)}) collective-permute-start(bf16[512,256]{1,0:T(8,128)(2,1)S(1)} %add_convert_fusion.10), channel_id=1, source_target_pairs={{0,16},{8,24},{16,0},{24,8},{1,17},{9,25},{17,1},{25,9},{2,18},{10... | collective-permute-start | bytes 786440 | tf_op jit(solution)/shard_map/ppermute | solution.py:31
  262.9 47.2 %collective-permute-start.16 = (bf16[2048,256]{1,0:T(8,128)(2,1)S(1)}, bf16[2048,256]{1,0:T(8,128)(2,1)S(1)}, u32[]{:S(2)}, u32[]{:S(2)}) collective-permute-start(bf16[2048,256]{1,0:T(8,128)(2,1)S(1)} %convolution_convert_fusion.1), channel_id=1, source_target_pairs={{0,8},{8,0},{16,24},{24,16},{1,9},{9,1},{17,25},{25,17},{2,10},{10... | collective-permute-start | bytes 3145736 | tf_op jit(solution)/shard_map/ppermute | solution.py:31
  266.9 34.0 %collective-permute-start.11 = (bf16[1024,512]{1,0:T(8,128)(2,1)S(1)}, bf16[1024,512]{1,0:T(8,128)(2,1)S(1)}, u32[]{:S(2)}, u32[]{:S(2)}) collective-permute-start(bf16[1024,512]{1,0:T(8,128)(2,1)S(1)} %fusion.30), channel_id=1, source_target_pairs={{2,0},{4,2},{6,4},{3,1},{5,3},{7,5},{10,8},{12,10},{14,12},{11,9},... | collective-permute-start | bytes 3145736 | tf_op jit(solution)/shard_map/ppermute | solution.py:18
  269.2 40.9 %collective-permute-start.18 = (bf16[2048,256]{1,0:T(8,128)(2,1)S(1)}, bf16[2048,256]{1,0:T(8,128)(2,1)S(1)}, u32[]{:S(2)}, u32[]{:S(2)}) collective-permute-start(bf16[2048,256]{1,0:T(8,128)(2,1)S(1)} %add_convert_fusion.1), channel_id=1, source_target_pairs={{0,16},{8,24},{16,0},{24,8},{1,17},{9,25},{17,1},{25,9},{2,18},{10... | collective-permute-start | bytes 3145736 | tf_op jit(solution)/shard_map/ppermute | solution.py:31
  301.2 3.9 copy-start.21
  305.2 26.1 %collective-permute-start.12 = (bf16[512,1024]{1,0:T(8,128)(2,1)}, bf16[512,1024]{1,0:T(8,128)(2,1)}, u32[]{:S(2)}, u32[]{:S(2)}) collective-permute-start(bf16[512,1024]{1,0:T(8,128)(2,1)} %fusion.32), channel_id=1, source_target_pairs={{0,1},{1,0},{2,3},{3,2},{4,5},{5,4},{6,7},{7,6},{8,9},{9,8},{10,11... | collective-permute-start | bytes 3145736 | tf_op jit(solution)/shard_map/ppermute | solution.py:24
  314.5 22.3 %collective-permute-start.23 = (bf16[256,1536]{1,0:T(8,128)(2,1)S(1)}, bf16[256,1536]{1,0:T(8,128)(2,1)S(1)}, u32[]{:S(2)}, u32[]{:S(2)}) collective-permute-start(bf16[256,1536]{1,0:T(8,128)(2,1)S(1)} %convolution_convert_fusion.4), channel_id=1, source_target_pairs={{0,8},{8,0},{16,24},{24,16},{1,9},{9,1},{17,25},{25,17},{2,10},{10... | collective-permute-start | bytes 2359304 | tf_op jit(solution)/shard_map/ppermute | solution.py:31
  316.2 15.1 %copy-start.14 = (bf16[1,512,1024]{2,1,0:T(8,128)(2,1)S(1)}, bf16[1,512,1024]{2,1,0:T(8,128)(2,1)}, u32[]{:S(2)}) copy-start(bf16[1,512,1024]{2,1,0:T(8,128)(2,1)} %param.14) | copy-start | bytes 3145732
  316.2 44.0 %collective-permute-start.22 = (bf16[256,1536]{1,0:T(8,128)(2,1)}, bf16[256,1536]{1,0:T(8,128)(2,1)}, u32[]{:S(2)}, u32[]{:S(2)}) collective-permute-start(bf16[256,1536]{1,0:T(8,128)(2,1)} %convolution_convert_fusion.5), channel_id=1, source_target_pairs={{0,8},{8,0},{16,24},{24,16},{1,9},{9,1},{17,25},{25,17},{2,10},{10... | collective-permute-start | bytes 2359304 | tf_op jit(solution)/shard_map/ppermute | solution.py:31
  316.8 17.3 %copy-start.12 = (f32[512,1024]{1,0:T(8,128)S(1)}, f32[512,1024]{1,0:T(8,128)}, u32[]{:S(2)}) copy-start(f32[512,1024]{1,0:T(8,128)} %copy-done.10) | copy-start | bytes 6291460
  334.0 1.6 collective-permute-start.31
  335.6 16.7 %copy-start.16 = (f32[512,1024]{1,0:T(8,128)S(1)}, f32[512,1024]{1,0:T(8,128)}, u32[]{:S(2)}) copy-start(f32[512,1024]{1,0:T(8,128)} %get-tuple-element.133) | copy-start | bytes 6291460
  335.6 4.0 collective-permute-start.32
  337.5 22.7 %collective-permute-start.24 = (bf16[256,1536]{1,0:T(8,128)(2,1)S(1)}, bf16[256,1536]{1,0:T(8,128)(2,1)S(1)}, u32[]{:S(2)}, u32[]{:S(2)}) collective-permute-start(bf16[256,1536]{1,0:T(8,128)(2,1)S(1)} %add_convert_fusion.7), channel_id=1, source_target_pairs={{0,16},{8,24},{16,0},{24,8},{1,17},{9,25},{17,1},{25,9},{2,18},{10... | collective-permute-start | bytes 2359304 | tf_op jit(solution)/shard_map/ppermute | solution.py:31
  339.6 11.6 %collective-permute-start.33 = (f32[9216]{0:T(1024)S(1)}, f32[9216]{0:T(1024)S(1)}, u32[]{:S(2)}, u32[]{:S(2)}) collective-permute-start(f32[9216]{0:T(1024)S(1)} %add.423), channel_id=1, source_target_pairs={{0,2},{2,0},{4,6},{6,4},{1,3},{3,1},{5,7},{7,5},{8,10},{10,8},{12,... | collective-permute-start | bytes 110600 | tf_op jit(solution)/shard_map/ppermute | solution.py:31
  351.2 8.0 %collective-permute-start.34 = (f32[9216]{0:T(1024)S(1)}, f32[9216]{0:T(1024)S(1)}, u32[]{:S(2)}, u32[]{:S(2)}) collective-permute-start(f32[9216]{0:T(1024)S(1)} %add.424), channel_id=1, source_target_pairs={{0,4},{2,6},{4,0},{6,2},{1,5},{3,7},{5,1},{7,3},{8,12},{10,14},{12... | collective-permute-start | bytes 110600 | tf_op jit(solution)/shard_map/ppermute | solution.py:31
  352.3 7.9 %copy-start.23 = (bf16[1024,512]{1,0:T(8,128)(2,1)S(1)}, bf16[1024,512]{1,0:T(8,128)(2,1)}, u32[]{:S(2)}) copy-start(bf16[1024,512]{1,0:T(8,128)(2,1)} %copy-done.21) | copy-start | bytes 3145732
  362.2 10.3 %collective-permute-start.27 = (bf16[64,1536]{1,0:T(8,128)(2,1)S(1)}, bf16[64,1536]{1,0:T(8,128)(2,1)S(1)}, u32[]{:S(2)}, u32[]{:S(2)}) collective-permute-start(bf16[64,1536]{1,0:T(8,128)(2,1)S(1)} %get-tuple-element.146), channel_id=1, source_target_pairs={{0,6},{2,0},{4,2},{6,4},{1,7},{3,1},{5,3},{7,5},{8,14},{10,8},{12,... | collective-permute-start | bytes 589832 | tf_op jit(solution)/shard_map/ppermute | solution.py:68
  365.7 35.8 %collective-permute-start.26 = (bf16[64,1536]{1,0:T(8,128)(2,1)S(1)}, bf16[64,1536]{1,0:T(8,128)(2,1)S(1)}, u32[]{:S(2)}, u32[]{:S(2)}) collective-permute-start(bf16[64,1536]{1,0:T(8,128)(2,1)S(1)} %get-tuple-element.147), channel_id=1, source_target_pairs={{0,4},{2,6},{4,0},{6,2},{1,5},{3,7},{5,1},{7,3},{8,12},{10,14},{12... | collective-permute-start | bytes 589832 | tf_op jit(solution)/shard_map/ppermute | solution.py:68
  367.3 34.1 %collective-permute-start.25 = (bf16[64,1536]{1,0:T(8,128)(2,1)S(1)}, bf16[64,1536]{1,0:T(8,128)(2,1)S(1)}, u32[]{:S(2)}, u32[]{:S(2)}) collective-permute-start(bf16[64,1536]{1,0:T(8,128)(2,1)S(1)} %get-tuple-element.145), channel_id=1, source_target_pairs={{0,2},{2,4},{4,6},{6,0},{1,3},{3,5},{5,7},{7,1},{8,10},{10,12},{12... | collective-permute-start | bytes 589832 | tf_op jit(solution)/shard_map/ppermute | solution.py:68
  401.6 12.8 %collective-permute-start.28 = (bf16[64,1536]{1,0:T(8,128)(2,1)S(1)}, bf16[64,1536]{1,0:T(8,128)(2,1)S(1)}, u32[]{:S(2)}, u32[]{:S(2)}) collective-permute-start(bf16[64,1536]{1,0:T(8,128)(2,1)S(1)} %get-tuple-element.135), channel_id=1, source_target_pairs={{0,2},{2,4},{4,6},{6,0},{1,3},{3,5},{5,7},{7,1},{8,10},{10,12},{12... | collective-permute-start | bytes 589832 | tf_op jit(solution)/shard_map/ppermute | solution.py:73
  406.2 22.1 %collective-permute-start.29 = (bf16[64,1536]{1,0:T(8,128)(2,1)S(1)}, bf16[64,1536]{1,0:T(8,128)(2,1)S(1)}, u32[]{:S(2)}, u32[]{:S(2)}) collective-permute-start(bf16[64,1536]{1,0:T(8,128)(2,1)S(1)} %get-tuple-element.135), channel_id=1, source_target_pairs={{0,4},{2,6},{4,0},{6,2},{1,5},{3,7},{5,1},{7,3},{8,12},{10,14},{12... | collective-permute-start | bytes 589832 | tf_op jit(solution)/shard_map/ppermute | solution.py:73
  408.2 20.7 %collective-permute-start.30 = (bf16[64,1536]{1,0:T(8,128)(2,1)S(1)}, bf16[64,1536]{1,0:T(8,128)(2,1)S(1)}, u32[]{:S(2)}, u32[]{:S(2)}) collective-permute-start(bf16[64,1536]{1,0:T(8,128)(2,1)S(1)} %get-tuple-element.135), channel_id=1, source_target_pairs={{0,6},{2,0},{4,2},{6,4},{1,7},{3,1},{5,3},{7,5},{8,14},{10,8},{12,... | collective-permute-start | bytes 589832 | tf_op jit(solution)/shard_map/ppermute | solution.py:73
  (23 other events, 41.3 us)
Sparse Core Ops, SparseCore 0:
  10.3 23.3 all-gather.13
  35.2 18.2 all-gather.7
  55.1 34.4 all-gather.9
  91.0 35.0 all-gather.11
  311.5 128.2 all-reduce.2
